TPU v7x, 256 devices: a whole 4x4x8 slice. The times are simulated.
256 devices in a mesh: ctx: 64 (over z, x, core), head: 4 (over y).
Axes of the slice: x: 4, y: 4, z: 8, core: 2. Of those that a mesh axis runs over, the one named last changes fastest.
Arguments:
- queries: bfloat16 [131072, 1024], P('ctx', 'head'), may hold values from -6 to 6
- keys_values: bfloat16 [2, 131072, 1024], P(None, 'ctx', 'head'), may hold values from -6 to 6
- out_weight: bfloat16 [1024, 1024], P('head'), may hold values from -0.1875 to 0.1875
Outputs:
- projected: bfloat16 [131072, 1024], P(('ctx', 'head'))
All inputs are finite; a program needn't handle non-finite values.
Results may differ from a plain program's by a relative error of at most 0.012.
The roundings to bfloat16 on the way count: a program that leaves them out, or rounds other values in their place, can miss the bound.
Values may be sent and summed in bfloat16 or wider, within the bound.
No kernel may reach another device: no remote copies, remote signals or barrier semaphores. Data moves between devices by JAX's collectives and lax.ppermute only.
A program may use at most 128 MiB of HBM per device.

v0:
```python
import functools
import math

import jax
import jax.numpy as jnp
from jax import lax
from jax.experimental import pallas as pl
from jax.experimental.pallas import tpu as pltpu
from jax.sharding import PartitionSpec as P

HD = 64
BLK = 128
WIDE = 256
CHUNK = 512
SCALE = math.log2(math.e) / math.sqrt(HD)
ROOT = 1.0 / math.sqrt(2.0)
HIDE = -1e30
NT = (((1,), (1,)), ((), ()))
F32 = jnp.float32
BF16 = jnp.bfloat16

VMEM = pl.BlockSpec(memory_space=pltpu.VMEM)
SMEM = pl.BlockSpec(memory_space=pltpu.SMEM)


def call(kernel, name, outs, args, n_scalar=1, limit=16):
    return list(pl.pallas_call(
        kernel,
        out_shape=[jax.ShapeDtypeStruct(shape, dtype) for shape, dtype in outs],
        in_specs=[SMEM] * n_scalar + [VMEM] * (len(args) - n_scalar),
        out_specs=[VMEM] * len(outs),
        compiler_params=pltpu.CompilerParams(vmem_limit_bytes=limit * 2**20),
        name=name,
    )(*args))


def halve(rows):
    n = rows.shape[0]
    out = lax.broadcasted_iota(jnp.int32, (n // 2, n), 0)
    col = lax.broadcasted_iota(jnp.int32, (n // 2, n), 1)
    pairs = (col // 2 == out).astype(BF16)
    return (jnp.dot(pairs, rows, preferred_element_type=F32) * ROOT).astype(BF16)


def spread(q, pair):
    x = q[:, pair * 128 : pair * 128 + 128].astype(F32) * SCALE
    head = x.astype(BF16)
    rest = (x - head.astype(F32)).astype(BF16)
    low = lax.broadcasted_iota(jnp.int32, head.shape, 1) < HD
    zero = jnp.zeros_like(head)
    return [
        jnp.concatenate([jnp.where(keep, head, zero), jnp.where(keep, rest, zero)], 1)
        for keep in (low, jnp.logical_not(low))
    ]


def twice(k, pair):
    k = k[:, pair * 128 : pair * 128 + 128]
    return jnp.concatenate([k, k], 1)


def ones_beside(v, pair):
    v = v[:, pair * 128 : pair * 128 + 128]
    return jnp.concatenate([v, jnp.ones_like(v)], 1)


def scores(q, k):
    return lax.dot_general(q, k, NT, preferred_element_type=F32)


def select(x0, x1):
    low = lax.broadcasted_iota(jnp.int32, (x0.shape[0], 128), 1) < HD
    return jnp.where(low, x0, x1)


def pyramid_kernel(at_ref, kv_ref, pyr_ref, face_ref, back_ref):
    even = jnp.bitwise_and(at_ref[1], 1) == 0
    for side in range(2):
        for i in range(8):
            pyr_ref[side, pl.ds(i * 128, 128)] = halve(kv_ref[side, pl.ds(i * 256, 256)])
        first, last = kv_ref[side, pl.ds(0, BLK)], kv_ref[side, pl.ds(2048 - BLK, BLK)]
        face_ref[side, pl.ds(BLK, BLK)] = jnp.where(even, last, first)
        back_ref[side] = jnp.where(even, first, last)
    for side in range(2):
        for i in range(4):
            pyr_ref[side, pl.ds(1024 + i * 128, 128)] = halve(pyr_ref[side, pl.ds(i * 256, 256)])
    for side in range(2):
        for i in range(2):
            pyr_ref[side, pl.ds(1536 + i * 128, 128)] = halve(
                pyr_ref[side, pl.ds(1024 + i * 256, 256)]
            )
    for side in range(2):
        face_ref[side, pl.ds(0, BLK)] = halve(pyr_ref[side, pl.ds(1536, 256)])


def climb_kernel(step, at_ref, mine_ref, other_ref, up_ref):
    place = at_ref[1]
    low = jnp.bitwise_and(lax.shift_right_logical(place, step - 1), 1) == 0
    if step == 1:
        side = jnp.bitwise_and(place, 1)
        mine, other = mine_ref[side, pl.ds(0, BLK)], other_ref[side, pl.ds(0, BLK)]
    else:
        mine, other = mine_ref[...], other_ref[...]
    mine, other = halve(mine), halve(other)
    up_ref[pl.ds(0, 64)] = jnp.where(low, mine, other)
    up_ref[pl.ds(64, 64)] = jnp.where(low, other, mine)


def near_kernel(by, shards, at_ref, q_ref, kv_ref, pyr_ref, face_ref, back_ref, o_ref, l_ref, m_ref):
    chunk, place = jnp.bitwise_and(at_ref[0] + by, 3), at_ref[1]
    even = jnp.bitwise_and(place, 1) == 0

    def panel(ref, side, start, rows=BLK):
        return ref[side, pl.ds(pl.multiple_of(start, BLK), rows)]
    for t in range(2):
        base = chunk * CHUNK + t * 256
        q = q_ref[pl.ds(pl.multiple_of(base, 256), 256)]
        parts = []
        for side in range(2):
            main = jnp.concatenate([
                panel(kv_ref, side, base, 256),
                panel(pyr_ref, side, chunk * 256 + (1 - t) * BLK),
                panel(pyr_ref, side, 1024 + jnp.bitwise_xor(chunk, 1) * BLK)], 0)
            third = panel(pyr_ref, side, 1536 + jnp.bitwise_xor(lax.shift_right_logical(chunk, 1), 1) * BLK)
            if t == 0:
                low = panel(kv_ref, side, jnp.maximum(base - BLK, 0))
                halo = jnp.where(even, back_ref[side], face_ref[side, pl.ds(BLK, BLK)])
                low = jnp.where(chunk == 0, halo, low)
                high = panel(kv_ref, side, base + 256)
            else:
                low = panel(kv_ref, side, base - BLK)
                high = panel(kv_ref, side, jnp.minimum(base + 256, 2048 - BLK))
                halo = jnp.where(even, face_ref[side, pl.ds(BLK, BLK)], back_ref[side])
                high = jnp.where(chunk == 3, halo, high)
            parts.append((main, jnp.concatenate([third, low], 0), jnp.concatenate([third, high], 0)))
        ks, vs = parts
        for pair in range(2):
            h0, h1 = spread(q, pair)
            qs = jnp.concatenate([h0[:128], h1[:128], h0[128:], h1[128:]], 0)
            k1, k2, k3 = [twice(k, pair) for k in ks]
            v1, v2, v3 = [ones_beside(v, pair) for v in vs]
            s1 = scores(qs, k1)
            s2 = scores(qs[:256], k2)
            s3 = scores(qs[256:], k3)
            if t == 0:
                bias = jnp.where((chunk == 0) & (place == 0), HIDE, 0.0)
                s2 = jnp.concatenate([s2[:, :128], s2[:, 128:] + bias], 1)
            else:
                bias = jnp.where((chunk == 3) & (place == shards - 1), HIDE, 0.0)
                s3 = jnp.concatenate([s3[:, :128], s3[:, 128:] + bias], 1)
            s23 = jnp.concatenate([s2, s3], 0)
            m = jnp.max(jnp.concatenate([s1, s23], 1), axis=1, keepdims=True)
            p1 = jnp.exp2(s1 - m).astype(BF16)
            p23 = jnp.exp2(s23 - m).astype(BF16)
            o = jnp.dot(p1, v1, preferred_element_type=F32)
            o = o + jnp.concatenate([jnp.dot(p23[:256], v2, preferred_element_type=F32),
                                     jnp.dot(p23[256:], v3, preferred_element_type=F32)], 0)
            for part in range(2):
                r = part * 256
                rows = pl.ds(t * 256 + part * 128, 128)
                cols = pl.ds(pair * 128, 128)
                o_ref[rows, cols] = select(o[r:r+128, :128], o[r+128:r+256, :128])
                l_ref[rows, cols] = select(o[r:r+128, 128:], o[r+128:r+256, 128:])
                m_ref[rows, cols] = select(m[r:r+128], m[r+128:r+256])


def far_kernel(by, at_ref, q_ref, o_ref, l_ref, m_ref, face_ref, mine_ref, other_ref, out_ref):
    chunk, core = jnp.bitwise_and(at_ref[0] + by, 3), jnp.bitwise_and(at_ref[1], 1)
    q = q_ref[pl.ds(pl.multiple_of(chunk * CHUNK, CHUNK), CHUNK)]
    mine, other = mine_ref[...].reshape(5 * BLK, WIDE), other_ref[...].reshape(5 * BLK, WIDE)
    k = jnp.concatenate([face_ref[0, pl.ds(0, BLK)], jnp.where(core == 0, mine, other)], 0)
    v = jnp.concatenate([face_ref[1, pl.ds(0, BLK)], jnp.where(core == 0, other, mine)], 0)
    for pair in range(2):
        k1, v1 = twice(k, pair), ones_beside(v, pair)
        sums, tops = [], []
        for qh in spread(q, pair):
            s = scores(qh, k1)
            m = jnp.max(s, axis=1, keepdims=True)
            sums.append(jnp.dot(jnp.exp2(s - m).astype(BF16), v1, preferred_element_type=F32))
            tops.append(m)
        cols = pl.ds(pair * 128, 128)
        o = select(sums[0][:, :128], sums[1][:, :128])
        l = select(sums[0][:, 128:], sums[1][:, 128:])
        m = select(*tops)
        before = m_ref[:, cols]
        top = jnp.maximum(m, before)
        a, b = jnp.exp2(before - top), jnp.exp2(m - top)
        out = (o * b + o_ref[:, cols] * a) / (l * b + l_ref[:, cols] * a)
        out_ref[:, cols] = out.astype(BF16)


def project_kernel(*refs):
    out_ref = refs[8]
    total = jnp.dot(refs[0][...], refs[4][...], preferred_element_type=F32)
    for i in range(1, 4):
        total = total + jnp.dot(refs[i][...], refs[4 + i][...], preferred_element_type=F32)
    out_ref[...] = total.astype(BF16)


def body(queries, keys_values, out_weight):
    shards = lax.axis_size("ctx")
    heads = lax.axis_size("head")
    place = lax.axis_index("ctx")
    rank = lax.axis_index("head")
    at = jnp.stack([rank, place]).astype(jnp.int32)

    def swap(x, bits):
        return lax.ppermute(x, "ctx", [(i, i ^ bits) for i in range(shards)])

    def turn(x, by):
        return lax.ppermute(x, "head", [(i, (i + by) % heads) for i in range(heads)])

    pyr, face, back = call(
        pyramid_kernel,
        "pyramid",
        [((2, 1792, WIDE), BF16), ((2, 2 * BLK, WIDE), BF16), ((2, BLK, WIDE), BF16)],
        (at, keys_values),
    )
    turns = (3, 1, 2, 0)
    sibling = swap(face, 1)
    ends = [(i, i + 1) for i in range(1, shards - 1, 2)]
    back = lax.ppermute(back, "ctx", ends + [(b, a) for a, b in ends])
    near, panels = [], []
    mine, other = face, sibling
    weights = [turn(out_weight, by) for by in turns[:3]]
    for step, bits in enumerate((2, 6, 8, 16, 56), 1):
        if step == 4:
            other, weights[0] = lax.optimization_barrier((other, weights[0]))
        if step == 5:
            other, *weights = lax.optimization_barrier((other, *weights))
        (mine,) = call(
            functools.partial(climb_kernel, step), "climb", [((BLK, WIDE), BF16)], (at, mine, other)
        )
        other = swap(mine, bits)
        if step <= 4:
            gate = lax.optimization_barrier((queries, mine))[0]
            state = call(
                functools.partial(near_kernel, turns[step - 1], shards),
                "near",
                [((CHUNK, WIDE), F32)] * 3,
                (at, gate, keys_values, pyr, sibling, back),
            )
            other, state[0] = lax.optimization_barrier((other, state[0]))
            near.append(state)
        panels.append(other)
    held = jnp.stack(panels)
    theirs = swap(held, 1)
    atts = []
    for by, state in zip(turns, near):
        (att,) = call(
            functools.partial(far_kernel, by),
            "far",
            [((CHUNK, WIDE), BF16)],
            (at, queries, *state, sibling, held, theirs),
        )
        atts.append(turn(att, by) if by else att)
    (out,) = call(
        project_kernel, "project", [((CHUNK, 1024), BF16)], (*atts, *weights, out_weight), n_scalar=0
    )
    return out


def solution(mesh):
    in_specs = (P("ctx", "head"), P(None, "ctx", "head"), P("head", None))
    out_specs = P(("ctx", "head"), None)
    return jax.shard_map(body, mesh=mesh, in_specs=in_specs, out_specs=out_specs, check_vma=False)
```

profile of v0, /device:TPU:1, one launch (start us, length us, event | category | flops | bytes accessed | tf_op | source)
XLA Modules:
  0.0 74.3 jit_solution(2524432077615635878)
XLA Ops:
  0.0 0.0 copy-start
  0.0 0.1 pad_add_fusion.at_ref
  0.1 0.0 copy-start.1
  0.1 1.7 %copy-done.1 = bf16[2,2048,256]{2,1,0:T(8,128)(2,1)S(1)} copy-done((bf16[2,2048,256]{2,1,0:T(8,128)(2,1)S(1)}, bf16[2,2048,256]{2,1,0:T(8,128)(2,1)}, u32[]{:S(2)}) %copy-start.1) | copy-done | bytes 2097176
  1.7 0.0 copy-start.4
  1.7 1.4 %pyramid.1 = (bf16[2,1792,256]{2,1,0:T(8,128)(2,1)S(1)}, bf16[2,256,256]{2,1,0:T(8,128)(2,1)S(1)}, bf16[2,128,256]{2,1,0:T(8,128)(2,1)S(1)}) custom-call(s32[2]{0:T(128)S(1)} %pad_add_fusion.at_ref, bf16[2,2048,256]{2,1,0:T(8,128)(2,1)S(1)} %copy-done.1), custom_call_target="tpu_custom_call" | custom-call | tf_op jit(solution)/shard_map/pyramid/pallas_call | solution.py:27
  3.2 3.3 %collective-permute-start = (bf16[2,256,256]{2,1,0:T(8,128)(2,1)S(1)}, bf16[2,256,256]{2,1,0:T(8,128)(2,1)S(1)}, u32[]{:S(2)}, u32[]{:S(2)}) collective-permute-start(bf16[2,256,256]{2,1,0:T(8,128)(2,1)S(1)} %get-tuple-element.38.mine_ref), channel_id=1, source_target_pairs={{0,4},{4,0},{8,12},{12,8},{16,20},{20,16},{24,28},{28,24},{32,36},... | collective-permute-start | bytes 786440 | tf_op jit(solution)/shard_map/ppermute | solution.py:208
  6.5 1.9 %collective-permute-start.2 = (bf16[2,128,256]{2,1,0:T(8,128)(2,1)S(1)}, bf16[2,128,256]{2,1,0:T(8,128)(2,1)S(1)}, u32[]{:S(2)}, u32[]{:S(2)}) collective-permute-start(bf16[2,128,256]{2,1,0:T(8,128)(2,1)S(1)} %get-tuple-element.41), channel_id=1, source_target_pairs={{4,8},{12,16},{20,24},{28,32},{36,40},{44,48},{52,56},{60,64},{68,... | collective-permute-start | bytes 393224 | tf_op jit(solution)/shard_map/ppermute | solution.py:222
  8.4 0.0 copy-done.4
  8.5 2.2 %collective-permute-start.5 = (bf16[256,1024]{1,0:T(8,128)(2,1)S(1)}, bf16[256,1024]{1,0:T(8,128)(2,1)S(1)}, u32[]{:S(2)}, u32[]{:S(2)}) collective-permute-start(bf16[256,1024]{1,0:T(8,128)(2,1)S(1)} %copy-done.4), channel_id=1, source_target_pairs={{0,3},{1,0},{2,1},{3,2},{4,7},{5,4},{6,5},{7,6},{8,11},{9,8},{10,9... | collective-permute-start | bytes 1572872 | tf_op jit(solution)/shard_map/ppermute | solution.py:211
  10.6 0.0 collective-permute-done.other_ref.face_ref
  10.6 0.7 climb.5.mine_ref
  11.3 1.3 %collective-permute-start.1 = (bf16[128,256]{1,0:T(8,128)(2,1)S(1)}, bf16[128,256]{1,0:T(8,128)(2,1)S(1)}, u32[]{:S(2)}, u32[]{:S(2)}) collective-permute-start(bf16[128,256]{1,0:T(8,128)(2,1)S(1)} %climb.5.mine_ref), channel_id=1, source_target_pairs={{0,8},{4,12},{8,0},{12,4},{16,24},{20,28},{24,16},{28,20},{32,40},... | collective-permute-start | bytes 196616 | tf_op jit(solution)/shard_map/ppermute | solution.py:208
  12.6 0.0 collective-permute-start.7
  12.6 1.7 %collective-permute-start.8 = (bf16[256,1024]{1,0:T(8,128)(2,1)S(1)}, bf16[256,1024]{1,0:T(8,128)(2,1)S(1)}, u32[]{:S(2)}, u32[]{:S(2)}) collective-permute-start(bf16[256,1024]{1,0:T(8,128)(2,1)S(1)} %copy-done.4), channel_id=1, source_target_pairs={{0,2},{1,3},{2,0},{3,1},{4,6},{5,7},{6,4},{7,5},{8,10},{9,11},{10,... | collective-permute-start | bytes 1572872 | tf_op jit(solution)/shard_map/ppermute | solution.py:211
  14.3 0.0 collective-permute-done.2.back_ref
  14.3 0.0 copy-done
  14.3 0.0 copy-start.2
  14.3 1.6 %copy-done.2 = bf16[2,2048,256]{2,1,0:T(8,128)(2,1)S(1)} copy-done((bf16[2,2048,256]{2,1,0:T(8,128)(2,1)S(1)}, bf16[2,2048,256]{2,1,0:T(8,128)(2,1)}, u32[]{:S(2)}) %copy-start.2) | copy-done | bytes 2097176
  15.9 0.0 copy-start.3
  15.9 3.3 %near.4 = (f32[512,256]{1,0:T(8,128)S(1)}, f32[512,256]{1,0:T(8,128)S(1)}, f32[512,256]{1,0:T(8,128)S(1)}) custom-call(s32[2]{0:T(128)S(1)} %pad_add_fusion.at_ref, bf16[2048,256]{1,0:T(8,128)(2,1)S(1)} %copy-done, bf16[2,2048,256]{2,1,0:T(8,128)(2,1)S(1)} %copy-done.2, bf16[2,1792,256]{2,1,0:T(8,128)(2,1)S(1)} %get-tuple-element.40.pyr_ref, ...), custom_call_target="tpu_custom_call" | custom-call | tf_op jit(solution)/shard_map/near/pallas_call | solution.py:27
  19.2 0.0 collective-permute-done.1.other_ref
  19.2 0.7 climb.6.mine_ref
  19.9 1.8 %collective-permute-start.3 = (bf16[128,256]{1,0:T(8,128)(2,1)S(1)}, bf16[128,256]{1,0:T(8,128)(2,1)S(1)}, u32[]{:S(2)}, u32[]{:S(2)}) collective-permute-start(bf16[128,256]{1,0:T(8,128)(2,1)S(1)} %climb.6.mine_ref), channel_id=1, source_target_pairs={{0,24},{4,28},{8,16},{12,20},{16,8},{20,12},{24,0},{28,4},{32,56},... | collective-permute-start | bytes 196616 | tf_op jit(solution)/shard_map/ppermute | solution.py:208
  21.6 0.0 copy-done.3
  21.7 3.3 %near.5 = (f32[512,256]{1,0:T(8,128)S(1)}, f32[512,256]{1,0:T(8,128)S(1)}, f32[512,256]{1,0:T(8,128)S(1)}) custom-call(s32[2]{0:T(128)S(1)} %pad_add_fusion.at_ref, bf16[2048,256]{1,0:T(8,128)(2,1)S(1)} %copy-done, bf16[2,2048,256]{2,1,0:T(8,128)(2,1)S(1)} %copy-done.3, bf16[2,1792,256]{2,1,0:T(8,128)(2,1)S(1)} %get-tuple-element.40.pyr_ref, ...), custom_call_target="tpu_custom_call" | custom-call | tf_op jit(solution)/shard_map/near/pallas_call | solution.py:27
  24.9 0.0 collective-permute-done.3.other_ref
  24.9 0.7 climb.7.mine_ref
  25.6 1.9 %collective-permute-start.4 = (bf16[128,256]{1,0:T(8,128)(2,1)S(1)}, bf16[128,256]{1,0:T(8,128)(2,1)S(1)}, u32[]{:S(2)}, u32[]{:S(2)}) collective-permute-start(bf16[128,256]{1,0:T(8,128)(2,1)S(1)} %climb.7.mine_ref), channel_id=1, source_target_pairs={{0,32},{4,36},{8,40},{12,44},{16,48},{20,52},{24,56},{28,60},{32,0... | collective-permute-start | bytes 196616 | tf_op jit(solution)/shard_map/ppermute | solution.py:208
  27.5 3.3 %near.6 = (f32[512,256]{1,0:T(8,128)S(1)}, f32[512,256]{1,0:T(8,128)S(1)}, f32[512,256]{1,0:T(8,128)S(1)}) custom-call(s32[2]{0:T(128)S(1)} %pad_add_fusion.at_ref, bf16[2048,256]{1,0:T(8,128)(2,1)S(1)} %copy-done, bf16[2,2048,256]{2,1,0:T(8,128)(2,1)S(1)} %copy-done.3, bf16[2,1792,256]{2,1,0:T(8,128)(2,1)S(1)} %get-tuple-element.40.pyr_ref, ...), custom_call_target="tpu_custom_call" | custom-call | tf_op jit(solution)/shard_map/near/pallas_call | solution.py:27
  30.8 0.0 collective-permute-done.4.other_ref
  30.8 0.0 collective-permute-done.5.refs_4_
  30.8 0.7 climb.8.mine_ref
  31.5 4.3 %collective-permute-start.6 = (bf16[128,256]{1,0:T(8,128)(2,1)S(1)}, bf16[128,256]{1,0:T(8,128)(2,1)S(1)}, u32[]{:S(2)}, u32[]{:S(2)}) collective-permute-start(bf16[128,256]{1,0:T(8,128)(2,1)S(1)} %climb.8.mine_ref), channel_id=1, source_target_pairs={{0,64},{4,68},{8,72},{12,76},{16,80},{20,84},{24,88},{28,92},{32,9... | collective-permute-start | bytes 196616 | tf_op jit(solution)/shard_map/ppermute | solution.py:208
  35.8 3.3 %near.7 = (f32[512,256]{1,0:T(8,128)S(1)}, f32[512,256]{1,0:T(8,128)S(1)}, f32[512,256]{1,0:T(8,128)S(1)}) custom-call(s32[2]{0:T(128)S(1)} %pad_add_fusion.at_ref, bf16[2048,256]{1,0:T(8,128)(2,1)S(1)} %copy-done, bf16[2,2048,256]{2,1,0:T(8,128)(2,1)S(1)} %copy-done.3, bf16[2,1792,256]{2,1,0:T(8,128)(2,1)S(1)} %get-tuple-element.40.pyr_ref, ...), custom_call_target="tpu_custom_call" | custom-call | tf_op jit(solution)/shard_map/near/pallas_call | solution.py:27
  39.1 0.0 collective-permute-done.6.other_ref
  39.1 0.0 collective-permute-done.7.refs_5_
  39.1 0.0 collective-permute-done.8.refs_6_
  39.1 0.7 climb.9
  39.8 2.7 %collective-permute-start.9 = (bf16[128,256]{1,0:T(8,128)(2,1)S(1)}, bf16[128,256]{1,0:T(8,128)(2,1)S(1)}, u32[]{:S(2)}, u32[]{:S(2)}) collective-permute-start(bf16[128,256]{1,0:T(8,128)(2,1)S(1)} %climb.9), channel_id=1, source_target_pairs={{0,224},{4,228},{8,232},{12,236},{16,240},{20,244},{24,248},{28,25... | collective-permute-start | bytes 196616 | tf_op jit(solution)/shard_map/ppermute | solution.py:208
  42.5 1.7 %collective-permute-done.9 = bf16[128,256]{1,0:T(8,128)(2,1)S(1)} collective-permute-done((bf16[128,256]{1,0:T(8,128)(2,1)S(1)}, bf16[128,256]{1,0:T(8,128)(2,1)S(1)}, u32[]{:S(2)}, u32[]{:S(2)}) %collective-permute-start.9) | collective-permute-done | bytes 65568 | tf_op jit(solution)/shard_map/ppermute | solution.py:208
  44.2 6.1 %collective-permute-start.10 = (bf16[5,128,256]{2,1,0:T(8,128)(2,1)S(1)}, bf16[5,128,256]{2,1,0:T(8,128)(2,1)S(1)}, u32[]{:S(2)}, u32[]{:S(2)}) collective-permute-start(bf16[5,128,256]{2,1,0:T(8,128)(2,1)S(1)} %bitcast_dynamic-update-slice_fusion.mine_ref), channel_id=1, source_target_pairs={{0,4},{4,0},{8,12},{12,8},{16,20},{20,16},{24,28},{28,24},{32,36},... | collective-permute-start | bytes 983048 | tf_op jit(solution)/shard_map/ppermute | solution.py:208
  50.4 1.3 %collective-permute-done.10.other_ref = bf16[5,128,256]{2,1,0:T(8,128)(2,1)S(1)} collective-permute-done((bf16[5,128,256]{2,1,0:T(8,128)(2,1)S(1)}, bf16[5,128,256]{2,1,0:T(8,128)(2,1)S(1)}, u32[]{:S(2)}, u32[]{:S(2)}) %collective-permute-start.10) | collective-permute-done | bytes 327712 | tf_op jit(solution)/shard_map/ppermute | solution.py:208
  51.6 3.1 %far.6 = bf16[512,256]{1,0:T(8,128)(2,1)S(1)} custom-call(s32[2]{0:T(128)S(1)} %pad_add_fusion.at_ref, bf16[2048,256]{1,0:T(8,128)(2,1)S(1)} %copy-done, f32[512,256]{1,0:T(8,128)S(1)} %get-tuple-element.62.o_ref, f32[512,256]{1,0:T(8,128)S(1)} %get-tuple-element.63.l_ref, f32[512,256]{1,0:T(8,128)S(1)} %get-tuple-element.64.m_ref, ...), custom_call_target="tpu_custom_call" | custom-call | tf_op jit(solution)/shard_map/far/pallas_call | solution.py:27
  54.7 0.3 collective-permute-start.13
  55.0 3.1 %far.5 = bf16[512,256]{1,0:T(8,128)(2,1)S(1)} custom-call(s32[2]{0:T(128)S(1)} %pad_add_fusion.at_ref, bf16[2048,256]{1,0:T(8,128)(2,1)S(1)} %copy-done, f32[512,256]{1,0:T(8,128)S(1)} %get-tuple-element.59.o_ref, f32[512,256]{1,0:T(8,128)S(1)} %get-tuple-element.60.l_ref, f32[512,256]{1,0:T(8,128)S(1)} %get-tuple-element.61.m_ref, ...), custom_call_target="tpu_custom_call" | custom-call | tf_op jit(solution)/shard_map/far/pallas_call | solution.py:27
  58.1 3.9 %collective-permute-start.12 = (bf16[512,256]{1,0:T(8,128)(2,1)S(1)}, bf16[512,256]{1,0:T(8,128)(2,1)S(1)}, u32[]{:S(2)}, u32[]{:S(2)}) collective-permute-start(bf16[512,256]{1,0:T(8,128)(2,1)S(1)} %far.5), channel_id=1, source_target_pairs={{0,1},{1,2},{2,3},{3,0},{4,5},{5,6},{6,7},{7,4},{8,9},{9,10},{10,1... | collective-permute-start | bytes 786440 | tf_op jit(solution)/shard_map/ppermute | solution.py:211
  62.0 3.1 %far.4 = bf16[512,256]{1,0:T(8,128)(2,1)S(1)} custom-call(s32[2]{0:T(128)S(1)} %pad_add_fusion.at_ref, bf16[2048,256]{1,0:T(8,128)(2,1)S(1)} %copy-done, f32[512,256]{1,0:T(8,128)S(1)} %get-tuple-element.43.o_ref, f32[512,256]{1,0:T(8,128)S(1)} %get-tuple-element.44.l_ref, f32[512,256]{1,0:T(8,128)S(1)} %get-tuple-element.45.m_ref, ...), custom_call_target="tpu_custom_call" | custom-call | tf_op jit(solution)/shard_map/far/pallas_call | solution.py:27
  65.1 0.1 collective-permute-start.11
  65.2 3.1 %far.7.refs_3_ = bf16[512,256]{1,0:T(8,128)(2,1)S(1)} custom-call(s32[2]{0:T(128)S(1)} %pad_add_fusion.at_ref, bf16[2048,256]{1,0:T(8,128)(2,1)S(1)} %copy-done, f32[512,256]{1,0:T(8,128)S(1)} %get-tuple-element.65.o_ref, f32[512,256]{1,0:T(8,128)S(1)} %get-tuple-element.66.l_ref, f32[512,256]{1,0:T(8,128)S(1)} %get-tuple-element.67.m_ref, ...), custom_call_target="tpu_custom_call" | custom-call | tf_op jit(solution)/shard_map/far/pallas_call | solution.py:27
  68.3 0.0 collective-permute-done.13.refs_2_
  68.3 2.1 %collective-permute-done.12.refs_1_ = bf16[512,256]{1,0:T(8,128)(2,1)S(1)} collective-permute-done((bf16[512,256]{1,0:T(8,128)(2,1)S(1)}, bf16[512,256]{1,0:T(8,128)(2,1)S(1)}, u32[]{:S(2)}, u32[]{:S(2)}) %collective-permute-start.12) | collective-permute-done | bytes 262176 | tf_op jit(solution)/shard_map/ppermute | solution.py:211
  70.4 1.7 %collective-permute-done.11.refs_0_ = bf16[512,256]{1,0:T(8,128)(2,1)S(1)} collective-permute-done((bf16[512,256]{1,0:T(8,128)(2,1)S(1)}, bf16[512,256]{1,0:T(8,128)(2,1)S(1)}, u32[]{:S(2)}, u32[]{:S(2)}) %collective-permute-start.11) | collective-permute-done | bytes 262176 | tf_op jit(solution)/shard_map/ppermute | solution.py:211
  72.1 2.2 %project.1 = bf16[512,1024]{1,0:T(8,128)(2,1)} custom-call(bf16[512,256]{1,0:T(8,128)(2,1)S(1)} %collective-permute-done.11.refs_0_, bf16[512,256]{1,0:T(8,128)(2,1)S(1)} %collective-permute-done.12.refs_1_, bf16[512,256]{1,0:T(8,128)(2,1)S(1)} %collective-permute-done.13.refs_2_, bf16[512,256]{1,0:T(8,128)(2,1)S(1)} %far.7.refs_3_, ...), custom_call_target="tpu_custom_call" | custom-call | tf_op jit(solution)/shard_map/project/pallas_call | solution.py:27
  (5 shorter events, 0.0 us)
Async XLA Ops:
  0.0 14.3 %copy-start = (bf16[2048,256]{1,0:T(8,128)(2,1)S(1)}, bf16[2048,256]{1,0:T(8,128)(2,1)}, u32[]{:S(2)}) copy-start(bf16[2048,256]{1,0:T(8,128)(2,1)} %q_ref.11) | copy-start | bytes 3145732
  0.1 1.7 %copy-start.1 = (bf16[2,2048,256]{2,1,0:T(8,128)(2,1)S(1)}, bf16[2,2048,256]{2,1,0:T(8,128)(2,1)}, u32[]{:S(2)}) copy-start(bf16[2,2048,256]{2,1,0:T(8,128)(2,1)} %kv_ref.9) | copy-start | bytes 6291460
  1.7 6.7 %copy-start.4 = (bf16[256,1024]{1,0:T(8,128)(2,1)S(1)}, bf16[256,1024]{1,0:T(8,128)(2,1)}, u32[]{:S(2)}) copy-start(bf16[256,1024]{1,0:T(8,128)(2,1)} %refs_7_.1) | copy-start | bytes 1572868
  3.2 7.4 %collective-permute-start = (bf16[2,256,256]{2,1,0:T(8,128)(2,1)S(1)}, bf16[2,256,256]{2,1,0:T(8,128)(2,1)S(1)}, u32[]{:S(2)}, u32[]{:S(2)}) collective-permute-start(bf16[2,256,256]{2,1,0:T(8,128)(2,1)S(1)} %get-tuple-element.38.mine_ref), channel_id=1, source_target_pairs={{0,4},{4,0},{8,12},{12,8},{16,20},{20,16},{24,28},{28,24},{32,36},... | collective-permute-start | bytes 786440 | tf_op jit(solution)/shard_map/ppermute | solution.py:208
  6.5 7.8 %collective-permute-start.2 = (bf16[2,128,256]{2,1,0:T(8,128)(2,1)S(1)}, bf16[2,128,256]{2,1,0:T(8,128)(2,1)S(1)}, u32[]{:S(2)}, u32[]{:S(2)}) collective-permute-start(bf16[2,128,256]{2,1,0:T(8,128)(2,1)S(1)} %get-tuple-element.41), channel_id=1, source_target_pairs={{4,8},{12,16},{20,24},{28,32},{36,40},{44,48},{52,56},{60,64},{68,... | collective-permute-start | bytes 393224 | tf_op jit(solution)/shard_map/ppermute | solution.py:222
  8.5 22.4 %collective-permute-start.5 = (bf16[256,1024]{1,0:T(8,128)(2,1)S(1)}, bf16[256,1024]{1,0:T(8,128)(2,1)S(1)}, u32[]{:S(2)}, u32[]{:S(2)}) collective-permute-start(bf16[256,1024]{1,0:T(8,128)(2,1)S(1)} %copy-done.4), channel_id=1, source_target_pairs={{0,3},{1,0},{2,1},{3,2},{4,7},{5,4},{6,5},{7,6},{8,11},{9,8},{10,9... | collective-permute-start | bytes 1572872 | tf_op jit(solution)/shard_map/ppermute | solution.py:211
  11.3 7.8 %collective-permute-start.1 = (bf16[128,256]{1,0:T(8,128)(2,1)S(1)}, bf16[128,256]{1,0:T(8,128)(2,1)S(1)}, u32[]{:S(2)}, u32[]{:S(2)}) collective-permute-start(bf16[128,256]{1,0:T(8,128)(2,1)S(1)} %climb.5.mine_ref), channel_id=1, source_target_pairs={{0,8},{4,12},{8,0},{12,4},{16,24},{20,28},{24,16},{28,20},{32,40},... | collective-permute-start | bytes 196616 | tf_op jit(solution)/shard_map/ppermute | solution.py:208
  12.6 26.4 %collective-permute-start.7 = (bf16[256,1024]{1,0:T(8,128)(2,1)S(1)}, bf16[256,1024]{1,0:T(8,128)(2,1)S(1)}, u32[]{:S(2)}, u32[]{:S(2)}) collective-permute-start(bf16[256,1024]{1,0:T(8,128)(2,1)S(1)} %copy-done.4), channel_id=1, source_target_pairs={{0,1},{1,2},{2,3},{3,0},{4,5},{5,6},{6,7},{7,4},{8,9},{9,10},{10,1... | collective-permute-start | bytes 1572872 | tf_op jit(solution)/shard_map/ppermute | solution.py:211
  12.6 26.4 %collective-permute-start.8 = (bf16[256,1024]{1,0:T(8,128)(2,1)S(1)}, bf16[256,1024]{1,0:T(8,128)(2,1)S(1)}, u32[]{:S(2)}, u32[]{:S(2)}) collective-permute-start(bf16[256,1024]{1,0:T(8,128)(2,1)S(1)} %copy-done.4), channel_id=1, source_target_pairs={{0,2},{1,3},{2,0},{3,1},{4,6},{5,7},{6,4},{7,5},{8,10},{9,11},{10,... | collective-permute-start | bytes 1572872 | tf_op jit(solution)/shard_map/ppermute | solution.py:211
  14.3 1.6 %copy-start.2 = (bf16[2,2048,256]{2,1,0:T(8,128)(2,1)S(1)}, bf16[2,2048,256]{2,1,0:T(8,128)(2,1)}, u32[]{:S(2)}) copy-start(bf16[2,2048,256]{2,1,0:T(8,128)(2,1)} %kv_ref.9) | copy-start | bytes 6291460
  15.9 5.7 %copy-start.3 = (bf16[2,2048,256]{2,1,0:T(8,128)(2,1)S(1)}, bf16[2,2048,256]{2,1,0:T(8,128)(2,1)}, u32[]{:S(2)}) copy-start(bf16[2,2048,256]{2,1,0:T(8,128)(2,1)} %kv_ref.9) | copy-start | bytes 6291460
  19.9 5.1 %collective-permute-start.3 = (bf16[128,256]{1,0:T(8,128)(2,1)S(1)}, bf16[128,256]{1,0:T(8,128)(2,1)S(1)}, u32[]{:S(2)}, u32[]{:S(2)}) collective-permute-start(bf16[128,256]{1,0:T(8,128)(2,1)S(1)} %climb.6.mine_ref), channel_id=1, source_target_pairs={{0,24},{4,28},{8,16},{12,20},{16,8},{20,12},{24,0},{28,4},{32,56},... | collective-permute-start | bytes 196616 | tf_op jit(solution)/shard_map/ppermute | solution.py:208
  25.6 5.2 %collective-permute-start.4 = (bf16[128,256]{1,0:T(8,128)(2,1)S(1)}, bf16[128,256]{1,0:T(8,128)(2,1)S(1)}, u32[]{:S(2)}, u32[]{:S(2)}) collective-permute-start(bf16[128,256]{1,0:T(8,128)(2,1)S(1)} %climb.7.mine_ref), channel_id=1, source_target_pairs={{0,32},{4,36},{8,40},{12,44},{16,48},{20,52},{24,56},{28,60},{32,0... | collective-permute-start | bytes 196616 | tf_op jit(solution)/shard_map/ppermute | solution.py:208
  31.5 7.6 %collective-permute-start.6 = (bf16[128,256]{1,0:T(8,128)(2,1)S(1)}, bf16[128,256]{1,0:T(8,128)(2,1)S(1)}, u32[]{:S(2)}, u32[]{:S(2)}) collective-permute-start(bf16[128,256]{1,0:T(8,128)(2,1)S(1)} %climb.8.mine_ref), channel_id=1, source_target_pairs={{0,64},{4,68},{8,72},{12,76},{16,80},{20,84},{24,88},{28,92},{32,9... | collective-permute-start | bytes 196616 | tf_op jit(solution)/shard_map/ppermute | solution.py:208
  39.8 4.4 %collective-permute-start.9 = (bf16[128,256]{1,0:T(8,128)(2,1)S(1)}, bf16[128,256]{1,0:T(8,128)(2,1)S(1)}, u32[]{:S(2)}, u32[]{:S(2)}) collective-permute-start(bf16[128,256]{1,0:T(8,128)(2,1)S(1)} %climb.9), channel_id=1, source_target_pairs={{0,224},{4,228},{8,232},{12,236},{16,240},{20,244},{24,248},{28,25... | collective-permute-start | bytes 196616 | tf_op jit(solution)/shard_map/ppermute | solution.py:208
  44.2 7.4 %collective-permute-start.10 = (bf16[5,128,256]{2,1,0:T(8,128)(2,1)S(1)}, bf16[5,128,256]{2,1,0:T(8,128)(2,1)S(1)}, u32[]{:S(2)}, u32[]{:S(2)}) collective-permute-start(bf16[5,128,256]{2,1,0:T(8,128)(2,1)S(1)} %bitcast_dynamic-update-slice_fusion.mine_ref), channel_id=1, source_target_pairs={{0,4},{4,0},{8,12},{12,8},{16,20},{20,16},{24,28},{28,24},{32,36},... | collective-permute-start | bytes 983048 | tf_op jit(solution)/shard_map/ppermute | solution.py:208
  54.7 13.6 %collective-permute-start.13 = (bf16[512,256]{1,0:T(8,128)(2,1)S(1)}, bf16[512,256]{1,0:T(8,128)(2,1)S(1)}, u32[]{:S(2)}, u32[]{:S(2)}) collective-permute-start(bf16[512,256]{1,0:T(8,128)(2,1)S(1)} %far.6), channel_id=1, source_target_pairs={{0,2},{1,3},{2,0},{3,1},{4,6},{5,7},{6,4},{7,5},{8,10},{9,11},{10,... | collective-permute-start | bytes 786440 | tf_op jit(solution)/shard_map/ppermute | solution.py:211
  58.1 12.3 %collective-permute-start.12 = (bf16[512,256]{1,0:T(8,128)(2,1)S(1)}, bf16[512,256]{1,0:T(8,128)(2,1)S(1)}, u32[]{:S(2)}, u32[]{:S(2)}) collective-permute-start(bf16[512,256]{1,0:T(8,128)(2,1)S(1)} %far.5), channel_id=1, source_target_pairs={{0,1},{1,2},{2,3},{3,0},{4,5},{5,6},{6,7},{7,4},{8,9},{9,10},{10,1... | collective-permute-start | bytes 786440 | tf_op jit(solution)/shard_map/ppermute | solution.py:211
  65.1 7.0 %collective-permute-start.11 = (bf16[512,256]{1,0:T(8,128)(2,1)S(1)}, bf16[512,256]{1,0:T(8,128)(2,1)S(1)}, u32[]{:S(2)}, u32[]{:S(2)}) collective-permute-start(bf16[512,256]{1,0:T(8,128)(2,1)S(1)} %far.4), channel_id=1, source_target_pairs={{0,3},{1,0},{2,1},{3,2},{4,7},{5,4},{6,5},{7,6},{8,11},{9,8},{10,9... | collective-permute-start | bytes 786440 | tf_op jit(solution)/shard_map/ppermute | solution.py:211
where the time goes:
time: 75.3 us; the launch traced here: 74.3 us
  Pallas kernels  32.4 us (43%)
  starting transfers between devices  31.5 us (42%)
  waiting for transfers between devices  6.74 us (9%)
  local copies, waits for them, and re-layouts  3.29 us (4%)
    pallas_call x15, Pallas kernels, call(): pl.pallas_call(kernel, out_shape=[jax.ShapeDtypeStruct(shape, dtype) for...  32.4 us
    ppermute x7, starting transfers between devices, swap(): return lax.ppermute(x, 'ctx', [(i, i ^ bits) for i in range(shards)])  21.4 us
    ppermute x6, starting transfers between devices, turn(): lax.ppermute(x, 'head', [(i, (i + by) % heads) for i in range(heads)])  8.19 us
    ppermute x6, waiting for transfers between devices, turn(): lax.ppermute(x, 'head', [(i, (i + by) % heads) for i in range(heads)])  3.78 us
    unnamed x14, local copies, waits for them, and re-layouts  3.29 us
    ppermute x7, waiting for transfers between devices, swap(): return lax.ppermute(x, 'ctx', [(i, i ^ bits) for i in range(shards)])  2.95 us
    ppermute x1, starting transfers between devices, body(): back = lax.ppermute(back, 'ctx', ends + [(b, a) for a, b in ends])  1.91 us
  transfers between devices with their start and end apart: 14, of which 4 were waited for; matrix products, arithmetic and copies ran while one was open for 0% of the time, Pallas kernels for 34%

commit v1 on v0

v1 whole, which is shorter than its diff:
```python
import functools
import math

import jax
import jax.numpy as jnp
from jax import lax
from jax.experimental import pallas as pl
from jax.experimental.pallas import tpu as pltpu
from jax.sharding import PartitionSpec as P

HD = 64
BLK = 128
WIDE = 256
CHUNK = 512
SCALE = math.log2(math.e) / math.sqrt(HD)
ROOT = 1.0 / math.sqrt(2.0)
HIDE = -1e30
NT = (((1,), (1,)), ((), ()))
F32 = jnp.float32
BF16 = jnp.bfloat16

VMEM = pl.BlockSpec(memory_space=pltpu.VMEM)
SMEM = pl.BlockSpec(memory_space=pltpu.SMEM)


def call(kernel, name, outs, args, after=(), limit=16):
    n, late = len(args), len(after)
    return list(
        pl.pallas_call(
            lambda *refs: kernel(*refs[:n], *refs[n + late :]),
            out_shape=[jax.ShapeDtypeStruct(shape, dtype) for shape, dtype in outs],
            in_specs=[SMEM] + [VMEM] * (n - 1) + [pl.BlockSpec(memory_space=pl.ANY)] * late,
            out_specs=[VMEM] * len(outs),
            compiler_params=pltpu.CompilerParams(vmem_limit_bytes=limit * 2**20),
            name=name,
        )(*args, *after)
    )


def halve(rows):
    n = rows.shape[0]
    out = lax.broadcasted_iota(jnp.int32, (n // 2, n), 0)
    col = lax.broadcasted_iota(jnp.int32, (n // 2, n), 1)
    pairs = (col // 2 == out).astype(BF16)
    return (jnp.dot(pairs, rows, preferred_element_type=F32) * ROOT).astype(BF16)


def spread(q, pair):
    x = q[:, pair * 128 : pair * 128 + 128].astype(F32) * SCALE
    head = x.astype(BF16)
    rest = (x - head.astype(F32)).astype(BF16)
    low = lax.broadcasted_iota(jnp.int32, head.shape, 1) < HD
    zero = jnp.zeros_like(head)
    return [
        jnp.concatenate([jnp.where(keep, head, zero), jnp.where(keep, rest, zero)], 1)
        for keep in (low, jnp.logical_not(low))
    ]


def twice(k, pair):
    k = k[:, pair * 128 : pair * 128 + 128]
    return jnp.concatenate([k, k], 1)


def ones_beside(v, pair):
    v = v[:, pair * 128 : pair * 128 + 128]
    return jnp.concatenate([v, jnp.ones_like(v)], 1)


def scores(q, k):
    return lax.dot_general(q, k, NT, preferred_element_type=F32)


def select(x0, x1):
    low = lax.broadcasted_iota(jnp.int32, (x0.shape[0], 128), 1) < HD
    return jnp.where(low, x0, x1)


def pyramid_kernel(at_ref, kv_ref, q_ref, lev_ref, face_ref, back_ref):
    even = jnp.bitwise_and(at_ref[1], 1) == 0
    for side in range(2):
        for i in range(8):
            rows = kv_ref[side, pl.ds(i * 256, 256)]
            lev_ref[side, pl.ds(i * 256, 256)] = rows
            lev_ref[side, pl.ds(2048 + i * 128, 128)] = halve(rows)
        first, last = kv_ref[side, pl.ds(0, BLK)], kv_ref[side, pl.ds(2048 - BLK, BLK)]
        face_ref[side, pl.ds(BLK, BLK)] = jnp.where(even, last, first)
        back_ref[side] = jnp.where(even, first, last)
    for side in range(2):
        for i in range(4):
            lev_ref[side, pl.ds(3072 + i * 128, 128)] = halve(lev_ref[side, pl.ds(2048 + i * 256, 256)])
    for side in range(2):
        for i in range(2):
            lev_ref[side, pl.ds(3584 + i * 128, 128)] = halve(lev_ref[side, pl.ds(3072 + i * 256, 256)])
    for side in range(2):
        face_ref[side, pl.ds(0, BLK)] = halve(lev_ref[side, pl.ds(3584, 256)])


def bit_of(at_ref, bit):
    return jnp.bitwise_and(lax.shift_right_logical(at_ref[1], bit), 1) == 0


def ordered(low, mine, other):
    return jnp.concatenate([jnp.where(low, mine, other), jnp.where(low, other, mine)], 0)


def start_kernel(at_ref, mine_ref, other_ref, up_ref, half_ref):
    side = jnp.bitwise_and(at_ref[1], 1)
    up = ordered(
        bit_of(at_ref, 0), halve(mine_ref[side, pl.ds(0, BLK)]), halve(other_ref[side, pl.ds(0, BLK)])
    )
    up_ref[...] = up
    half_ref[...] = halve(up)


def climb(bit, at_ref, mine_ref, near_ref, same_ref, cross_ref):
    low = bit_of(at_ref, bit)
    own = ordered(low, halve(mine_ref[...]), halve(near_ref[...]))
    sibling = ordered(low, same_ref[...], cross_ref[...])
    return sibling, ordered(bit_of(at_ref, bit + 1), halve(own), halve(sibling))


def middle_kernel(at_ref, mine_ref, near_ref, same_ref, cross_ref, w_ref, sib_ref, up_ref, half_ref, w_half_ref):
    sib_ref[...], up = climb(1, at_ref, mine_ref, near_ref, same_ref, cross_ref)
    up_ref[...] = up
    half_ref[...] = halve(up)
    core = jnp.bitwise_and(at_ref[1], 1)
    w_half_ref[...] = w_ref[pl.ds(pl.multiple_of(core * 128, 128), 128)]


def last_kernel(at_ref, mine_ref, near_ref, same_ref, cross_ref, p5_ref, p6_ref, up_ref, held_ref):
    held_ref[0], held_ref[1], held_ref[2] = p5_ref[...], p6_ref[...], near_ref[...]
    held_ref[3], up_ref[...] = climb(3, at_ref, mine_ref, near_ref, same_ref, cross_ref)


def near_chunk(by, shards, at_ref, q_ref, lev_ref, face_ref, back_ref, o_ref, l_ref, m_ref):
    chunk, place = jnp.bitwise_and(at_ref[0] + by, 3), at_ref[1]
    even = jnp.bitwise_and(place, 1) == 0

    def panel(ref, side, start, rows=BLK):
        return ref[side, pl.ds(pl.multiple_of(start, BLK), rows)]
    for t in range(2):
        base = chunk * CHUNK + t * 256
        q = q_ref[pl.ds(pl.multiple_of(base, 256), 256)]
        parts = []
        for side in range(2):
            main = jnp.concatenate([
                panel(lev_ref, side, base, 256),
                panel(lev_ref, side, 2048 + chunk * 256 + (1 - t) * BLK),
                panel(lev_ref, side, 3072 + jnp.bitwise_xor(chunk, 1) * BLK)], 0)
            third = panel(lev_ref, side, 3584 + jnp.bitwise_xor(lax.shift_right_logical(chunk, 1), 1) * BLK)
            if t == 0:
                low = panel(lev_ref, side, jnp.maximum(base - BLK, 0))
                halo = jnp.where(even, back_ref[side], face_ref[side, pl.ds(BLK, BLK)])
                low = jnp.where(chunk == 0, halo, low)
                high = panel(lev_ref, side, base + 256)
            else:
                low = panel(lev_ref, side, base - BLK)
                high = panel(lev_ref, side, jnp.minimum(base + 256, 2048 - BLK))
                halo = jnp.where(even, face_ref[side, pl.ds(BLK, BLK)], back_ref[side])
                high = jnp.where(chunk == 3, halo, high)
            parts.append((main, jnp.concatenate([third, low], 0), jnp.concatenate([third, high], 0)))
        ks, vs = parts
        for pair in range(2):
            h0, h1 = spread(q, pair)
            qs = jnp.concatenate([h0[:128], h1[:128], h0[128:], h1[128:]], 0)
            k1, k2, k3 = [twice(k, pair) for k in ks]
            v1, v2, v3 = [ones_beside(v, pair) for v in vs]
            s1 = scores(qs, k1)
            s2 = scores(qs[:256], k2)
            s3 = scores(qs[256:], k3)
            if t == 0:
                bias = jnp.where((chunk == 0) & (place == 0), HIDE, 0.0)
                s2 = jnp.concatenate([s2[:, :128], s2[:, 128:] + bias], 1)
            else:
                bias = jnp.where((chunk == 3) & (place == shards - 1), HIDE, 0.0)
                s3 = jnp.concatenate([s3[:, :128], s3[:, 128:] + bias], 1)
            s23 = jnp.concatenate([s2, s3], 0)
            m = jnp.max(jnp.concatenate([s1, s23], 1), axis=1, keepdims=True)
            p1 = jnp.exp2(s1 - m).astype(BF16)
            p23 = jnp.exp2(s23 - m).astype(BF16)
            o = jnp.dot(p1, v1, preferred_element_type=F32)
            o = o + jnp.concatenate([jnp.dot(p23[:256], v2, preferred_element_type=F32),
                                     jnp.dot(p23[256:], v3, preferred_element_type=F32)], 0)
            for part in range(2):
                r = part * 256
                rows = pl.ds(t * 256 + part * 128, 128)
                cols = pl.ds(pair * 128, 128)
                o_ref[rows, cols] = select(o[r:r+128, :128], o[r+128:r+256, :128])
                l_ref[rows, cols] = select(o[r:r+128, 128:], o[r+128:r+256, 128:])
                m_ref[rows, cols] = select(m[r:r+128], m[r+128:r+256])


def near_kernel(turns, shards, *refs):
    for i, by in enumerate(turns):
        near_chunk(by, shards, *refs[:5], *refs[5 + 3 * i : 8 + 3 * i])


def far_kernel(by, at_ref, q_ref, o_ref, l_ref, m_ref, face_ref, mine_ref, other_ref, mine9_ref, other9_ref, out_ref):
    chunk, core = jnp.bitwise_and(at_ref[0] + by, 3), jnp.bitwise_and(at_ref[1], 1)
    q = q_ref[pl.ds(pl.multiple_of(chunk * CHUNK, CHUNK), CHUNK)]
    mine, other = [
        jnp.concatenate([four[...].reshape(4 * BLK, WIDE), last[...]], 0)
        for four, last in ((mine_ref, mine9_ref), (other_ref, other9_ref))
    ]
    k = jnp.concatenate([face_ref[0, pl.ds(0, BLK)], jnp.where(core == 0, mine, other)], 0)
    v = jnp.concatenate([face_ref[1, pl.ds(0, BLK)], jnp.where(core == 0, other, mine)], 0)
    for pair in range(2):
        k1, v1 = twice(k, pair), ones_beside(v, pair)
        sums, tops = [], []
        for qh in spread(q, pair):
            s = scores(qh, k1)
            m = jnp.max(s, axis=1, keepdims=True)
            sums.append(jnp.dot(jnp.exp2(s - m).astype(BF16), v1, preferred_element_type=F32))
            tops.append(m)
        cols = pl.ds(pair * 128, 128)
        o = select(sums[0][:, :128], sums[1][:, :128])
        l = select(sums[0][:, 128:], sums[1][:, 128:])
        m = select(*tops)
        before = m_ref[:, cols]
        top = jnp.maximum(m, before)
        a, b = jnp.exp2(before - top), jnp.exp2(m - top)
        out = (o * b + o_ref[:, cols] * a) / (l * b + l_ref[:, cols] * a)
        out_ref[:, cols] = out.astype(BF16)


def times(at_ref, att_ref, mine_ref, other_ref):
    first = jnp.bitwise_and(at_ref[1], 1) == 0
    return jnp.dot(
        att_ref[...], ordered(first, mine_ref[...], other_ref[...]), preferred_element_type=F32
    )


def project_kernel(at_ref, own_ref, w_own_ref, *refs):
    total = jnp.dot(own_ref[...], w_own_ref[...], preferred_element_type=F32)
    for i in range(3):
        total = total + times(at_ref, *refs[3 * i : 3 * i + 3])
    refs[9][...] = total.astype(BF16)


def body(queries, keys_values, out_weight):
    shards = lax.axis_size("ctx")
    heads = lax.axis_size("head")
    place = lax.axis_index("ctx")
    rank = lax.axis_index("head")
    at = jnp.stack([rank, place]).astype(jnp.int32)
    barrier = lax.optimization_barrier

    def swap(x, bits):
        return lax.ppermute(x, "ctx", [(i, i ^ bits) for i in range(shards)])

    def turn(x, by):
        return lax.ppermute(x, "head", [(i, (i + by) % heads) for i in range(heads)])

    panel, half = ((BLK, WIDE), BF16), ((BLK // 2, WIDE), BF16)
    levels, face, back = call(
        pyramid_kernel,
        "pyramid",
        [((2, 3840, WIDE), BF16), ((2, 2 * BLK, WIDE), BF16), ((2, BLK, WIDE), BF16)],
        (at, keys_values, queries),
    )
    turns = (2, 1, 3, 0)
    sibling = swap(face, 1)
    ends = [(i, i + 1) for i in range(1, shards - 1, 2)]
    back = lax.ppermute(back, "ctx", ends + [(b, a) for a, b in ends])

    def near(chunks, gate):
        return call(
            functools.partial(near_kernel, [turns[i] for i in chunks], shards),
            "near",
            [((CHUNK, WIDE), F32)] * (3 * len(chunks)),
            (at, queries, levels, sibling, back),
            (gate,),
        )

    def exchange(up, part, bit):
        return swap(up, 1 << bit), swap(part, 2 << bit), swap(part, 3 << bit)

    up5, part6 = call(start_kernel, "start", [panel, half], (at, face, sibling))
    got = exchange(up5, part6, 1)
    near0 = near((0,), up5)
    *got, near0[0] = barrier((*got, near0[0]))
    p6, up7, part8, w_half = call(
        middle_kernel,
        "middle",
        [panel, panel, half, ((128, 1024), BF16)],
        (at, up5, *got, out_weight),
    )
    p5 = got[0]
    got = exchange(up7, part8, 3)
    near1 = near((1,), up7)
    *got, near1[0] = barrier((*got, near1[0]))
    w2 = turn(w_half, 2)
    up9, held = call(last_kernel, "last", [panel, ((4, BLK, WIDE), BF16)], (at, up7, *got, p5, p6))
    p9 = swap(up9, 56)
    theirs = swap(held, 1)
    near23 = near((2, 3), up9)
    p9, near23[0] = barrier((p9, near23[0]))
    near2, near3 = near23[:3], near23[3:]
    theirs9 = swap(p9, 1)
    w2, source = barrier((w2, w_half))
    w_mine = [w2, turn(source, 1), turn(source, 3)]
    w_other = [swap(w, 1) for w in w_mine]
    atts = []
    for by, state in zip(turns, (near0, near1, near2, near3)):
        (att,) = call(
            functools.partial(far_kernel, by),
            "far",
            [((CHUNK, WIDE), BF16)],
            (at, queries, *state, sibling, held, theirs, p9, theirs9),
        )
        atts.append(turn(att, by) if by else att)
    pieces = list(zip(atts, w_mine, w_other))
    (out,) = call(
        project_kernel,
        "project",
        [((CHUNK, 1024), BF16)],
        (at, atts[3], out_weight, *pieces[2], *pieces[1], *pieces[0]),
    )
    return out


def solution(mesh):
    in_specs = (P("ctx", "head"), P(None, "ctx", "head"), P("head", None))
    out_specs = P(("ctx", "head"), None)
    return jax.shard_map(body, mesh=mesh, in_specs=in_specs, out_specs=out_specs, check_vma=False)
```

time: 75.3 us -> 70 us (0.930); the launches traced: 74.3 us -> 69.9 us
  waiting for transfers between devices: 6.74 us -> 5.08 us
  starting transfers between devices: 31.5 us -> 30.3 us
  Pallas kernels: 32.4 us -> 31.5 us
    ppermute x6, waiting for transfers between devices: 3.78 us -> 2.1 us  [turn(): lax.ppermute(x, 'head', [(i, (i + by) % heads) for i in range(heads)])]
    pallas_call x15 -> x12, Pallas kernels: 32.4 us -> 31.5 us  [call(): pl.pallas_call(lambda *refs: kernel(*refs[:n], *refs[n + late:]), out_sha...]
    ppermute x7 -> x13, waiting for transfers between devices: 2.95 us -> 2.27 us  [swap(): return lax.ppermute(x, 'ctx', [(i, i ^ bits) for i in range(shards)])]
    ppermute x7 -> x13, starting transfers between devices: 21.4 us -> 20.9 us  [swap(): return lax.ppermute(x, 'ctx', [(i, i ^ bits) for i in range(shards)])]
    unnamed x14 -> x8, local copies, waits for them, and re-layouts: 3.29 us -> 2.82 us
  transfers between devices with their start and end apart: 14 -> 20, of which waited for: 4 -> 5; matrix products, arithmetic and copies ran while one was open for 0% -> 0% of each run, Pallas kernels for 34% -> 37%
where the time goes in v1:
time: 70 us; the launch traced here: 69.9 us
  Pallas kernels  31.5 us (45%)
  starting transfers between devices  30.3 us (43%)
  waiting for transfers between devices  5.08 us (7%)
  local copies, waits for them, and re-layouts  2.82 us (4%)
    pallas_call x12, Pallas kernels, call(): pl.pallas_call(lambda *refs: kernel(*refs[:n], *refs[n + late:]), out_sha...  31.5 us
    ppermute x13, starting transfers between devices, swap(): return lax.ppermute(x, 'ctx', [(i, i ^ bits) for i in range(shards)])  20.9 us
    ppermute x6, starting transfers between devices, turn(): lax.ppermute(x, 'head', [(i, (i + by) % heads) for i in range(heads)])  7.46 us
    unnamed x8, local copies, waits for them, and re-layouts  2.82 us
    ppermute x13, waiting for transfers between devices, swap(): return lax.ppermute(x, 'ctx', [(i, i ^ bits) for i in range(shards)])  2.27 us
    ppermute x6, waiting for transfers between devices, turn(): lax.ppermute(x, 'head', [(i, (i + by) % heads) for i in range(heads)])  2.1 us
    ppermute x1, starting transfers between devices, body(): back = lax.ppermute(back, 'ctx', ends + [(b, a) for a, b in ends])  1.91 us
  transfers between devices with their start and end apart: 20, of which 5 were waited for; matrix products, arithmetic and copies ran while one was open for 0% of the time, Pallas kernels for 37%

profile of v1, /device:TPU:1, one launch (start us, length us, event | category | flops | bytes accessed | tf_op | source)
XLA Modules:
  0.0 69.9 jit_solution(6931140831373901650)
XLA Ops:
  0.0 0.1 pad_add_fusion.refs_0_
  0.1 0.0 copy-start
  0.1 1.2 %copy-done = bf16[2048,256]{1,0:T(8,128)(2,1)S(1)} copy-done((bf16[2048,256]{1,0:T(8,128)(2,1)S(1)}, bf16[2048,256]{1,0:T(8,128)(2,1)}, u32[]{:S(2)}) %copy-start) | copy-done | bytes 1048600
  1.3 0.0 copy-start.3
  1.3 1.6 %copy-done.3 = bf16[2,2048,256]{2,1,0:T(8,128)(2,1)S(1)} copy-done((bf16[2,2048,256]{2,1,0:T(8,128)(2,1)S(1)}, bf16[2,2048,256]{2,1,0:T(8,128)(2,1)}, u32[]{:S(2)}) %copy-start.3) | copy-done | bytes 2097176
  2.9 0.0 copy-start.1
  2.9 0.0 copy-start.2
  2.9 1.5 %pyramid.1 = (bf16[2,3840,256]{2,1,0:T(8,128)(2,1)S(1)}, bf16[2,256,256]{2,1,0:T(8,128)(2,1)S(1)}, bf16[2,128,256]{2,1,0:T(8,128)(2,1)S(1)}) custom-call(s32[2]{0:T(128)S(1)} %pad_add_fusion.refs_0_, bf16[2,2048,256]{2,1,0:T(8,128)(2,1)S(1)} %copy-done.3, bf16[2048,256]{1,0:T(8,128)(2,1)S(1)} %copy-done), custom_call_target="tpu_custom_call" | custom-call | tf_op jit(solution)/shard_map/pyramid/pallas_call | solution.py:29
  4.4 3.3 %collective-permute-start = (bf16[2,256,256]{2,1,0:T(8,128)(2,1)S(1)}, bf16[2,256,256]{2,1,0:T(8,128)(2,1)S(1)}, u32[]{:S(2)}, u32[]{:S(2)}) collective-permute-start(bf16[2,256,256]{2,1,0:T(8,128)(2,1)S(1)} %get-tuple-element.41.refs_1_), channel_id=1, source_target_pairs={{0,4},{4,0},{8,12},{12,8},{16,20},{20,16},{24,28},{28,24},{32,36},... | collective-permute-start | bytes 786440 | tf_op jit(solution)/shard_map/ppermute | solution.py:250
  7.7 1.9 %collective-permute-start.1 = (bf16[2,128,256]{2,1,0:T(8,128)(2,1)S(1)}, bf16[2,128,256]{2,1,0:T(8,128)(2,1)S(1)}, u32[]{:S(2)}, u32[]{:S(2)}) collective-permute-start(bf16[2,128,256]{2,1,0:T(8,128)(2,1)S(1)} %get-tuple-element.42), channel_id=1, source_target_pairs={{4,8},{12,16},{20,24},{28,32},{36,40},{44,48},{52,56},{60,64},{68,... | collective-permute-start | bytes 393224 | tf_op jit(solution)/shard_map/ppermute | solution.py:265
  9.7 0.0 collective-permute-done.refs_2_.refs_3_.refs_5_
  9.7 0.8 %start.1 = (bf16[128,256]{1,0:T(8,128)(2,1)S(1)}, bf16[64,256]{1,0:T(8,128)(2,1)S(1)}) custom-call(s32[2]{0:T(128)S(1)} %pad_add_fusion.refs_0_, bf16[2,256,256]{2,1,0:T(8,128)(2,1)S(1)} %get-tuple-element.41.refs_1_, bf16[2,256,256]{2,1,0:T(8,128)(2,1)S(1)} %collective-permute-done.refs_2_.refs_3_.refs_5_), custom_call_target="tpu_custom_call" | custom-call | tf_op jit(solution)/shard_map/start/pallas_call | solution.py:29
  10.5 0.6 collective-permute-start.2
  11.1 2.8 %collective-permute-start.3 = (bf16[64,256]{1,0:T(8,128)(2,1)S(1)}, bf16[64,256]{1,0:T(8,128)(2,1)S(1)}, u32[]{:S(2)}, u32[]{:S(2)}) collective-permute-start(bf16[64,256]{1,0:T(8,128)(2,1)S(1)} %get-tuple-element.44), channel_id=1, source_target_pairs={{0,16},{4,20},{8,24},{12,28},{16,0},{20,4},{24,8},{28,12},{32,48},... | collective-permute-start | bytes 98312 | tf_op jit(solution)/shard_map/ppermute | solution.py:250
  13.9 0.5 collective-permute-start.4
  14.4 0.7 %collective-permute-done.1.refs_4_ = bf16[2,128,256]{2,1,0:T(8,128)(2,1)S(1)} collective-permute-done((bf16[2,128,256]{2,1,0:T(8,128)(2,1)S(1)}, bf16[2,128,256]{2,1,0:T(8,128)(2,1)S(1)}, u32[]{:S(2)}, u32[]{:S(2)}) %collective-permute-start.1) | collective-permute-done | bytes 131104 | tf_op jit(solution)/shard_map/ppermute | solution.py:265
  15.1 0.0 copy-done.1
  15.1 3.3 %near.3 = (f32[512,256]{1,0:T(8,128)S(1)}, f32[512,256]{1,0:T(8,128)S(1)}, f32[512,256]{1,0:T(8,128)S(1)}) custom-call(s32[2]{0:T(128)S(1)} %pad_add_fusion.refs_0_, bf16[2048,256]{1,0:T(8,128)(2,1)S(1)} %copy-done.1, bf16[2,3840,256]{2,1,0:T(8,128)(2,1)S(1)} %get-tuple-element.40.refs_2_, ...), custom_call_target="tpu_custom_call" | custom-call | tf_op jit(solution)/shard_map/near/pallas_call | solution.py:29
  18.4 0.0 collective-permute-done.3.refs_3_
  18.4 0.0 collective-permute-done.4.refs_4_
  18.4 0.0 collective-permute-done.2.refs_2_.refs_5_
  18.4 0.0 copy-done.2
  18.4 1.0 %middle.1 = (bf16[128,256]{1,0:T(8,128)(2,1)S(1)}, bf16[128,256]{1,0:T(8,128)(2,1)S(1)}, bf16[64,256]{1,0:T(8,128)(2,1)S(1)}, bf16[128,1024]{1,0:T(8,128)(2,1)S(1)}) custom-call(s32[2]{0:T(128)S(1)} %pad_add_fusion.refs_0_, bf16[128,256]{1,0:T(8,128)(2,1)S(1)} %get-tuple-element.43.refs_5_.refs_1_, ...), custom_call_target="tpu_custom_call" | custom-call | tf_op jit(solution)/shard_map/middle/pallas_call | solution.py:29
  19.4 2.4 %collective-permute-start.12 = (bf16[128,1024]{1,0:T(8,128)(2,1)S(1)}, bf16[128,1024]{1,0:T(8,128)(2,1)S(1)}, u32[]{:S(2)}, u32[]{:S(2)}) collective-permute-start(bf16[128,1024]{1,0:T(8,128)(2,1)S(1)} %get-tuple-element.67), channel_id=1, source_target_pairs={{0,2},{1,3},{2,0},{3,1},{4,6},{5,7},{6,4},{7,5},{8,10},{9,11},{10,... | collective-permute-start | bytes 786440 | tf_op jit(solution)/shard_map/ppermute | solution.py:253
  21.8 1.6 %collective-permute-start.5 = (bf16[128,256]{1,0:T(8,128)(2,1)S(1)}, bf16[128,256]{1,0:T(8,128)(2,1)S(1)}, u32[]{:S(2)}, u32[]{:S(2)}) collective-permute-start(bf16[128,256]{1,0:T(8,128)(2,1)S(1)} %get-tuple-element.49.refs_5_.refs_1_), channel_id=1, source_target_pairs={{0,32},{4,36},{8,40},{12,44},{16,48},{20,52},{24,56},{28,60},{32,0... | collective-permute-start | bytes 196616 | tf_op jit(solution)/shard_map/ppermute | solution.py:250
  23.4 4.2 %collective-permute-start.6 = (bf16[64,256]{1,0:T(8,128)(2,1)S(1)}, bf16[64,256]{1,0:T(8,128)(2,1)S(1)}, u32[]{:S(2)}, u32[]{:S(2)}) collective-permute-start(bf16[64,256]{1,0:T(8,128)(2,1)S(1)} %get-tuple-element.50), channel_id=1, source_target_pairs={{0,64},{4,68},{8,72},{12,76},{16,80},{20,84},{24,88},{28,92},{32,9... | collective-permute-start | bytes 98312 | tf_op jit(solution)/shard_map/ppermute | solution.py:250
  27.6 0.0 collective-permute-start.7
  27.6 3.3 %near.4 = (f32[512,256]{1,0:T(8,128)S(1)}, f32[512,256]{1,0:T(8,128)S(1)}, f32[512,256]{1,0:T(8,128)S(1)}) custom-call(s32[2]{0:T(128)S(1)} %pad_add_fusion.refs_0_, bf16[2048,256]{1,0:T(8,128)(2,1)S(1)} %copy-done.1, bf16[2,3840,256]{2,1,0:T(8,128)(2,1)S(1)} %get-tuple-element.40.refs_2_, ...), custom_call_target="tpu_custom_call" | custom-call | tf_op jit(solution)/shard_map/near/pallas_call | solution.py:29
  30.9 0.0 collective-permute-done.6.refs_3_
  30.9 1.3 %collective-permute-done.7.refs_4_ = bf16[64,256]{1,0:T(8,128)(2,1)S(1)} collective-permute-done((bf16[64,256]{1,0:T(8,128)(2,1)S(1)}, bf16[64,256]{1,0:T(8,128)(2,1)S(1)}, u32[]{:S(2)}, u32[]{:S(2)}) %collective-permute-start.7) | collective-permute-done | bytes 32800 | tf_op jit(solution)/shard_map/ppermute | solution.py:250
  32.2 0.0 collective-permute-done.5.refs_2_
  32.2 0.9 %last.1 = (bf16[128,256]{1,0:T(8,128)(2,1)S(1)}, bf16[4,128,256]{2,1,0:T(8,128)(2,1)S(1)}) custom-call(s32[2]{0:T(128)S(1)} %pad_add_fusion.refs_0_, bf16[128,256]{1,0:T(8,128)(2,1)S(1)} %get-tuple-element.49.refs_5_.refs_1_, bf16[128,256]{1,0:T(8,128)(2,1)S(1)} %collective-permute-done.5.refs_2_, bf16[64,256]{1,0:T(8,128)(2,1)S(1)} %collective-permute-done.6.refs_3_, ...), custom_call_target="tpu_custom_call" | custom-call | tf_op jit(solution)/shard_map/last/pallas_call | solution.py:29
  33.0 2.2 %collective-permute-start.8 = (bf16[4,128,256]{2,1,0:T(8,128)(2,1)S(1)}, bf16[4,128,256]{2,1,0:T(8,128)(2,1)S(1)}, u32[]{:S(2)}, u32[]{:S(2)}) collective-permute-start(bf16[4,128,256]{2,1,0:T(8,128)(2,1)S(1)} %get-tuple-element.60.refs_6_), channel_id=1, source_target_pairs={{0,4},{4,0},{8,12},{12,8},{16,20},{20,16},{24,28},{28,24},{32,36},... | collective-permute-start | bytes 786440 | tf_op jit(solution)/shard_map/ppermute | solution.py:250
  35.3 0.0 collective-permute-done.12.refs_10_
  35.3 0.8 %collective-permute-start.13 = (bf16[128,1024]{1,0:T(8,128)(2,1)S(1)}, bf16[128,1024]{1,0:T(8,128)(2,1)S(1)}, u32[]{:S(2)}, u32[]{:S(2)}) collective-permute-start(bf16[128,1024]{1,0:T(8,128)(2,1)S(1)} %get-tuple-element.67), channel_id=1, source_target_pairs={{0,3},{1,0},{2,1},{3,2},{4,7},{5,4},{6,5},{7,6},{8,11},{9,8},{10,9... | collective-permute-start | bytes 786440 | tf_op jit(solution)/shard_map/ppermute | solution.py:253
  36.0 0.7 collective-permute-start.16
  36.7 0.8 %collective-permute-start.19 = (bf16[128,1024]{1,0:T(8,128)(2,1)S(1)}, bf16[128,1024]{1,0:T(8,128)(2,1)S(1)}, u32[]{:S(2)}, u32[]{:S(2)}) collective-permute-start(bf16[128,1024]{1,0:T(8,128)(2,1)S(1)} %collective-permute-done.12.refs_10_), channel_id=1, source_target_pairs={{0,4},{4,0},{8,12},{12,8},{16,20},{20,16},{24,28},{28,24},{32,36},... | collective-permute-start | bytes 786440 | tf_op jit(solution)/shard_map/ppermute | solution.py:250
  37.6 3.2 %collective-permute-start.9 = (bf16[128,256]{1,0:T(8,128)(2,1)S(1)}, bf16[128,256]{1,0:T(8,128)(2,1)S(1)}, u32[]{:S(2)}, u32[]{:S(2)}) collective-permute-start(bf16[128,256]{1,0:T(8,128)(2,1)S(1)} %get-tuple-element.56.refs_5_), channel_id=1, source_target_pairs={{0,224},{4,228},{8,232},{12,236},{16,240},{20,244},{24,248},{28,25... | collective-permute-start | bytes 196616 | tf_op jit(solution)/shard_map/ppermute | solution.py:250
  40.8 5.6 %near.5 = (f32[512,256]{1,0:T(8,128)S(1)}, f32[512,256]{1,0:T(8,128)S(1)}, f32[512,256]{1,0:T(8,128)S(1)}, f32[512,256]{1,0:T(8,128)S(1)}, f32[512,256]{1,0:T(8,128)S(1)}, /*index=5*/f32[512,256]{1,0:T(8,128)S(1)}) custom-call(s32[2]{0:T(128)S(1)} %pad_add_fusion.refs_0_, bf16[2048,256]{1,0:T(8,128)(2,1)S(1)} %copy-done.1, ...), custom_call_target="tpu_custom_call" | custom-call | tf_op jit(solution)/shard_map/near/pallas_call | solution.py:29
  46.4 0.0 collective-permute-done.9.refs_8_
  46.4 0.4 collective-permute-start.10
  46.8 1.0 %collective-permute-done.10.refs_9_ = bf16[128,256]{1,0:T(8,128)(2,1)S(1)} collective-permute-done((bf16[128,256]{1,0:T(8,128)(2,1)S(1)}, bf16[128,256]{1,0:T(8,128)(2,1)S(1)}, u32[]{:S(2)}, u32[]{:S(2)}) %collective-permute-start.10) | collective-permute-done | bytes 65568 | tf_op jit(solution)/shard_map/ppermute | solution.py:250
  47.8 0.0 collective-permute-done.8.refs_7_
  47.8 3.1 %far.7 = bf16[512,256]{1,0:T(8,128)(2,1)S(1)} custom-call(s32[2]{0:T(128)S(1)} %pad_add_fusion.refs_0_, bf16[2048,256]{1,0:T(8,128)(2,1)S(1)} %copy-done.1, f32[512,256]{1,0:T(8,128)S(1)} %get-tuple-element.71.refs_2_, f32[512,256]{1,0:T(8,128)S(1)} %get-tuple-element.72.refs_3_, f32[512,256]{1,0:T(8,128)S(1)} %get-tuple-element.73.refs_4_, ...), custom_call_target="tpu_custom_call" | custom-call | tf_op jit(solution)/shard_map/far/pallas_call | solution.py:29
  50.9 0.7 %collective-permute-start.18 = (bf16[512,256]{1,0:T(8,128)(2,1)S(1)}, bf16[512,256]{1,0:T(8,128)(2,1)S(1)}, u32[]{:S(2)}, u32[]{:S(2)}) collective-permute-start(bf16[512,256]{1,0:T(8,128)(2,1)S(1)} %far.7), channel_id=1, source_target_pairs={{0,2},{1,3},{2,0},{3,1},{4,6},{5,7},{6,4},{7,5},{8,10},{9,11},{10,... | collective-permute-start | bytes 786440 | tf_op jit(solution)/shard_map/ppermute | solution.py:253
  51.6 3.1 %far.6 = bf16[512,256]{1,0:T(8,128)(2,1)S(1)} custom-call(s32[2]{0:T(128)S(1)} %pad_add_fusion.refs_0_, bf16[2048,256]{1,0:T(8,128)(2,1)S(1)} %copy-done.1, f32[512,256]{1,0:T(8,128)S(1)} %get-tuple-element.68.refs_2_, f32[512,256]{1,0:T(8,128)S(1)} %get-tuple-element.69.refs_3_, f32[512,256]{1,0:T(8,128)S(1)} %get-tuple-element.70.refs_4_, ...), custom_call_target="tpu_custom_call" | custom-call | tf_op jit(solution)/shard_map/far/pallas_call | solution.py:29
  54.7 2.2 %collective-permute-start.15 = (bf16[512,256]{1,0:T(8,128)(2,1)S(1)}, bf16[512,256]{1,0:T(8,128)(2,1)S(1)}, u32[]{:S(2)}, u32[]{:S(2)}) collective-permute-start(bf16[512,256]{1,0:T(8,128)(2,1)S(1)} %far.6), channel_id=1, source_target_pairs={{0,1},{1,2},{2,3},{3,0},{4,5},{5,6},{6,7},{7,4},{8,9},{9,10},{10,1... | collective-permute-start | bytes 786440 | tf_op jit(solution)/shard_map/ppermute | solution.py:253
  56.9 3.1 %far.5 = bf16[512,256]{1,0:T(8,128)(2,1)S(1)} custom-call(s32[2]{0:T(128)S(1)} %pad_add_fusion.refs_0_, bf16[2048,256]{1,0:T(8,128)(2,1)S(1)} %copy-done.1, f32[512,256]{1,0:T(8,128)S(1)} %get-tuple-element.63.refs_2_, f32[512,256]{1,0:T(8,128)S(1)} %get-tuple-element.64.refs_3_, f32[512,256]{1,0:T(8,128)S(1)} %get-tuple-element.65.refs_4_, ...), custom_call_target="tpu_custom_call" | custom-call | tf_op jit(solution)/shard_map/far/pallas_call | solution.py:29
  60.0 0.0 collective-permute-done.13.refs_4_
  60.0 0.6 collective-permute-start.11
  60.7 0.0 collective-permute-done.16.refs_7_
  60.7 1.1 %collective-permute-start.14 = (bf16[128,1024]{1,0:T(8,128)(2,1)S(1)}, bf16[128,1024]{1,0:T(8,128)(2,1)S(1)}, u32[]{:S(2)}, u32[]{:S(2)}) collective-permute-start(bf16[128,1024]{1,0:T(8,128)(2,1)S(1)} %collective-permute-done.13.refs_4_), channel_id=1, source_target_pairs={{0,4},{4,0},{8,12},{12,8},{16,20},{20,16},{24,28},{28,24},{32,36},... | collective-permute-start | bytes 786440 | tf_op jit(solution)/shard_map/ppermute | solution.py:250
  61.8 0.0 collective-permute-done.19.refs_11_
  61.8 0.1 collective-permute-start.17
  61.9 3.1 %far.4.refs_1_ = bf16[512,256]{1,0:T(8,128)(2,1)S(1)} custom-call(s32[2]{0:T(128)S(1)} %pad_add_fusion.refs_0_, bf16[2048,256]{1,0:T(8,128)(2,1)S(1)} %copy-done.1, f32[512,256]{1,0:T(8,128)S(1)} %get-tuple-element.57.refs_2_, f32[512,256]{1,0:T(8,128)S(1)} %get-tuple-element.58.refs_3_, f32[512,256]{1,0:T(8,128)S(1)} %get-tuple-element.59.refs_4_, ...), custom_call_target="tpu_custom_call" | custom-call | tf_op jit(solution)/shard_map/far/pallas_call | solution.py:29
  65.0 0.0 collective-permute-done.18.refs_9_
  65.0 1.5 %collective-permute-done.15.refs_6_ = bf16[512,256]{1,0:T(8,128)(2,1)S(1)} collective-permute-done((bf16[512,256]{1,0:T(8,128)(2,1)S(1)}, bf16[512,256]{1,0:T(8,128)(2,1)S(1)}, u32[]{:S(2)}, u32[]{:S(2)}) %collective-permute-start.15) | collective-permute-done | bytes 262176 | tf_op jit(solution)/shard_map/ppermute | solution.py:253
  66.5 0.6 collective-permute-done.11.refs_3_
  67.1 0.0 collective-permute-done.14.refs_5_
  67.1 0.0 collective-permute-done.17.refs_8_
  67.1 2.8 %project.1 = bf16[512,1024]{1,0:T(8,128)(2,1)} custom-call(s32[2]{0:T(128)S(1)} %pad_add_fusion.refs_0_, bf16[512,256]{1,0:T(8,128)(2,1)S(1)} %far.4.refs_1_, bf16[256,1024]{1,0:T(8,128)(2,1)S(1)} %copy-done.2, bf16[512,256]{1,0:T(8,128)(2,1)S(1)} %collective-permute-done.11.refs_3_, bf16[128,1024]{1,0:T(8,128)(2,1)S(1)} %collective-permute-done.13.refs_4_, ...), custom_call_target="tpu_custom_call" | custom-call | tf_op jit(solution)/shard_map/project/pallas_call | solution.py:29
Async XLA Ops:
  0.1 1.2 %copy-start = (bf16[2048,256]{1,0:T(8,128)(2,1)S(1)}, bf16[2048,256]{1,0:T(8,128)(2,1)}, u32[]{:S(2)}) copy-start(bf16[2048,256]{1,0:T(8,128)(2,1)} %refs_1_.15) | copy-start | bytes 3145732
  1.3 1.6 %copy-start.3 = (bf16[2,2048,256]{2,1,0:T(8,128)(2,1)S(1)}, bf16[2,2048,256]{2,1,0:T(8,128)(2,1)}, u32[]{:S(2)}) copy-start(bf16[2,2048,256]{2,1,0:T(8,128)(2,1)} %refs_1_.8) | copy-start | bytes 6291460
  2.9 12.2 %copy-start.1 = (bf16[2048,256]{1,0:T(8,128)(2,1)S(1)}, bf16[2048,256]{1,0:T(8,128)(2,1)}, u32[]{:S(2)}) copy-start(bf16[2048,256]{1,0:T(8,128)(2,1)} %refs_1_.15) | copy-start | bytes 3145732
  2.9 15.5 %copy-start.2 = (bf16[256,1024]{1,0:T(8,128)(2,1)S(1)}, bf16[256,1024]{1,0:T(8,128)(2,1)}, u32[]{:S(2)}) copy-start(bf16[256,1024]{1,0:T(8,128)(2,1)} %refs_2_.3) | copy-start | bytes 1572868
  4.4 5.2 %collective-permute-start = (bf16[2,256,256]{2,1,0:T(8,128)(2,1)S(1)}, bf16[2,256,256]{2,1,0:T(8,128)(2,1)S(1)}, u32[]{:S(2)}, u32[]{:S(2)}) collective-permute-start(bf16[2,256,256]{2,1,0:T(8,128)(2,1)S(1)} %get-tuple-element.41.refs_1_), channel_id=1, source_target_pairs={{0,4},{4,0},{8,12},{12,8},{16,20},{20,16},{24,28},{28,24},{32,36},... | collective-permute-start | bytes 786440 | tf_op jit(solution)/shard_map/ppermute | solution.py:250
  7.7 7.3 %collective-permute-start.1 = (bf16[2,128,256]{2,1,0:T(8,128)(2,1)S(1)}, bf16[2,128,256]{2,1,0:T(8,128)(2,1)S(1)}, u32[]{:S(2)}, u32[]{:S(2)}) collective-permute-start(bf16[2,128,256]{2,1,0:T(8,128)(2,1)S(1)} %get-tuple-element.42), channel_id=1, source_target_pairs={{4,8},{12,16},{20,24},{28,32},{36,40},{44,48},{52,56},{60,64},{68,... | collective-permute-start | bytes 393224 | tf_op jit(solution)/shard_map/ppermute | solution.py:265
  10.5 7.9 %collective-permute-start.2 = (bf16[128,256]{1,0:T(8,128)(2,1)S(1)}, bf16[128,256]{1,0:T(8,128)(2,1)S(1)}, u32[]{:S(2)}, u32[]{:S(2)}) collective-permute-start(bf16[128,256]{1,0:T(8,128)(2,1)S(1)} %get-tuple-element.43.refs_5_.refs_1_), channel_id=1, source_target_pairs={{0,8},{4,12},{8,0},{12,4},{16,24},{20,28},{24,16},{28,20},{32,40},... | collective-permute-start | bytes 196616 | tf_op jit(solution)/shard_map/ppermute | solution.py:250
  11.1 7.3 %collective-permute-start.3 = (bf16[64,256]{1,0:T(8,128)(2,1)S(1)}, bf16[64,256]{1,0:T(8,128)(2,1)S(1)}, u32[]{:S(2)}, u32[]{:S(2)}) collective-permute-start(bf16[64,256]{1,0:T(8,128)(2,1)S(1)} %get-tuple-element.44), channel_id=1, source_target_pairs={{0,16},{4,20},{8,24},{12,28},{16,0},{20,4},{24,8},{28,12},{32,48},... | collective-permute-start | bytes 98312 | tf_op jit(solution)/shard_map/ppermute | solution.py:250
  13.9 4.5 %collective-permute-start.4 = (bf16[64,256]{1,0:T(8,128)(2,1)S(1)}, bf16[64,256]{1,0:T(8,128)(2,1)S(1)}, u32[]{:S(2)}, u32[]{:S(2)}) collective-permute-start(bf16[64,256]{1,0:T(8,128)(2,1)S(1)} %get-tuple-element.44), channel_id=1, source_target_pairs={{0,24},{4,28},{8,16},{12,20},{16,8},{20,12},{24,0},{28,4},{32,56},... | collective-permute-start | bytes 98312 | tf_op jit(solution)/shard_map/ppermute | solution.py:250
  19.4 15.9 %collective-permute-start.12 = (bf16[128,1024]{1,0:T(8,128)(2,1)S(1)}, bf16[128,1024]{1,0:T(8,128)(2,1)S(1)}, u32[]{:S(2)}, u32[]{:S(2)}) collective-permute-start(bf16[128,1024]{1,0:T(8,128)(2,1)S(1)} %get-tuple-element.67), channel_id=1, source_target_pairs={{0,2},{1,3},{2,0},{3,1},{4,6},{5,7},{6,4},{7,5},{8,10},{9,11},{10,... | collective-permute-start | bytes 786440 | tf_op jit(solution)/shard_map/ppermute | solution.py:253
  21.8 10.4 %collective-permute-start.5 = (bf16[128,256]{1,0:T(8,128)(2,1)S(1)}, bf16[128,256]{1,0:T(8,128)(2,1)S(1)}, u32[]{:S(2)}, u32[]{:S(2)}) collective-permute-start(bf16[128,256]{1,0:T(8,128)(2,1)S(1)} %get-tuple-element.49.refs_5_.refs_1_), channel_id=1, source_target_pairs={{0,32},{4,36},{8,40},{12,44},{16,48},{20,52},{24,56},{28,60},{32,0... | collective-permute-start | bytes 196616 | tf_op jit(solution)/shard_map/ppermute | solution.py:250
  23.4 7.5 %collective-permute-start.6 = (bf16[64,256]{1,0:T(8,128)(2,1)S(1)}, bf16[64,256]{1,0:T(8,128)(2,1)S(1)}, u32[]{:S(2)}, u32[]{:S(2)}) collective-permute-start(bf16[64,256]{1,0:T(8,128)(2,1)S(1)} %get-tuple-element.50), channel_id=1, source_target_pairs={{0,64},{4,68},{8,72},{12,76},{16,80},{20,84},{24,88},{28,92},{32,9... | collective-permute-start | bytes 98312 | tf_op jit(solution)/shard_map/ppermute | solution.py:250
  27.6 4.6 %collective-permute-start.7 = (bf16[64,256]{1,0:T(8,128)(2,1)S(1)}, bf16[64,256]{1,0:T(8,128)(2,1)S(1)}, u32[]{:S(2)}, u32[]{:S(2)}) collective-permute-start(bf16[64,256]{1,0:T(8,128)(2,1)S(1)} %get-tuple-element.50), channel_id=1, source_target_pairs={{0,96},{4,100},{8,104},{12,108},{16,112},{20,116},{24,120},{28,124... | collective-permute-start | bytes 98312 | tf_op jit(solution)/shard_map/ppermute | solution.py:250
  33.0 14.8 %collective-permute-start.8 = (bf16[4,128,256]{2,1,0:T(8,128)(2,1)S(1)}, bf16[4,128,256]{2,1,0:T(8,128)(2,1)S(1)}, u32[]{:S(2)}, u32[]{:S(2)}) collective-permute-start(bf16[4,128,256]{2,1,0:T(8,128)(2,1)S(1)} %get-tuple-element.60.refs_6_), channel_id=1, source_target_pairs={{0,4},{4,0},{8,12},{12,8},{16,20},{20,16},{24,28},{28,24},{32,36},... | collective-permute-start | bytes 786440 | tf_op jit(solution)/shard_map/ppermute | solution.py:250
  35.3 24.8 %collective-permute-start.13 = (bf16[128,1024]{1,0:T(8,128)(2,1)S(1)}, bf16[128,1024]{1,0:T(8,128)(2,1)S(1)}, u32[]{:S(2)}, u32[]{:S(2)}) collective-permute-start(bf16[128,1024]{1,0:T(8,128)(2,1)S(1)} %get-tuple-element.67), channel_id=1, source_target_pairs={{0,3},{1,0},{2,1},{3,2},{4,7},{5,4},{6,5},{7,6},{8,11},{9,8},{10,9... | collective-permute-start | bytes 786440 | tf_op jit(solution)/shard_map/ppermute | solution.py:253
  36.0 24.6 %collective-permute-start.16 = (bf16[128,1024]{1,0:T(8,128)(2,1)S(1)}, bf16[128,1024]{1,0:T(8,128)(2,1)S(1)}, u32[]{:S(2)}, u32[]{:S(2)}) collective-permute-start(bf16[128,1024]{1,0:T(8,128)(2,1)S(1)} %get-tuple-element.67), channel_id=1, source_target_pairs={{0,1},{1,2},{2,3},{3,0},{4,5},{5,6},{6,7},{7,4},{8,9},{9,10},{10,1... | collective-permute-start | bytes 786440 | tf_op jit(solution)/shard_map/ppermute | solution.py:253
  36.7 25.1 %collective-permute-start.19 = (bf16[128,1024]{1,0:T(8,128)(2,1)S(1)}, bf16[128,1024]{1,0:T(8,128)(2,1)S(1)}, u32[]{:S(2)}, u32[]{:S(2)}) collective-permute-start(bf16[128,1024]{1,0:T(8,128)(2,1)S(1)} %collective-permute-done.12.refs_10_), channel_id=1, source_target_pairs={{0,4},{4,0},{8,12},{12,8},{16,20},{20,16},{24,28},{28,24},{32,36},... | collective-permute-start | bytes 786440 | tf_op jit(solution)/shard_map/ppermute | solution.py:250
  37.6 8.9 %collective-permute-start.9 = (bf16[128,256]{1,0:T(8,128)(2,1)S(1)}, bf16[128,256]{1,0:T(8,128)(2,1)S(1)}, u32[]{:S(2)}, u32[]{:S(2)}) collective-permute-start(bf16[128,256]{1,0:T(8,128)(2,1)S(1)} %get-tuple-element.56.refs_5_), channel_id=1, source_target_pairs={{0,224},{4,228},{8,232},{12,236},{16,240},{20,244},{24,248},{28,25... | collective-permute-start | bytes 196616 | tf_op jit(solution)/shard_map/ppermute | solution.py:250
  46.4 1.3 %collective-permute-start.10 = (bf16[128,256]{1,0:T(8,128)(2,1)S(1)}, bf16[128,256]{1,0:T(8,128)(2,1)S(1)}, u32[]{:S(2)}, u32[]{:S(2)}) collective-permute-start(bf16[128,256]{1,0:T(8,128)(2,1)S(1)} %collective-permute-done.9.refs_8_), channel_id=1, source_target_pairs={{0,4},{4,0},{8,12},{12,8},{16,20},{20,16},{24,28},{28,24},{32,36},... | collective-permute-start | bytes 196616 | tf_op jit(solution)/shard_map/ppermute | solution.py:250
  50.9 14.1 %collective-permute-start.18 = (bf16[512,256]{1,0:T(8,128)(2,1)S(1)}, bf16[512,256]{1,0:T(8,128)(2,1)S(1)}, u32[]{:S(2)}, u32[]{:S(2)}) collective-permute-start(bf16[512,256]{1,0:T(8,128)(2,1)S(1)} %far.7), channel_id=1, source_target_pairs={{0,2},{1,3},{2,0},{3,1},{4,6},{5,7},{6,4},{7,5},{8,10},{9,11},{10,... | collective-permute-start | bytes 786440 | tf_op jit(solution)/shard_map/ppermute | solution.py:253
  54.7 11.8 %collective-permute-start.15 = (bf16[512,256]{1,0:T(8,128)(2,1)S(1)}, bf16[512,256]{1,0:T(8,128)(2,1)S(1)}, u32[]{:S(2)}, u32[]{:S(2)}) collective-permute-start(bf16[512,256]{1,0:T(8,128)(2,1)S(1)} %far.6), channel_id=1, source_target_pairs={{0,1},{1,2},{2,3},{3,0},{4,5},{5,6},{6,7},{7,4},{8,9},{9,10},{10,1... | collective-permute-start | bytes 786440 | tf_op jit(solution)/shard_map/ppermute | solution.py:253
  60.0 7.1 %collective-permute-start.11 = (bf16[512,256]{1,0:T(8,128)(2,1)S(1)}, bf16[512,256]{1,0:T(8,128)(2,1)S(1)}, u32[]{:S(2)}, u32[]{:S(2)}) collective-permute-start(bf16[512,256]{1,0:T(8,128)(2,1)S(1)} %far.5), channel_id=1, source_target_pairs={{0,3},{1,0},{2,1},{3,2},{4,7},{5,4},{6,5},{7,6},{8,11},{9,8},{10,9... | collective-permute-start | bytes 786440 | tf_op jit(solution)/shard_map/ppermute | solution.py:253
  60.7 6.4 %collective-permute-start.14 = (bf16[128,1024]{1,0:T(8,128)(2,1)S(1)}, bf16[128,1024]{1,0:T(8,128)(2,1)S(1)}, u32[]{:S(2)}, u32[]{:S(2)}) collective-permute-start(bf16[128,1024]{1,0:T(8,128)(2,1)S(1)} %collective-permute-done.13.refs_4_), channel_id=1, source_target_pairs={{0,4},{4,0},{8,12},{12,8},{16,20},{20,16},{24,28},{28,24},{32,36},... | collective-permute-start | bytes 786440 | tf_op jit(solution)/shard_map/ppermute | solution.py:250
  61.8 5.3 %collective-permute-start.17 = (bf16[128,1024]{1,0:T(8,128)(2,1)S(1)}, bf16[128,1024]{1,0:T(8,128)(2,1)S(1)}, u32[]{:S(2)}, u32[]{:S(2)}) collective-permute-start(bf16[128,1024]{1,0:T(8,128)(2,1)S(1)} %collective-permute-done.16.refs_7_), channel_id=1, source_target_pairs={{0,4},{4,0},{8,12},{12,8},{16,20},{20,16},{24,28},{28,24},{32,36},... | collective-permute-start | bytes 786440 | tf_op jit(solution)/shard_map/ppermute | solution.py:250

commit v2 on v1

--- a/solution.py
+++ b/solution.py
@@ -290,7 +290,7 @@
     got = exchange(up7, part8, 3)
     near1 = near((1,), up7)
     *got, near1[0] = barrier((*got, near1[0]))
-    w2 = turn(w_half, 2)
+    w2, w1 = turn(w_half, 2), turn(w_half, 1)
     up9, held = call(last_kernel, "last", [panel, ((4, BLK, WIDE), BF16)], (at, up7, *got, p5, p6))
     p9 = swap(up9, 56)
     theirs = swap(held, 1)
@@ -299,7 +299,7 @@
     near2, near3 = near23[:3], near23[3:]
     theirs9 = swap(p9, 1)
     w2, source = barrier((w2, w_half))
-    w_mine = [w2, turn(source, 1), turn(source, 3)]
+    w_mine = [w2, w1, turn(source, 3)]
     w_other = [swap(w, 1) for w in w_mine]
     atts = []
     for by, state in zip(turns, (near0, near1, near2, near3)):

time: 70 us -> 70.8 us (1.011)
  starting transfers between devices: 30.3 us -> 31.4 us
    ppermute x13, starting transfers between devices: 20.9 us -> 22.8 us  [swap(): return lax.ppermute(x, 'ctx', [(i, i ^ bits) for i in range(shards)])]
    ppermute x6, starting transfers between devices: 7.46 us -> 6.74 us  [turn(): lax.ppermute(x, 'head', [(i, (i + by) % heads) for i in range(heads)])]
  transfers between devices with their start and end apart: 20 -> 20, of which waited for: 5 -> 4; matrix products, arithmetic and copies ran while one was open for 0% -> 0% of each run, Pallas kernels for 37% -> 37%
where the time goes in v2:
time: 70.8 us; the launch traced here: 70.7 us
  Pallas kernels  31.5 us (44%)
  starting transfers between devices  31.4 us (44%)
  waiting for transfers between devices  4.69 us (7%)
  local copies, waits for them, and re-layouts  2.82 us (4%)
    pallas_call x12, Pallas kernels, call(): pl.pallas_call(lambda *refs: kernel(*refs[:n], *refs[n + late:]), out_sha...  31.5 us
    ppermute x13, starting transfers between devices, swap(): return lax.ppermute(x, 'ctx', [(i, i ^ bits) for i in range(shards)])  22.8 us
    ppermute x6, starting transfers between devices, turn(): lax.ppermute(x, 'head', [(i, (i + by) % heads) for i in range(heads)])  6.74 us
    unnamed x8, local copies, waits for them, and re-layouts  2.82 us
    ppermute x6, waiting for transfers between devices, turn(): lax.ppermute(x, 'head', [(i, (i + by) % heads) for i in range(heads)])  2.28 us
    ppermute x1, starting transfers between devices, body(): back = lax.ppermute(back, 'ctx', ends + [(b, a) for a, b in ends])  1.91 us
    ppermute x13, waiting for transfers between devices, swap(): return lax.ppermute(x, 'ctx', [(i, i ^ bits) for i in range(shards)])  1.7 us
  transfers between devices with their start and end apart: 20, of which 4 were waited for; matrix products, arithmetic and copies ran while one was open for 0% of the time, Pallas kernels for 37%

profile of v2, /device:TPU:1, one launch (start us, length us, event | category | flops | bytes accessed | tf_op | source)
XLA Modules:
  0.0 70.7 jit_solution(11991817298624101375)
XLA Ops:
  0.0 0.1 pad_add_fusion.refs_0_
  0.1 0.0 copy-start
  0.1 1.2 %copy-done = bf16[2048,256]{1,0:T(8,128)(2,1)S(1)} copy-done((bf16[2048,256]{1,0:T(8,128)(2,1)S(1)}, bf16[2048,256]{1,0:T(8,128)(2,1)}, u32[]{:S(2)}) %copy-start) | copy-done | bytes 1048600
  1.3 0.0 copy-start.3
  1.3 1.6 %copy-done.3 = bf16[2,2048,256]{2,1,0:T(8,128)(2,1)S(1)} copy-done((bf16[2,2048,256]{2,1,0:T(8,128)(2,1)S(1)}, bf16[2,2048,256]{2,1,0:T(8,128)(2,1)}, u32[]{:S(2)}) %copy-start.3) | copy-done | bytes 2097176
  2.9 0.0 copy-start.1
  2.9 0.0 copy-start.2
  2.9 1.5 %pyramid.1 = (bf16[2,3840,256]{2,1,0:T(8,128)(2,1)S(1)}, bf16[2,256,256]{2,1,0:T(8,128)(2,1)S(1)}, bf16[2,128,256]{2,1,0:T(8,128)(2,1)S(1)}) custom-call(s32[2]{0:T(128)S(1)} %pad_add_fusion.refs_0_, bf16[2,2048,256]{2,1,0:T(8,128)(2,1)S(1)} %copy-done.3, bf16[2048,256]{1,0:T(8,128)(2,1)S(1)} %copy-done), custom_call_target="tpu_custom_call" | custom-call | tf_op jit(solution)/shard_map/pyramid/pallas_call | solution.py:29
  4.4 3.3 %collective-permute-start = (bf16[2,256,256]{2,1,0:T(8,128)(2,1)S(1)}, bf16[2,256,256]{2,1,0:T(8,128)(2,1)S(1)}, u32[]{:S(2)}, u32[]{:S(2)}) collective-permute-start(bf16[2,256,256]{2,1,0:T(8,128)(2,1)S(1)} %get-tuple-element.41.refs_1_), channel_id=1, source_target_pairs={{0,4},{4,0},{8,12},{12,8},{16,20},{20,16},{24,28},{28,24},{32,36},... | collective-permute-start | bytes 786440 | tf_op jit(solution)/shard_map/ppermute | solution.py:250
  7.7 1.9 %collective-permute-start.1 = (bf16[2,128,256]{2,1,0:T(8,128)(2,1)S(1)}, bf16[2,128,256]{2,1,0:T(8,128)(2,1)S(1)}, u32[]{:S(2)}, u32[]{:S(2)}) collective-permute-start(bf16[2,128,256]{2,1,0:T(8,128)(2,1)S(1)} %get-tuple-element.42), channel_id=1, source_target_pairs={{4,8},{12,16},{20,24},{28,32},{36,40},{44,48},{52,56},{60,64},{68,... | collective-permute-start | bytes 393224 | tf_op jit(solution)/shard_map/ppermute | solution.py:265
  9.7 0.0 collective-permute-done.refs_2_.refs_3_.refs_5_
  9.7 0.8 %start.1 = (bf16[128,256]{1,0:T(8,128)(2,1)S(1)}, bf16[64,256]{1,0:T(8,128)(2,1)S(1)}) custom-call(s32[2]{0:T(128)S(1)} %pad_add_fusion.refs_0_, bf16[2,256,256]{2,1,0:T(8,128)(2,1)S(1)} %get-tuple-element.41.refs_1_, bf16[2,256,256]{2,1,0:T(8,128)(2,1)S(1)} %collective-permute-done.refs_2_.refs_3_.refs_5_), custom_call_target="tpu_custom_call" | custom-call | tf_op jit(solution)/shard_map/start/pallas_call | solution.py:29
  10.5 0.6 collective-permute-start.2
  11.1 2.8 %collective-permute-start.3 = (bf16[64,256]{1,0:T(8,128)(2,1)S(1)}, bf16[64,256]{1,0:T(8,128)(2,1)S(1)}, u32[]{:S(2)}, u32[]{:S(2)}) collective-permute-start(bf16[64,256]{1,0:T(8,128)(2,1)S(1)} %get-tuple-element.44), channel_id=1, source_target_pairs={{0,16},{4,20},{8,24},{12,28},{16,0},{20,4},{24,8},{28,12},{32,48},... | collective-permute-start | bytes 98312 | tf_op jit(solution)/shard_map/ppermute | solution.py:250
  13.9 0.5 collective-permute-start.4
  14.4 0.7 collective-permute-done.1.refs_4_
  15.1 0.0 copy-done.1
  15.1 3.3 %near.3 = (f32[512,256]{1,0:T(8,128)S(1)}, f32[512,256]{1,0:T(8,128)S(1)}, f32[512,256]{1,0:T(8,128)S(1)}) custom-call(s32[2]{0:T(128)S(1)} %pad_add_fusion.refs_0_, bf16[2048,256]{1,0:T(8,128)(2,1)S(1)} %copy-done.1, bf16[2,3840,256]{2,1,0:T(8,128)(2,1)S(1)} %get-tuple-element.40.refs_2_, ...), custom_call_target="tpu_custom_call" | custom-call | tf_op jit(solution)/shard_map/near/pallas_call | solution.py:29
  18.4 0.0 collective-permute-done.3.refs_3_
  18.4 0.0 collective-permute-done.4.refs_4_
  18.4 0.0 collective-permute-done.2.refs_2_.refs_5_
  18.4 0.0 copy-done.2
  18.4 1.0 %middle.1 = (bf16[128,256]{1,0:T(8,128)(2,1)S(1)}, bf16[128,256]{1,0:T(8,128)(2,1)S(1)}, bf16[64,256]{1,0:T(8,128)(2,1)S(1)}, bf16[128,1024]{1,0:T(8,128)(2,1)S(1)}) custom-call(s32[2]{0:T(128)S(1)} %pad_add_fusion.refs_0_, bf16[128,256]{1,0:T(8,128)(2,1)S(1)} %get-tuple-element.43.refs_5_.refs_1_, ...), custom_call_target="tpu_custom_call" | custom-call | tf_op jit(solution)/shard_map/middle/pallas_call | solution.py:29
  19.4 2.4 %collective-permute-start.12 = (bf16[128,1024]{1,0:T(8,128)(2,1)S(1)}, bf16[128,1024]{1,0:T(8,128)(2,1)S(1)}, u32[]{:S(2)}, u32[]{:S(2)}) collective-permute-start(bf16[128,1024]{1,0:T(8,128)(2,1)S(1)} %get-tuple-element.67), channel_id=1, source_target_pairs={{0,2},{1,3},{2,0},{3,1},{4,6},{5,7},{6,4},{7,5},{8,10},{9,11},{10,... | collective-permute-start | bytes 786440 | tf_op jit(solution)/shard_map/ppermute | solution.py:253
  21.8 1.6 %collective-permute-start.5 = (bf16[128,256]{1,0:T(8,128)(2,1)S(1)}, bf16[128,256]{1,0:T(8,128)(2,1)S(1)}, u32[]{:S(2)}, u32[]{:S(2)}) collective-permute-start(bf16[128,256]{1,0:T(8,128)(2,1)S(1)} %get-tuple-element.49.refs_5_.refs_1_), channel_id=1, source_target_pairs={{0,32},{4,36},{8,40},{12,44},{16,48},{20,52},{24,56},{28,60},{32,0... | collective-permute-start | bytes 196616 | tf_op jit(solution)/shard_map/ppermute | solution.py:250
  23.4 4.2 %collective-permute-start.6 = (bf16[64,256]{1,0:T(8,128)(2,1)S(1)}, bf16[64,256]{1,0:T(8,128)(2,1)S(1)}, u32[]{:S(2)}, u32[]{:S(2)}) collective-permute-start(bf16[64,256]{1,0:T(8,128)(2,1)S(1)} %get-tuple-element.50), channel_id=1, source_target_pairs={{0,64},{4,68},{8,72},{12,76},{16,80},{20,84},{24,88},{28,92},{32,9... | collective-permute-start | bytes 98312 | tf_op jit(solution)/shard_map/ppermute | solution.py:250
  27.6 0.0 collective-permute-start.7
  27.6 0.4 collective-permute-start.16
  28.0 3.3 %near.4 = (f32[512,256]{1,0:T(8,128)S(1)}, f32[512,256]{1,0:T(8,128)S(1)}, f32[512,256]{1,0:T(8,128)S(1)}) custom-call(s32[2]{0:T(128)S(1)} %pad_add_fusion.refs_0_, bf16[2048,256]{1,0:T(8,128)(2,1)S(1)} %copy-done.1, bf16[2,3840,256]{2,1,0:T(8,128)(2,1)S(1)} %get-tuple-element.40.refs_2_, ...), custom_call_target="tpu_custom_call" | custom-call | tf_op jit(solution)/shard_map/near/pallas_call | solution.py:29
  31.3 0.0 collective-permute-done.6.refs_3_
  31.3 0.9 %collective-permute-done.7.refs_4_ = bf16[64,256]{1,0:T(8,128)(2,1)S(1)} collective-permute-done((bf16[64,256]{1,0:T(8,128)(2,1)S(1)}, bf16[64,256]{1,0:T(8,128)(2,1)S(1)}, u32[]{:S(2)}, u32[]{:S(2)}) %collective-permute-start.7) | collective-permute-done | bytes 32800 | tf_op jit(solution)/shard_map/ppermute | solution.py:250
  32.2 0.0 collective-permute-done.5.refs_2_
  32.2 0.9 %last.1 = (bf16[128,256]{1,0:T(8,128)(2,1)S(1)}, bf16[4,128,256]{2,1,0:T(8,128)(2,1)S(1)}) custom-call(s32[2]{0:T(128)S(1)} %pad_add_fusion.refs_0_, bf16[128,256]{1,0:T(8,128)(2,1)S(1)} %get-tuple-element.49.refs_5_.refs_1_, bf16[128,256]{1,0:T(8,128)(2,1)S(1)} %collective-permute-done.5.refs_2_, bf16[64,256]{1,0:T(8,128)(2,1)S(1)} %collective-permute-done.6.refs_3_, ...), custom_call_target="tpu_custom_call" | custom-call | tf_op jit(solution)/shard_map/last/pallas_call | solution.py:29
  33.0 2.4 %collective-permute-start.8 = (bf16[4,128,256]{2,1,0:T(8,128)(2,1)S(1)}, bf16[4,128,256]{2,1,0:T(8,128)(2,1)S(1)}, u32[]{:S(2)}, u32[]{:S(2)}) collective-permute-start(bf16[4,128,256]{2,1,0:T(8,128)(2,1)S(1)} %get-tuple-element.60.refs_6_), channel_id=1, source_target_pairs={{0,4},{4,0},{8,12},{12,8},{16,20},{20,16},{24,28},{28,24},{32,36},... | collective-permute-start | bytes 786440 | tf_op jit(solution)/shard_map/ppermute | solution.py:250
  35.4 0.0 collective-permute-done.12.refs_10_
  35.4 0.8 %collective-permute-start.13 = (bf16[128,1024]{1,0:T(8,128)(2,1)S(1)}, bf16[128,1024]{1,0:T(8,128)(2,1)S(1)}, u32[]{:S(2)}, u32[]{:S(2)}) collective-permute-start(bf16[128,1024]{1,0:T(8,128)(2,1)S(1)} %get-tuple-element.67), channel_id=1, source_target_pairs={{0,3},{1,0},{2,1},{3,2},{4,7},{5,4},{6,5},{7,6},{8,11},{9,8},{10,9... | collective-permute-start | bytes 786440 | tf_op jit(solution)/shard_map/ppermute | solution.py:253
  36.2 0.4 collective-permute-start.19
  36.6 5.4 %collective-permute-start.9 = (bf16[128,256]{1,0:T(8,128)(2,1)S(1)}, bf16[128,256]{1,0:T(8,128)(2,1)S(1)}, u32[]{:S(2)}, u32[]{:S(2)}) collective-permute-start(bf16[128,256]{1,0:T(8,128)(2,1)S(1)} %get-tuple-element.56.refs_5_), channel_id=1, source_target_pairs={{0,224},{4,228},{8,232},{12,236},{16,240},{20,244},{24,248},{28,25... | collective-permute-start | bytes 196616 | tf_op jit(solution)/shard_map/ppermute | solution.py:250
  42.0 5.6 %near.5 = (f32[512,256]{1,0:T(8,128)S(1)}, f32[512,256]{1,0:T(8,128)S(1)}, f32[512,256]{1,0:T(8,128)S(1)}, f32[512,256]{1,0:T(8,128)S(1)}, f32[512,256]{1,0:T(8,128)S(1)}, /*index=5*/f32[512,256]{1,0:T(8,128)S(1)}) custom-call(s32[2]{0:T(128)S(1)} %pad_add_fusion.refs_0_, bf16[2048,256]{1,0:T(8,128)(2,1)S(1)} %copy-done.1, ...), custom_call_target="tpu_custom_call" | custom-call | tf_op jit(solution)/shard_map/near/pallas_call | solution.py:29
  47.6 0.0 collective-permute-done.9.refs_8_
  47.6 0.5 collective-permute-start.10
  48.2 0.0 collective-permute-done.16.refs_7_
  48.2 0.1 collective-permute-start.17
  48.3 0.8 %collective-permute-done.10.refs_9_ = bf16[128,256]{1,0:T(8,128)(2,1)S(1)} collective-permute-done((bf16[128,256]{1,0:T(8,128)(2,1)S(1)}, bf16[128,256]{1,0:T(8,128)(2,1)S(1)}, u32[]{:S(2)}, u32[]{:S(2)}) %collective-permute-start.10) | collective-permute-done | bytes 65568 | tf_op jit(solution)/shard_map/ppermute | solution.py:250
  49.1 0.0 collective-permute-done.8.refs_7_
  49.1 3.1 %far.7 = bf16[512,256]{1,0:T(8,128)(2,1)S(1)} custom-call(s32[2]{0:T(128)S(1)} %pad_add_fusion.refs_0_, bf16[2048,256]{1,0:T(8,128)(2,1)S(1)} %copy-done.1, f32[512,256]{1,0:T(8,128)S(1)} %get-tuple-element.71.refs_2_, f32[512,256]{1,0:T(8,128)S(1)} %get-tuple-element.72.refs_3_, f32[512,256]{1,0:T(8,128)S(1)} %get-tuple-element.73.refs_4_, ...), custom_call_target="tpu_custom_call" | custom-call | tf_op jit(solution)/shard_map/far/pallas_call | solution.py:29
  52.2 0.3 collective-permute-start.18
  52.5 3.1 %far.6 = bf16[512,256]{1,0:T(8,128)(2,1)S(1)} custom-call(s32[2]{0:T(128)S(1)} %pad_add_fusion.refs_0_, bf16[2048,256]{1,0:T(8,128)(2,1)S(1)} %copy-done.1, f32[512,256]{1,0:T(8,128)S(1)} %get-tuple-element.68.refs_2_, f32[512,256]{1,0:T(8,128)S(1)} %get-tuple-element.69.refs_3_, f32[512,256]{1,0:T(8,128)S(1)} %get-tuple-element.70.refs_4_, ...), custom_call_target="tpu_custom_call" | custom-call | tf_op jit(solution)/shard_map/far/pallas_call | solution.py:29
  55.6 0.6 collective-permute-start.15
  56.2 3.1 %far.5 = bf16[512,256]{1,0:T(8,128)(2,1)S(1)} custom-call(s32[2]{0:T(128)S(1)} %pad_add_fusion.refs_0_, bf16[2048,256]{1,0:T(8,128)(2,1)S(1)} %copy-done.1, f32[512,256]{1,0:T(8,128)S(1)} %get-tuple-element.63.refs_2_, f32[512,256]{1,0:T(8,128)S(1)} %get-tuple-element.64.refs_3_, f32[512,256]{1,0:T(8,128)S(1)} %get-tuple-element.65.refs_4_, ...), custom_call_target="tpu_custom_call" | custom-call | tf_op jit(solution)/shard_map/far/pallas_call | solution.py:29
  59.3 0.0 collective-permute-done.13.refs_4_
  59.3 2.2 %collective-permute-start.11 = (bf16[512,256]{1,0:T(8,128)(2,1)S(1)}, bf16[512,256]{1,0:T(8,128)(2,1)S(1)}, u32[]{:S(2)}, u32[]{:S(2)}) collective-permute-start(bf16[512,256]{1,0:T(8,128)(2,1)S(1)} %far.5), channel_id=1, source_target_pairs={{0,3},{1,0},{2,1},{3,2},{4,7},{5,4},{6,5},{7,6},{8,11},{9,8},{10,9... | collective-permute-start | bytes 786440 | tf_op jit(solution)/shard_map/ppermute | solution.py:253
  61.6 0.0 collective-permute-done.19.refs_11_
  61.6 0.9 %collective-permute-start.14 = (bf16[128,1024]{1,0:T(8,128)(2,1)S(1)}, bf16[128,1024]{1,0:T(8,128)(2,1)S(1)}, u32[]{:S(2)}, u32[]{:S(2)}) collective-permute-start(bf16[128,1024]{1,0:T(8,128)(2,1)S(1)} %collective-permute-done.13.refs_4_), channel_id=1, source_target_pairs={{0,4},{4,0},{8,12},{12,8},{16,20},{20,16},{24,28},{28,24},{32,36},... | collective-permute-start | bytes 786440 | tf_op jit(solution)/shard_map/ppermute | solution.py:250
  62.5 3.1 %far.4.refs_1_ = bf16[512,256]{1,0:T(8,128)(2,1)S(1)} custom-call(s32[2]{0:T(128)S(1)} %pad_add_fusion.refs_0_, bf16[2048,256]{1,0:T(8,128)(2,1)S(1)} %copy-done.1, f32[512,256]{1,0:T(8,128)S(1)} %get-tuple-element.57.refs_2_, f32[512,256]{1,0:T(8,128)S(1)} %get-tuple-element.58.refs_3_, f32[512,256]{1,0:T(8,128)S(1)} %get-tuple-element.59.refs_4_, ...), custom_call_target="tpu_custom_call" | custom-call | tf_op jit(solution)/shard_map/far/pallas_call | solution.py:29
  65.6 0.0 collective-permute-done.17.refs_8_
  65.6 0.0 collective-permute-done.18.refs_9_
  65.6 2.3 %collective-permute-done.15.refs_6_ = bf16[512,256]{1,0:T(8,128)(2,1)S(1)} collective-permute-done((bf16[512,256]{1,0:T(8,128)(2,1)S(1)}, bf16[512,256]{1,0:T(8,128)(2,1)S(1)}, u32[]{:S(2)}, u32[]{:S(2)}) %collective-permute-start.15) | collective-permute-done | bytes 262176 | tf_op jit(solution)/shard_map/ppermute | solution.py:253
  67.9 0.0 collective-permute-done.11.refs_3_
  67.9 0.0 collective-permute-done.14.refs_5_
  67.9 2.8 %project.1 = bf16[512,1024]{1,0:T(8,128)(2,1)} custom-call(s32[2]{0:T(128)S(1)} %pad_add_fusion.refs_0_, bf16[512,256]{1,0:T(8,128)(2,1)S(1)} %far.4.refs_1_, bf16[256,1024]{1,0:T(8,128)(2,1)S(1)} %copy-done.2, bf16[512,256]{1,0:T(8,128)(2,1)S(1)} %collective-permute-done.11.refs_3_, bf16[128,1024]{1,0:T(8,128)(2,1)S(1)} %collective-permute-done.13.refs_4_, ...), custom_call_target="tpu_custom_call" | custom-call | tf_op jit(solution)/shard_map/project/pallas_call | solution.py:29
Async XLA Ops:
  0.1 1.2 %copy-start = (bf16[2048,256]{1,0:T(8,128)(2,1)S(1)}, bf16[2048,256]{1,0:T(8,128)(2,1)}, u32[]{:S(2)}) copy-start(bf16[2048,256]{1,0:T(8,128)(2,1)} %refs_1_.15) | copy-start | bytes 3145732
  1.3 1.6 %copy-start.3 = (bf16[2,2048,256]{2,1,0:T(8,128)(2,1)S(1)}, bf16[2,2048,256]{2,1,0:T(8,128)(2,1)}, u32[]{:S(2)}) copy-start(bf16[2,2048,256]{2,1,0:T(8,128)(2,1)} %refs_1_.8) | copy-start | bytes 6291460
  2.9 12.2 %copy-start.1 = (bf16[2048,256]{1,0:T(8,128)(2,1)S(1)}, bf16[2048,256]{1,0:T(8,128)(2,1)}, u32[]{:S(2)}) copy-start(bf16[2048,256]{1,0:T(8,128)(2,1)} %refs_1_.15) | copy-start | bytes 3145732
  2.9 15.5 %copy-start.2 = (bf16[256,1024]{1,0:T(8,128)(2,1)S(1)}, bf16[256,1024]{1,0:T(8,128)(2,1)}, u32[]{:S(2)}) copy-start(bf16[256,1024]{1,0:T(8,128)(2,1)} %refs_2_.3) | copy-start | bytes 1572868
  4.4 5.2 %collective-permute-start = (bf16[2,256,256]{2,1,0:T(8,128)(2,1)S(1)}, bf16[2,256,256]{2,1,0:T(8,128)(2,1)S(1)}, u32[]{:S(2)}, u32[]{:S(2)}) collective-permute-start(bf16[2,256,256]{2,1,0:T(8,128)(2,1)S(1)} %get-tuple-element.41.refs_1_), channel_id=1, source_target_pairs={{0,4},{4,0},{8,12},{12,8},{16,20},{20,16},{24,28},{28,24},{32,36},... | collective-permute-start | bytes 786440 | tf_op jit(solution)/shard_map/ppermute | solution.py:250
  7.7 7.3 %collective-permute-start.1 = (bf16[2,128,256]{2,1,0:T(8,128)(2,1)S(1)}, bf16[2,128,256]{2,1,0:T(8,128)(2,1)S(1)}, u32[]{:S(2)}, u32[]{:S(2)}) collective-permute-start(bf16[2,128,256]{2,1,0:T(8,128)(2,1)S(1)} %get-tuple-element.42), channel_id=1, source_target_pairs={{4,8},{12,16},{20,24},{28,32},{36,40},{44,48},{52,56},{60,64},{68,... | collective-permute-start | bytes 393224 | tf_op jit(solution)/shard_map/ppermute | solution.py:265
  10.5 7.9 %collective-permute-start.2 = (bf16[128,256]{1,0:T(8,128)(2,1)S(1)}, bf16[128,256]{1,0:T(8,128)(2,1)S(1)}, u32[]{:S(2)}, u32[]{:S(2)}) collective-permute-start(bf16[128,256]{1,0:T(8,128)(2,1)S(1)} %get-tuple-element.43.refs_5_.refs_1_), channel_id=1, source_target_pairs={{0,8},{4,12},{8,0},{12,4},{16,24},{20,28},{24,16},{28,20},{32,40},... | collective-permute-start | bytes 196616 | tf_op jit(solution)/shard_map/ppermute | solution.py:250
  11.1 7.3 %collective-permute-start.3 = (bf16[64,256]{1,0:T(8,128)(2,1)S(1)}, bf16[64,256]{1,0:T(8,128)(2,1)S(1)}, u32[]{:S(2)}, u32[]{:S(2)}) collective-permute-start(bf16[64,256]{1,0:T(8,128)(2,1)S(1)} %get-tuple-element.44), channel_id=1, source_target_pairs={{0,16},{4,20},{8,24},{12,28},{16,0},{20,4},{24,8},{28,12},{32,48},... | collective-permute-start | bytes 98312 | tf_op jit(solution)/shard_map/ppermute | solution.py:250
  13.9 4.5 %collective-permute-start.4 = (bf16[64,256]{1,0:T(8,128)(2,1)S(1)}, bf16[64,256]{1,0:T(8,128)(2,1)S(1)}, u32[]{:S(2)}, u32[]{:S(2)}) collective-permute-start(bf16[64,256]{1,0:T(8,128)(2,1)S(1)} %get-tuple-element.44), channel_id=1, source_target_pairs={{0,24},{4,28},{8,16},{12,20},{16,8},{20,12},{24,0},{28,4},{32,56},... | collective-permute-start | bytes 98312 | tf_op jit(solution)/shard_map/ppermute | solution.py:250
  19.4 16.1 %collective-permute-start.12 = (bf16[128,1024]{1,0:T(8,128)(2,1)S(1)}, bf16[128,1024]{1,0:T(8,128)(2,1)S(1)}, u32[]{:S(2)}, u32[]{:S(2)}) collective-permute-start(bf16[128,1024]{1,0:T(8,128)(2,1)S(1)} %get-tuple-element.67), channel_id=1, source_target_pairs={{0,2},{1,3},{2,0},{3,1},{4,6},{5,7},{6,4},{7,5},{8,10},{9,11},{10,... | collective-permute-start | bytes 786440 | tf_op jit(solution)/shard_map/ppermute | solution.py:253
  21.8 10.4 %collective-permute-start.5 = (bf16[128,256]{1,0:T(8,128)(2,1)S(1)}, bf16[128,256]{1,0:T(8,128)(2,1)S(1)}, u32[]{:S(2)}, u32[]{:S(2)}) collective-permute-start(bf16[128,256]{1,0:T(8,128)(2,1)S(1)} %get-tuple-element.49.refs_5_.refs_1_), channel_id=1, source_target_pairs={{0,32},{4,36},{8,40},{12,44},{16,48},{20,52},{24,56},{28,60},{32,0... | collective-permute-start | bytes 196616 | tf_op jit(solution)/shard_map/ppermute | solution.py:250
  23.4 7.9 %collective-permute-start.6 = (bf16[64,256]{1,0:T(8,128)(2,1)S(1)}, bf16[64,256]{1,0:T(8,128)(2,1)S(1)}, u32[]{:S(2)}, u32[]{:S(2)}) collective-permute-start(bf16[64,256]{1,0:T(8,128)(2,1)S(1)} %get-tuple-element.50), channel_id=1, source_target_pairs={{0,64},{4,68},{8,72},{12,76},{16,80},{20,84},{24,88},{28,92},{32,9... | collective-permute-start | bytes 98312 | tf_op jit(solution)/shard_map/ppermute | solution.py:250
  27.6 4.6 %collective-permute-start.7 = (bf16[64,256]{1,0:T(8,128)(2,1)S(1)}, bf16[64,256]{1,0:T(8,128)(2,1)S(1)}, u32[]{:S(2)}, u32[]{:S(2)}) collective-permute-start(bf16[64,256]{1,0:T(8,128)(2,1)S(1)} %get-tuple-element.50), channel_id=1, source_target_pairs={{0,96},{4,100},{8,104},{12,108},{16,112},{20,116},{24,120},{28,124... | collective-permute-start | bytes 98312 | tf_op jit(solution)/shard_map/ppermute | solution.py:250
  27.6 20.6 %collective-permute-start.16 = (bf16[128,1024]{1,0:T(8,128)(2,1)S(1)}, bf16[128,1024]{1,0:T(8,128)(2,1)S(1)}, u32[]{:S(2)}, u32[]{:S(2)}) collective-permute-start(bf16[128,1024]{1,0:T(8,128)(2,1)S(1)} %get-tuple-element.67), channel_id=1, source_target_pairs={{0,1},{1,2},{2,3},{3,0},{4,5},{5,6},{6,7},{7,4},{8,9},{9,10},{10,1... | collective-permute-start | bytes 786440 | tf_op jit(solution)/shard_map/ppermute | solution.py:253
  33.0 16.1 %collective-permute-start.8 = (bf16[4,128,256]{2,1,0:T(8,128)(2,1)S(1)}, bf16[4,128,256]{2,1,0:T(8,128)(2,1)S(1)}, u32[]{:S(2)}, u32[]{:S(2)}) collective-permute-start(bf16[4,128,256]{2,1,0:T(8,128)(2,1)S(1)} %get-tuple-element.60.refs_6_), channel_id=1, source_target_pairs={{0,4},{4,0},{8,12},{12,8},{16,20},{20,16},{24,28},{28,24},{32,36},... | collective-permute-start | bytes 786440 | tf_op jit(solution)/shard_map/ppermute | solution.py:250
  35.4 23.9 %collective-permute-start.13 = (bf16[128,1024]{1,0:T(8,128)(2,1)S(1)}, bf16[128,1024]{1,0:T(8,128)(2,1)S(1)}, u32[]{:S(2)}, u32[]{:S(2)}) collective-permute-start(bf16[128,1024]{1,0:T(8,128)(2,1)S(1)} %get-tuple-element.67), channel_id=1, source_target_pairs={{0,3},{1,0},{2,1},{3,2},{4,7},{5,4},{6,5},{7,6},{8,11},{9,8},{10,9... | collective-permute-start | bytes 786440 | tf_op jit(solution)/shard_map/ppermute | solution.py:253
  36.2 25.3 %collective-permute-start.19 = (bf16[128,1024]{1,0:T(8,128)(2,1)S(1)}, bf16[128,1024]{1,0:T(8,128)(2,1)S(1)}, u32[]{:S(2)}, u32[]{:S(2)}) collective-permute-start(bf16[128,1024]{1,0:T(8,128)(2,1)S(1)} %collective-permute-done.12.refs_10_), channel_id=1, source_target_pairs={{0,4},{4,0},{8,12},{12,8},{16,20},{20,16},{24,28},{28,24},{32,36},... | collective-permute-start | bytes 786440 | tf_op jit(solution)/shard_map/ppermute | solution.py:250
  36.6 11.0 %collective-permute-start.9 = (bf16[128,256]{1,0:T(8,128)(2,1)S(1)}, bf16[128,256]{1,0:T(8,128)(2,1)S(1)}, u32[]{:S(2)}, u32[]{:S(2)}) collective-permute-start(bf16[128,256]{1,0:T(8,128)(2,1)S(1)} %get-tuple-element.56.refs_5_), channel_id=1, source_target_pairs={{0,224},{4,228},{8,232},{12,236},{16,240},{20,244},{24,248},{28,25... | collective-permute-start | bytes 196616 | tf_op jit(solution)/shard_map/ppermute | solution.py:250
  47.6 1.4 %collective-permute-start.10 = (bf16[128,256]{1,0:T(8,128)(2,1)S(1)}, bf16[128,256]{1,0:T(8,128)(2,1)S(1)}, u32[]{:S(2)}, u32[]{:S(2)}) collective-permute-start(bf16[128,256]{1,0:T(8,128)(2,1)S(1)} %collective-permute-done.9.refs_8_), channel_id=1, source_target_pairs={{0,4},{4,0},{8,12},{12,8},{16,20},{20,16},{24,28},{28,24},{32,36},... | collective-permute-start | bytes 196616 | tf_op jit(solution)/shard_map/ppermute | solution.py:250
  48.2 17.4 %collective-permute-start.17 = (bf16[128,1024]{1,0:T(8,128)(2,1)S(1)}, bf16[128,1024]{1,0:T(8,128)(2,1)S(1)}, u32[]{:S(2)}, u32[]{:S(2)}) collective-permute-start(bf16[128,1024]{1,0:T(8,128)(2,1)S(1)} %collective-permute-done.16.refs_7_), channel_id=1, source_target_pairs={{0,4},{4,0},{8,12},{12,8},{16,20},{20,16},{24,28},{28,24},{32,36},... | collective-permute-start | bytes 786440 | tf_op jit(solution)/shard_map/ppermute | solution.py:250
  52.2 13.4 %collective-permute-start.18 = (bf16[512,256]{1,0:T(8,128)(2,1)S(1)}, bf16[512,256]{1,0:T(8,128)(2,1)S(1)}, u32[]{:S(2)}, u32[]{:S(2)}) collective-permute-start(bf16[512,256]{1,0:T(8,128)(2,1)S(1)} %far.7), channel_id=1, source_target_pairs={{0,2},{1,3},{2,0},{3,1},{4,6},{5,7},{6,4},{7,5},{8,10},{9,11},{10,... | collective-permute-start | bytes 786440 | tf_op jit(solution)/shard_map/ppermute | solution.py:253
  55.6 12.3 %collective-permute-start.15 = (bf16[512,256]{1,0:T(8,128)(2,1)S(1)}, bf16[512,256]{1,0:T(8,128)(2,1)S(1)}, u32[]{:S(2)}, u32[]{:S(2)}) collective-permute-start(bf16[512,256]{1,0:T(8,128)(2,1)S(1)} %far.6), channel_id=1, source_target_pairs={{0,1},{1,2},{2,3},{3,0},{4,5},{5,6},{6,7},{7,4},{8,9},{9,10},{10,1... | collective-permute-start | bytes 786440 | tf_op jit(solution)/shard_map/ppermute | solution.py:253
  59.3 8.5 %collective-permute-start.11 = (bf16[512,256]{1,0:T(8,128)(2,1)S(1)}, bf16[512,256]{1,0:T(8,128)(2,1)S(1)}, u32[]{:S(2)}, u32[]{:S(2)}) collective-permute-start(bf16[512,256]{1,0:T(8,128)(2,1)S(1)} %far.5), channel_id=1, source_target_pairs={{0,3},{1,0},{2,1},{3,2},{4,7},{5,4},{6,5},{7,6},{8,11},{9,8},{10,9... | collective-permute-start | bytes 786440 | tf_op jit(solution)/shard_map/ppermute | solution.py:253
  61.6 6.3 %collective-permute-start.14 = (bf16[128,1024]{1,0:T(8,128)(2,1)S(1)}, bf16[128,1024]{1,0:T(8,128)(2,1)S(1)}, u32[]{:S(2)}, u32[]{:S(2)}) collective-permute-start(bf16[128,1024]{1,0:T(8,128)(2,1)S(1)} %collective-permute-done.13.refs_4_), channel_id=1, source_target_pairs={{0,4},{4,0},{8,12},{12,8},{16,20},{20,16},{24,28},{28,24},{32,36},... | collective-permute-start | bytes 786440 | tf_op jit(solution)/shard_map/ppermute | solution.py:250

commit v3 on v1

--- a/solution.py
+++ b/solution.py
@@ -128,7 +128,8 @@
     w_half_ref[...] = w_ref[pl.ds(pl.multiple_of(core * 128, 128), 128)]
 
 
-def last_kernel(at_ref, mine_ref, near_ref, same_ref, cross_ref, p5_ref, p6_ref, up_ref, held_ref):
+def last_kernel(at_ref, mine_ref, near_ref, same_ref, cross_ref, p5_ref, p6_ref, w_ref, up_ref, held_ref, w_out_ref):
+    w_out_ref[...] = w_ref[...]
     held_ref[0], held_ref[1], held_ref[2] = p5_ref[...], p6_ref[...], near_ref[...]
     held_ref[3], up_ref[...] = climb(3, at_ref, mine_ref, near_ref, same_ref, cross_ref)
 
@@ -224,18 +225,21 @@
         out_ref[:, cols] = out.astype(BF16)
 
 
-def times(at_ref, att_ref, mine_ref, other_ref):
+def pack_kernel(at_ref, *refs):
+    for i in range(3):
+        refs[3][i] = refs[i][...]
+
+
+def times(at_ref, att_ref, mine, other):
     first = jnp.bitwise_and(at_ref[1], 1) == 0
-    return jnp.dot(
-        att_ref[...], ordered(first, mine_ref[...], other_ref[...]), preferred_element_type=F32
-    )
-
-
-def project_kernel(at_ref, own_ref, w_own_ref, *refs):
+    return jnp.dot(att_ref[...], ordered(first, mine, other), preferred_element_type=F32)
+
+
+def project_kernel(at_ref, own_ref, w_own_ref, mine_ref, other_ref, *refs):
     total = jnp.dot(own_ref[...], w_own_ref[...], preferred_element_type=F32)
     for i in range(3):
-        total = total + times(at_ref, *refs[3 * i : 3 * i + 3])
-    refs[9][...] = total.astype(BF16)
+        total = total + times(at_ref, refs[i], mine_ref[i], other_ref[i])
+    refs[3][...] = total.astype(BF16)
 
 
 def body(queries, keys_values, out_weight):
@@ -291,16 +295,21 @@
     near1 = near((1,), up7)
     *got, near1[0] = barrier((*got, near1[0]))
     w2 = turn(w_half, 2)
-    up9, held = call(last_kernel, "last", [panel, ((4, BLK, WIDE), BF16)], (at, up7, *got, p5, p6))
+    up9, held, w_late = call(
+        last_kernel,
+        "last",
+        [panel, ((4, BLK, WIDE), BF16), ((128, 1024), BF16)],
+        (at, up7, *got, p5, p6, w_half),
+    )
     p9 = swap(up9, 56)
     theirs = swap(held, 1)
     near23 = near((2, 3), up9)
     p9, near23[0] = barrier((p9, near23[0]))
     near2, near3 = near23[:3], near23[3:]
     theirs9 = swap(p9, 1)
-    w2, source = barrier((w2, w_half))
-    w_mine = [w2, turn(source, 1), turn(source, 3)]
-    w_other = [swap(w, 1) for w in w_mine]
+    w_mine = [w2, turn(w_half, 1), turn(w_late, 3)]
+    (packed,) = call(pack_kernel, "pack", [((3, 128, 1024), BF16)], (at, *w_mine), (near2[0],))
+    packed_other = swap(packed, 1)
     atts = []
     for by, state in zip(turns, (near0, near1, near2, near3)):
         (att,) = call(
@@ -310,12 +319,11 @@
             (at, queries, *state, sibling, held, theirs, p9, theirs9),
         )
         atts.append(turn(att, by) if by else att)
-    pieces = list(zip(atts, w_mine, w_other))
     (out,) = call(
         project_kernel,
         "project",
         [((CHUNK, 1024), BF16)],
-        (at, atts[3], out_weight, *pieces[2], *pieces[1], *pieces[0]),
+        (at, atts[3], out_weight, packed, packed_other, *atts[:3]),
     )
     return out
 

time: 70 us -> 73.6 us (1.051)
  waiting for transfers between devices: 5.08 us -> 7.95 us
    ppermute x6, waiting for transfers between devices: 2.1 us -> 5.35 us  [turn(): lax.ppermute(x, 'head', [(i, (i + by) % heads) for i in range(heads)])]
    pallas_call x12 -> x13, Pallas kernels: 31.5 us -> 32.1 us  [call(): pl.pallas_call(lambda *refs: kernel(*refs[:n], *refs[n + late:]), out_sha...]
    ppermute x13 -> x11, waiting for transfers between devices: 2.27 us -> 1.9 us  [swap(): return lax.ppermute(x, 'ctx', [(i, i ^ bits) for i in range(shards)])]
    ppermute x13 -> x11, starting transfers between devices: 20.9 us -> 20.6 us  [swap(): return lax.ppermute(x, 'ctx', [(i, i ^ bits) for i in range(shards)])]
  transfers between devices with their start and end apart: 20 -> 18, of which waited for: 5 -> 4; matrix products, arithmetic and copies ran while one was open for 0% -> 0% of each run, Pallas kernels for 37% -> 36%
where the time goes in v3:
time: 73.6 us; the launch traced here: 73.4 us
  Pallas kernels  32.1 us (44%)
  starting transfers between devices  30.3 us (41%)
  waiting for transfers between devices  7.95 us (11%)
  local copies, waits for them, and re-layouts  2.82 us (4%)
    pallas_call x13, Pallas kernels, call(): pl.pallas_call(lambda *refs: kernel(*refs[:n], *refs[n + late:]), out_sha...  32.1 us
    ppermute x11, starting transfers between devices, swap(): return lax.ppermute(x, 'ctx', [(i, i ^ bits) for i in range(shards)])  20.6 us
    ppermute x6, starting transfers between devices, turn(): lax.ppermute(x, 'head', [(i, (i + by) % heads) for i in range(heads)])  7.77 us
    ppermute x6, waiting for transfers between devices, turn(): lax.ppermute(x, 'head', [(i, (i + by) % heads) for i in range(heads)])  5.35 us
    unnamed x8, local copies, waits for them, and re-layouts  2.82 us
    ppermute x1, starting transfers between devices, body(): back = lax.ppermute(back, 'ctx', ends + [(b, a) for a, b in ends])  1.91 us
    ppermute x11, waiting for transfers between devices, swap(): return lax.ppermute(x, 'ctx', [(i, i ^ bits) for i in range(shards)])  1.9 us
  transfers between devices with their start and end apart: 18, of which 4 were waited for; matrix products, arithmetic and copies ran while one was open for 0% of the time, Pallas kernels for 36%

profile of v3, /device:TPU:1, one launch (start us, length us, event | category | flops | bytes accessed | tf_op | source)
XLA Modules:
  0.0 73.4 jit_solution(17235590381015253353)
XLA Ops:
  0.0 0.1 pad_add_fusion.refs_0_
  0.1 0.0 copy-start
  0.1 1.2 %copy-done = bf16[2048,256]{1,0:T(8,128)(2,1)S(1)} copy-done((bf16[2048,256]{1,0:T(8,128)(2,1)S(1)}, bf16[2048,256]{1,0:T(8,128)(2,1)}, u32[]{:S(2)}) %copy-start) | copy-done | bytes 1048600
  1.3 0.0 copy-start.3
  1.3 1.6 %copy-done.3 = bf16[2,2048,256]{2,1,0:T(8,128)(2,1)S(1)} copy-done((bf16[2,2048,256]{2,1,0:T(8,128)(2,1)S(1)}, bf16[2,2048,256]{2,1,0:T(8,128)(2,1)}, u32[]{:S(2)}) %copy-start.3) | copy-done | bytes 2097176
  2.9 0.0 copy-start.1
  2.9 0.0 copy-start.2
  2.9 1.5 %pyramid.1 = (bf16[2,3840,256]{2,1,0:T(8,128)(2,1)S(1)}, bf16[2,256,256]{2,1,0:T(8,128)(2,1)S(1)}, bf16[2,128,256]{2,1,0:T(8,128)(2,1)S(1)}) custom-call(s32[2]{0:T(128)S(1)} %pad_add_fusion.refs_0_, bf16[2,2048,256]{2,1,0:T(8,128)(2,1)S(1)} %copy-done.3, bf16[2048,256]{1,0:T(8,128)(2,1)S(1)} %copy-done), custom_call_target="tpu_custom_call" | custom-call | tf_op jit(solution)/shard_map/pyramid/pallas_call | solution.py:29
  4.4 3.3 %collective-permute-start = (bf16[2,256,256]{2,1,0:T(8,128)(2,1)S(1)}, bf16[2,256,256]{2,1,0:T(8,128)(2,1)S(1)}, u32[]{:S(2)}, u32[]{:S(2)}) collective-permute-start(bf16[2,256,256]{2,1,0:T(8,128)(2,1)S(1)} %get-tuple-element.40.refs_1_), channel_id=1, source_target_pairs={{0,4},{4,0},{8,12},{12,8},{16,20},{20,16},{24,28},{28,24},{32,36},... | collective-permute-start | bytes 786440 | tf_op jit(solution)/shard_map/ppermute | solution.py:254
  7.7 1.9 %collective-permute-start.1 = (bf16[2,128,256]{2,1,0:T(8,128)(2,1)S(1)}, bf16[2,128,256]{2,1,0:T(8,128)(2,1)S(1)}, u32[]{:S(2)}, u32[]{:S(2)}) collective-permute-start(bf16[2,128,256]{2,1,0:T(8,128)(2,1)S(1)} %get-tuple-element.41), channel_id=1, source_target_pairs={{4,8},{12,16},{20,24},{28,32},{36,40},{44,48},{52,56},{60,64},{68,... | collective-permute-start | bytes 393224 | tf_op jit(solution)/shard_map/ppermute | solution.py:269
  9.7 0.0 collective-permute-done.refs_2_.refs_3_.refs_5_
  9.7 0.8 %start.1 = (bf16[128,256]{1,0:T(8,128)(2,1)S(1)}, bf16[64,256]{1,0:T(8,128)(2,1)S(1)}) custom-call(s32[2]{0:T(128)S(1)} %pad_add_fusion.refs_0_, bf16[2,256,256]{2,1,0:T(8,128)(2,1)S(1)} %get-tuple-element.40.refs_1_, bf16[2,256,256]{2,1,0:T(8,128)(2,1)S(1)} %collective-permute-done.refs_2_.refs_3_.refs_5_), custom_call_target="tpu_custom_call" | custom-call | tf_op jit(solution)/shard_map/start/pallas_call | solution.py:29
  10.5 0.6 collective-permute-start.2
  11.1 2.8 %collective-permute-start.3 = (bf16[64,256]{1,0:T(8,128)(2,1)S(1)}, bf16[64,256]{1,0:T(8,128)(2,1)S(1)}, u32[]{:S(2)}, u32[]{:S(2)}) collective-permute-start(bf16[64,256]{1,0:T(8,128)(2,1)S(1)} %get-tuple-element.43), channel_id=1, source_target_pairs={{0,16},{4,20},{8,24},{12,28},{16,0},{20,4},{24,8},{28,12},{32,48},... | collective-permute-start | bytes 98312 | tf_op jit(solution)/shard_map/ppermute | solution.py:254
  13.9 0.5 collective-permute-start.4
  14.4 0.7 collective-permute-done.1.refs_4_
  15.1 0.0 copy-done.1
  15.1 3.3 %near.3 = (f32[512,256]{1,0:T(8,128)S(1)}, f32[512,256]{1,0:T(8,128)S(1)}, f32[512,256]{1,0:T(8,128)S(1)}) custom-call(s32[2]{0:T(128)S(1)} %pad_add_fusion.refs_0_, bf16[2048,256]{1,0:T(8,128)(2,1)S(1)} %copy-done.1, bf16[2,3840,256]{2,1,0:T(8,128)(2,1)S(1)} %get-tuple-element.39.refs_2_, ...), custom_call_target="tpu_custom_call" | custom-call | tf_op jit(solution)/shard_map/near/pallas_call | solution.py:29
  18.4 0.0 collective-permute-done.3.refs_3_
  18.4 0.0 collective-permute-done.4.refs_4_
  18.4 0.0 collective-permute-done.2.refs_2_.refs_5_
  18.4 0.0 copy-done.2
  18.4 1.0 %middle.1 = (bf16[128,256]{1,0:T(8,128)(2,1)S(1)}, bf16[128,256]{1,0:T(8,128)(2,1)S(1)}, bf16[64,256]{1,0:T(8,128)(2,1)S(1)}, bf16[128,1024]{1,0:T(8,128)(2,1)S(1)}) custom-call(s32[2]{0:T(128)S(1)} %pad_add_fusion.refs_0_, bf16[128,256]{1,0:T(8,128)(2,1)S(1)} %get-tuple-element.42.refs_5_.refs_1_, ...), custom_call_target="tpu_custom_call" | custom-call | tf_op jit(solution)/shard_map/middle/pallas_call | solution.py:29
  19.4 1.1 %collective-permute-start.5 = (bf16[128,256]{1,0:T(8,128)(2,1)S(1)}, bf16[128,256]{1,0:T(8,128)(2,1)S(1)}, u32[]{:S(2)}, u32[]{:S(2)}) collective-permute-start(bf16[128,256]{1,0:T(8,128)(2,1)S(1)} %get-tuple-element.48.refs_5_.refs_1_), channel_id=1, source_target_pairs={{0,32},{4,36},{8,40},{12,44},{16,48},{20,52},{24,56},{28,60},{32,0... | collective-permute-start | bytes 196616 | tf_op jit(solution)/shard_map/ppermute | solution.py:254
  20.5 4.2 %collective-permute-start.6 = (bf16[64,256]{1,0:T(8,128)(2,1)S(1)}, bf16[64,256]{1,0:T(8,128)(2,1)S(1)}, u32[]{:S(2)}, u32[]{:S(2)}) collective-permute-start(bf16[64,256]{1,0:T(8,128)(2,1)S(1)} %get-tuple-element.49), channel_id=1, source_target_pairs={{0,64},{4,68},{8,72},{12,76},{16,80},{20,84},{24,88},{28,92},{32,9... | collective-permute-start | bytes 98312 | tf_op jit(solution)/shard_map/ppermute | solution.py:254
  24.7 0.0 collective-permute-start.7
  24.7 2.9 %collective-permute-start.11 = (bf16[128,1024]{1,0:T(8,128)(2,1)S(1)}, bf16[128,1024]{1,0:T(8,128)(2,1)S(1)}, u32[]{:S(2)}, u32[]{:S(2)}) collective-permute-start(bf16[128,1024]{1,0:T(8,128)(2,1)S(1)} %get-tuple-element.55.refs_7_), channel_id=1, source_target_pairs={{0,2},{1,3},{2,0},{3,1},{4,6},{5,7},{6,4},{7,5},{8,10},{9,11},{10,... | collective-permute-start | bytes 786440 | tf_op jit(solution)/shard_map/ppermute | solution.py:257
  27.6 0.4 collective-permute-start.12
  28.0 3.3 %near.4 = (f32[512,256]{1,0:T(8,128)S(1)}, f32[512,256]{1,0:T(8,128)S(1)}, f32[512,256]{1,0:T(8,128)S(1)}) custom-call(s32[2]{0:T(128)S(1)} %pad_add_fusion.refs_0_, bf16[2048,256]{1,0:T(8,128)(2,1)S(1)} %copy-done.1, bf16[2,3840,256]{2,1,0:T(8,128)(2,1)S(1)} %get-tuple-element.39.refs_2_, ...), custom_call_target="tpu_custom_call" | custom-call | tf_op jit(solution)/shard_map/near/pallas_call | solution.py:29
  31.3 0.0 collective-permute-done.6.refs_3_
  31.3 0.0 collective-permute-done.7.refs_4_
  31.3 0.0 collective-permute-done.5.refs_2_
  31.3 0.9 %last.1 = (bf16[128,256]{1,0:T(8,128)(2,1)S(1)}, bf16[4,128,256]{2,1,0:T(8,128)(2,1)S(1)}, bf16[128,1024]{1,0:T(8,128)(2,1)S(1)}) custom-call(s32[2]{0:T(128)S(1)} %pad_add_fusion.refs_0_, bf16[128,256]{1,0:T(8,128)(2,1)S(1)} %get-tuple-element.48.refs_5_.refs_1_, bf16[128,256]{1,0:T(8,128)(2,1)S(1)} %collective-permute-done.5.refs_2_, ...), custom_call_target="tpu_custom_call" | custom-call | tf_op jit(solution)/shard_map/last/pallas_call | solution.py:29
  32.2 2.5 %collective-permute-start.13 = (bf16[128,1024]{1,0:T(8,128)(2,1)S(1)}, bf16[128,1024]{1,0:T(8,128)(2,1)S(1)}, u32[]{:S(2)}, u32[]{:S(2)}) collective-permute-start(bf16[128,1024]{1,0:T(8,128)(2,1)S(1)} %get-tuple-element.63), channel_id=1, source_target_pairs={{0,3},{1,0},{2,1},{3,2},{4,7},{5,4},{6,5},{7,6},{8,11},{9,8},{10,9... | collective-permute-start | bytes 786440 | tf_op jit(solution)/shard_map/ppermute | solution.py:257
  34.7 2.5 %collective-permute-start.9 = (bf16[128,256]{1,0:T(8,128)(2,1)S(1)}, bf16[128,256]{1,0:T(8,128)(2,1)S(1)}, u32[]{:S(2)}, u32[]{:S(2)}) collective-permute-start(bf16[128,256]{1,0:T(8,128)(2,1)S(1)} %get-tuple-element.56.refs_5_), channel_id=1, source_target_pairs={{0,224},{4,228},{8,232},{12,236},{16,240},{20,244},{24,248},{28,25... | collective-permute-start | bytes 196616 | tf_op jit(solution)/shard_map/ppermute | solution.py:254
  37.2 5.6 %near.5 = (f32[512,256]{1,0:T(8,128)S(1)}, f32[512,256]{1,0:T(8,128)S(1)}, f32[512,256]{1,0:T(8,128)S(1)}, f32[512,256]{1,0:T(8,128)S(1)}, f32[512,256]{1,0:T(8,128)S(1)}, /*index=5*/f32[512,256]{1,0:T(8,128)S(1)}) custom-call(s32[2]{0:T(128)S(1)} %pad_add_fusion.refs_0_, bf16[2048,256]{1,0:T(8,128)(2,1)S(1)} %copy-done.1, ...), custom_call_target="tpu_custom_call" | custom-call | tf_op jit(solution)/shard_map/near/pallas_call | solution.py:29
  42.8 0.0 collective-permute-done.9.refs_8_
  42.8 0.0 collective-permute-done.11.refs_1_
  42.8 0.0 collective-permute-done.12.refs_2_
  42.9 0.0 collective-permute-done.13.refs_3_
  42.9 0.6 pack.1.refs_3_
  43.5 5.1 %collective-permute-start.14 = (bf16[3,128,1024]{2,1,0:T(8,128)(2,1)S(1)}, bf16[3,128,1024]{2,1,0:T(8,128)(2,1)S(1)}, u32[]{:S(2)}, u32[]{:S(2)}) collective-permute-start(bf16[3,128,1024]{2,1,0:T(8,128)(2,1)S(1)} %pack.1.refs_3_), channel_id=1, source_target_pairs={{0,4},{4,0},{8,12},{12,8},{16,20},{20,16},{24,28},{28,24},{32,36},... | collective-permute-start | bytes 2359304 | tf_op jit(solution)/shard_map/ppermute | solution.py:254
  48.6 0.1 collective-permute-start.8
  48.7 0.4 collective-permute-start.10
  49.1 1.9 %collective-permute-done.10.refs_9_ = bf16[128,256]{1,0:T(8,128)(2,1)S(1)} collective-permute-done((bf16[128,256]{1,0:T(8,128)(2,1)S(1)}, bf16[128,256]{1,0:T(8,128)(2,1)S(1)}, u32[]{:S(2)}, u32[]{:S(2)}) %collective-permute-start.10) | collective-permute-done | bytes 65568 | tf_op jit(solution)/shard_map/ppermute | solution.py:254
  50.9 0.0 collective-permute-done.8.refs_7_
  50.9 3.1 %far.7 = bf16[512,256]{1,0:T(8,128)(2,1)S(1)} custom-call(s32[2]{0:T(128)S(1)} %pad_add_fusion.refs_0_, bf16[2048,256]{1,0:T(8,128)(2,1)S(1)} %copy-done.1, f32[512,256]{1,0:T(8,128)S(1)} %get-tuple-element.64.refs_4_.refs_2_, f32[512,256]{1,0:T(8,128)S(1)} %get-tuple-element.71.refs_3_, f32[512,256]{1,0:T(8,128)S(1)} %get-tuple-element.72.refs_4_, ...), custom_call_target="tpu_custom_call" | custom-call | tf_op jit(solution)/shard_map/far/pallas_call | solution.py:29
  54.0 0.3 collective-permute-start.17
  54.4 3.1 %far.6 = bf16[512,256]{1,0:T(8,128)(2,1)S(1)} custom-call(s32[2]{0:T(128)S(1)} %pad_add_fusion.refs_0_, bf16[2048,256]{1,0:T(8,128)(2,1)S(1)} %copy-done.1, f32[512,256]{1,0:T(8,128)S(1)} %get-tuple-element.68.refs_2_, f32[512,256]{1,0:T(8,128)S(1)} %get-tuple-element.69.refs_3_, f32[512,256]{1,0:T(8,128)S(1)} %get-tuple-element.70.refs_4_, ...), custom_call_target="tpu_custom_call" | custom-call | tf_op jit(solution)/shard_map/far/pallas_call | solution.py:29
  57.5 1.5 %collective-permute-start.16 = (bf16[512,256]{1,0:T(8,128)(2,1)S(1)}, bf16[512,256]{1,0:T(8,128)(2,1)S(1)}, u32[]{:S(2)}, u32[]{:S(2)}) collective-permute-start(bf16[512,256]{1,0:T(8,128)(2,1)S(1)} %far.6), channel_id=1, source_target_pairs={{0,1},{1,2},{2,3},{3,0},{4,5},{5,6},{6,7},{7,4},{8,9},{9,10},{10,1... | collective-permute-start | bytes 786440 | tf_op jit(solution)/shard_map/ppermute | solution.py:257
  59.0 3.1 %far.5 = bf16[512,256]{1,0:T(8,128)(2,1)S(1)} custom-call(s32[2]{0:T(128)S(1)} %pad_add_fusion.refs_0_, bf16[2048,256]{1,0:T(8,128)(2,1)S(1)} %copy-done.1, f32[512,256]{1,0:T(8,128)S(1)} %get-tuple-element.65.refs_2_, f32[512,256]{1,0:T(8,128)S(1)} %get-tuple-element.66.refs_3_, f32[512,256]{1,0:T(8,128)S(1)} %get-tuple-element.67.refs_4_, ...), custom_call_target="tpu_custom_call" | custom-call | tf_op jit(solution)/shard_map/far/pallas_call | solution.py:29
  62.1 0.1 collective-permute-start.15
  62.2 3.1 %far.4.refs_1_ = bf16[512,256]{1,0:T(8,128)(2,1)S(1)} custom-call(s32[2]{0:T(128)S(1)} %pad_add_fusion.refs_0_, bf16[2048,256]{1,0:T(8,128)(2,1)S(1)} %copy-done.1, f32[512,256]{1,0:T(8,128)S(1)} %get-tuple-element.57.refs_2_, f32[512,256]{1,0:T(8,128)S(1)} %get-tuple-element.58.refs_3_, f32[512,256]{1,0:T(8,128)S(1)} %get-tuple-element.59.refs_4_, ...), custom_call_target="tpu_custom_call" | custom-call | tf_op jit(solution)/shard_map/far/pallas_call | solution.py:29
  65.3 0.0 collective-permute-done.17.refs_7_
  65.3 0.9 %collective-permute-done.16.refs_6_ = bf16[512,256]{1,0:T(8,128)(2,1)S(1)} collective-permute-done((bf16[512,256]{1,0:T(8,128)(2,1)S(1)}, bf16[512,256]{1,0:T(8,128)(2,1)S(1)}, u32[]{:S(2)}, u32[]{:S(2)}) %collective-permute-start.16) | collective-permute-done | bytes 262176 | tf_op jit(solution)/shard_map/ppermute | solution.py:257
  66.2 4.5 %collective-permute-done.15.refs_5_ = bf16[512,256]{1,0:T(8,128)(2,1)S(1)} collective-permute-done((bf16[512,256]{1,0:T(8,128)(2,1)S(1)}, bf16[512,256]{1,0:T(8,128)(2,1)S(1)}, u32[]{:S(2)}, u32[]{:S(2)}) %collective-permute-start.15) | collective-permute-done | bytes 262176 | tf_op jit(solution)/shard_map/ppermute | solution.py:257
  70.6 0.0 collective-permute-done.14.refs_4_
  70.6 2.8 %project.1 = bf16[512,1024]{1,0:T(8,128)(2,1)} custom-call(s32[2]{0:T(128)S(1)} %pad_add_fusion.refs_0_, bf16[512,256]{1,0:T(8,128)(2,1)S(1)} %far.4.refs_1_, bf16[256,1024]{1,0:T(8,128)(2,1)S(1)} %copy-done.2, bf16[3,128,1024]{2,1,0:T(8,128)(2,1)S(1)} %pack.1.refs_3_, bf16[3,128,1024]{2,1,0:T(8,128)(2,1)S(1)} %collective-permute-done.14.refs_4_, ...), custom_call_target="tpu_custom_call" | custom-call | tf_op jit(solution)/shard_map/project/pallas_call | solution.py:29
Async XLA Ops:
  0.1 1.2 %copy-start = (bf16[2048,256]{1,0:T(8,128)(2,1)S(1)}, bf16[2048,256]{1,0:T(8,128)(2,1)}, u32[]{:S(2)}) copy-start(bf16[2048,256]{1,0:T(8,128)(2,1)} %refs_1_.15) | copy-start | bytes 3145732
  1.3 1.6 %copy-start.3 = (bf16[2,2048,256]{2,1,0:T(8,128)(2,1)S(1)}, bf16[2,2048,256]{2,1,0:T(8,128)(2,1)}, u32[]{:S(2)}) copy-start(bf16[2,2048,256]{2,1,0:T(8,128)(2,1)} %refs_1_.8) | copy-start | bytes 6291460
  2.9 12.2 %copy-start.1 = (bf16[2048,256]{1,0:T(8,128)(2,1)S(1)}, bf16[2048,256]{1,0:T(8,128)(2,1)}, u32[]{:S(2)}) copy-start(bf16[2048,256]{1,0:T(8,128)(2,1)} %refs_1_.15) | copy-start | bytes 3145732
  2.9 15.5 %copy-start.2 = (bf16[256,1024]{1,0:T(8,128)(2,1)S(1)}, bf16[256,1024]{1,0:T(8,128)(2,1)}, u32[]{:S(2)}) copy-start(bf16[256,1024]{1,0:T(8,128)(2,1)} %refs_2_.3) | copy-start | bytes 1572868
  4.4 5.2 %collective-permute-start = (bf16[2,256,256]{2,1,0:T(8,128)(2,1)S(1)}, bf16[2,256,256]{2,1,0:T(8,128)(2,1)S(1)}, u32[]{:S(2)}, u32[]{:S(2)}) collective-permute-start(bf16[2,256,256]{2,1,0:T(8,128)(2,1)S(1)} %get-tuple-element.40.refs_1_), channel_id=1, source_target_pairs={{0,4},{4,0},{8,12},{12,8},{16,20},{20,16},{24,28},{28,24},{32,36},... | collective-permute-start | bytes 786440 | tf_op jit(solution)/shard_map/ppermute | solution.py:254
  7.7 7.3 %collective-permute-start.1 = (bf16[2,128,256]{2,1,0:T(8,128)(2,1)S(1)}, bf16[2,128,256]{2,1,0:T(8,128)(2,1)S(1)}, u32[]{:S(2)}, u32[]{:S(2)}) collective-permute-start(bf16[2,128,256]{2,1,0:T(8,128)(2,1)S(1)} %get-tuple-element.41), channel_id=1, source_target_pairs={{4,8},{12,16},{20,24},{28,32},{36,40},{44,48},{52,56},{60,64},{68,... | collective-permute-start | bytes 393224 | tf_op jit(solution)/shard_map/ppermute | solution.py:269
  10.5 7.9 %collective-permute-start.2 = (bf16[128,256]{1,0:T(8,128)(2,1)S(1)}, bf16[128,256]{1,0:T(8,128)(2,1)S(1)}, u32[]{:S(2)}, u32[]{:S(2)}) collective-permute-start(bf16[128,256]{1,0:T(8,128)(2,1)S(1)} %get-tuple-element.42.refs_5_.refs_1_), channel_id=1, source_target_pairs={{0,8},{4,12},{8,0},{12,4},{16,24},{20,28},{24,16},{28,20},{32,40},... | collective-permute-start | bytes 196616 | tf_op jit(solution)/shard_map/ppermute | solution.py:254
  11.1 7.3 %collective-permute-start.3 = (bf16[64,256]{1,0:T(8,128)(2,1)S(1)}, bf16[64,256]{1,0:T(8,128)(2,1)S(1)}, u32[]{:S(2)}, u32[]{:S(2)}) collective-permute-start(bf16[64,256]{1,0:T(8,128)(2,1)S(1)} %get-tuple-element.43), channel_id=1, source_target_pairs={{0,16},{4,20},{8,24},{12,28},{16,0},{20,4},{24,8},{28,12},{32,48},... | collective-permute-start | bytes 98312 | tf_op jit(solution)/shard_map/ppermute | solution.py:254
  13.9 4.5 %collective-permute-start.4 = (bf16[64,256]{1,0:T(8,128)(2,1)S(1)}, bf16[64,256]{1,0:T(8,128)(2,1)S(1)}, u32[]{:S(2)}, u32[]{:S(2)}) collective-permute-start(bf16[64,256]{1,0:T(8,128)(2,1)S(1)} %get-tuple-element.43), channel_id=1, source_target_pairs={{0,24},{4,28},{8,16},{12,20},{16,8},{20,12},{24,0},{28,4},{32,56},... | collective-permute-start | bytes 98312 | tf_op jit(solution)/shard_map/ppermute | solution.py:254
  19.4 11.9 %collective-permute-start.5 = (bf16[128,256]{1,0:T(8,128)(2,1)S(1)}, bf16[128,256]{1,0:T(8,128)(2,1)S(1)}, u32[]{:S(2)}, u32[]{:S(2)}) collective-permute-start(bf16[128,256]{1,0:T(8,128)(2,1)S(1)} %get-tuple-element.48.refs_5_.refs_1_), channel_id=1, source_target_pairs={{0,32},{4,36},{8,40},{12,44},{16,48},{20,52},{24,56},{28,60},{32,0... | collective-permute-start | bytes 196616 | tf_op jit(solution)/shard_map/ppermute | solution.py:254
  20.5 10.8 %collective-permute-start.6 = (bf16[64,256]{1,0:T(8,128)(2,1)S(1)}, bf16[64,256]{1,0:T(8,128)(2,1)S(1)}, u32[]{:S(2)}, u32[]{:S(2)}) collective-permute-start(bf16[64,256]{1,0:T(8,128)(2,1)S(1)} %get-tuple-element.49), channel_id=1, source_target_pairs={{0,64},{4,68},{8,72},{12,76},{16,80},{20,84},{24,88},{28,92},{32,9... | collective-permute-start | bytes 98312 | tf_op jit(solution)/shard_map/ppermute | solution.py:254
  24.7 6.6 %collective-permute-start.7 = (bf16[64,256]{1,0:T(8,128)(2,1)S(1)}, bf16[64,256]{1,0:T(8,128)(2,1)S(1)}, u32[]{:S(2)}, u32[]{:S(2)}) collective-permute-start(bf16[64,256]{1,0:T(8,128)(2,1)S(1)} %get-tuple-element.49), channel_id=1, source_target_pairs={{0,96},{4,100},{8,104},{12,108},{16,112},{20,116},{24,120},{28,124... | collective-permute-start | bytes 98312 | tf_op jit(solution)/shard_map/ppermute | solution.py:254
  24.7 18.2 %collective-permute-start.11 = (bf16[128,1024]{1,0:T(8,128)(2,1)S(1)}, bf16[128,1024]{1,0:T(8,128)(2,1)S(1)}, u32[]{:S(2)}, u32[]{:S(2)}) collective-permute-start(bf16[128,1024]{1,0:T(8,128)(2,1)S(1)} %get-tuple-element.55.refs_7_), channel_id=1, source_target_pairs={{0,2},{1,3},{2,0},{3,1},{4,6},{5,7},{6,4},{7,5},{8,10},{9,11},{10,... | collective-permute-start | bytes 786440 | tf_op jit(solution)/shard_map/ppermute | solution.py:257
  27.6 15.2 %collective-permute-start.12 = (bf16[128,1024]{1,0:T(8,128)(2,1)S(1)}, bf16[128,1024]{1,0:T(8,128)(2,1)S(1)}, u32[]{:S(2)}, u32[]{:S(2)}) collective-permute-start(bf16[128,1024]{1,0:T(8,128)(2,1)S(1)} %get-tuple-element.55.refs_7_), channel_id=1, source_target_pairs={{0,1},{1,2},{2,3},{3,0},{4,5},{5,6},{6,7},{7,4},{8,9},{9,10},{10,1... | collective-permute-start | bytes 786440 | tf_op jit(solution)/shard_map/ppermute | solution.py:257
  32.2 10.7 %collective-permute-start.13 = (bf16[128,1024]{1,0:T(8,128)(2,1)S(1)}, bf16[128,1024]{1,0:T(8,128)(2,1)S(1)}, u32[]{:S(2)}, u32[]{:S(2)}) collective-permute-start(bf16[128,1024]{1,0:T(8,128)(2,1)S(1)} %get-tuple-element.63), channel_id=1, source_target_pairs={{0,3},{1,0},{2,1},{3,2},{4,7},{5,4},{6,5},{7,6},{8,11},{9,8},{10,9... | collective-permute-start | bytes 786440 | tf_op jit(solution)/shard_map/ppermute | solution.py:257
  34.7 8.1 %collective-permute-start.9 = (bf16[128,256]{1,0:T(8,128)(2,1)S(1)}, bf16[128,256]{1,0:T(8,128)(2,1)S(1)}, u32[]{:S(2)}, u32[]{:S(2)}) collective-permute-start(bf16[128,256]{1,0:T(8,128)(2,1)S(1)} %get-tuple-element.56.refs_5_), channel_id=1, source_target_pairs={{0,224},{4,228},{8,232},{12,236},{16,240},{20,244},{24,248},{28,25... | collective-permute-start | bytes 196616 | tf_op jit(solution)/shard_map/ppermute | solution.py:254
  43.5 27.2 %collective-permute-start.14 = (bf16[3,128,1024]{2,1,0:T(8,128)(2,1)S(1)}, bf16[3,128,1024]{2,1,0:T(8,128)(2,1)S(1)}, u32[]{:S(2)}, u32[]{:S(2)}) collective-permute-start(bf16[3,128,1024]{2,1,0:T(8,128)(2,1)S(1)} %pack.1.refs_3_), channel_id=1, source_target_pairs={{0,4},{4,0},{8,12},{12,8},{16,20},{20,16},{24,28},{28,24},{32,36},... | collective-permute-start | bytes 2359304 | tf_op jit(solution)/shard_map/ppermute | solution.py:254
  48.6 2.4 %collective-permute-start.8 = (bf16[4,128,256]{2,1,0:T(8,128)(2,1)S(1)}, bf16[4,128,256]{2,1,0:T(8,128)(2,1)S(1)}, u32[]{:S(2)}, u32[]{:S(2)}) collective-permute-start(bf16[4,128,256]{2,1,0:T(8,128)(2,1)S(1)} %get-tuple-element.60.refs_6_), channel_id=1, source_target_pairs={{0,4},{4,0},{8,12},{12,8},{16,20},{20,16},{24,28},{28,24},{32,36},... | collective-permute-start | bytes 786440 | tf_op jit(solution)/shard_map/ppermute | solution.py:254
  48.7 2.3 %collective-permute-start.10 = (bf16[128,256]{1,0:T(8,128)(2,1)S(1)}, bf16[128,256]{1,0:T(8,128)(2,1)S(1)}, u32[]{:S(2)}, u32[]{:S(2)}) collective-permute-start(bf16[128,256]{1,0:T(8,128)(2,1)S(1)} %collective-permute-done.9.refs_8_), channel_id=1, source_target_pairs={{0,4},{4,0},{8,12},{12,8},{16,20},{20,16},{24,28},{28,24},{32,36},... | collective-permute-start | bytes 196616 | tf_op jit(solution)/shard_map/ppermute | solution.py:254
  54.0 11.3 %collective-permute-start.17 = (bf16[512,256]{1,0:T(8,128)(2,1)S(1)}, bf16[512,256]{1,0:T(8,128)(2,1)S(1)}, u32[]{:S(2)}, u32[]{:S(2)}) collective-permute-start(bf16[512,256]{1,0:T(8,128)(2,1)S(1)} %far.7), channel_id=1, source_target_pairs={{0,3},{1,0},{2,1},{3,2},{4,7},{5,4},{6,5},{7,6},{8,11},{9,8},{10,9... | collective-permute-start | bytes 786440 | tf_op jit(solution)/shard_map/ppermute | solution.py:257
  57.5 8.7 %collective-permute-start.16 = (bf16[512,256]{1,0:T(8,128)(2,1)S(1)}, bf16[512,256]{1,0:T(8,128)(2,1)S(1)}, u32[]{:S(2)}, u32[]{:S(2)}) collective-permute-start(bf16[512,256]{1,0:T(8,128)(2,1)S(1)} %far.6), channel_id=1, source_target_pairs={{0,1},{1,2},{2,3},{3,0},{4,5},{5,6},{6,7},{7,4},{8,9},{9,10},{10,1... | collective-permute-start | bytes 786440 | tf_op jit(solution)/shard_map/ppermute | solution.py:257
  62.1 8.6 %collective-permute-start.15 = (bf16[512,256]{1,0:T(8,128)(2,1)S(1)}, bf16[512,256]{1,0:T(8,128)(2,1)S(1)}, u32[]{:S(2)}, u32[]{:S(2)}) collective-permute-start(bf16[512,256]{1,0:T(8,128)(2,1)S(1)} %far.5), channel_id=1, source_target_pairs={{0,2},{1,3},{2,0},{3,1},{4,6},{5,7},{6,4},{7,5},{8,10},{9,11},{10,... | collective-permute-start | bytes 786440 | tf_op jit(solution)/shard_map/ppermute | solution.py:257

commit v4 on v3

--- a/solution.py
+++ b/solution.py
@@ -263,7 +263,7 @@
         [((2, 3840, WIDE), BF16), ((2, 2 * BLK, WIDE), BF16), ((2, BLK, WIDE), BF16)],
         (at, keys_values, queries),
     )
-    turns = (2, 1, 3, 0)
+    turns = (3, 1, 2, 0)
     sibling = swap(face, 1)
     ends = [(i, i + 1) for i in range(1, shards - 1, 2)]
     back = lax.ppermute(back, "ctx", ends + [(b, a) for a, b in ends])
@@ -307,7 +307,7 @@
     p9, near23[0] = barrier((p9, near23[0]))
     near2, near3 = near23[:3], near23[3:]
     theirs9 = swap(p9, 1)
-    w_mine = [w2, turn(w_half, 1), turn(w_late, 3)]
+    w_mine = [turn(w_late, 3), turn(w_half, 1), w2]
     (packed,) = call(pack_kernel, "pack", [((3, 128, 1024), BF16)], (at, *w_mine), (near2[0],))
     packed_other = swap(packed, 1)
     atts = []

time: 73.6 us -> 72 us (0.978)
  waiting for transfers between devices: 7.95 us -> 5.69 us
    ppermute x6, waiting for transfers between devices: 5.35 us -> 3.08 us  [turn(): lax.ppermute(x, 'head', [(i, (i + by) % heads) for i in range(heads)])]
    ppermute x6, starting transfers between devices: 7.77 us -> 8.51 us  [turn(): lax.ppermute(x, 'head', [(i, (i + by) % heads) for i in range(heads)])]
  transfers between devices with their start and end apart: 18 -> 18, of which waited for: 4 -> 3; matrix products, arithmetic and copies ran while one was open for 0% -> 0% of each run, Pallas kernels for 36% -> 36%
where the time goes in v4:
time: 72 us; the launch traced here: 71.9 us
  Pallas kernels  32.1 us (45%)
  starting transfers between devices  31 us (43%)
  waiting for transfers between devices  5.69 us (8%)
  local copies, waits for them, and re-layouts  2.82 us (4%)
    pallas_call x13, Pallas kernels, call(): pl.pallas_call(lambda *refs: kernel(*refs[:n], *refs[n + late:]), out_sha...  32.1 us
    ppermute x11, starting transfers between devices, swap(): return lax.ppermute(x, 'ctx', [(i, i ^ bits) for i in range(shards)])  20.6 us
    ppermute x6, starting transfers between devices, turn(): lax.ppermute(x, 'head', [(i, (i + by) % heads) for i in range(heads)])  8.51 us
    ppermute x6, waiting for transfers between devices, turn(): lax.ppermute(x, 'head', [(i, (i + by) % heads) for i in range(heads)])  3.08 us
    unnamed x8, local copies, waits for them, and re-layouts  2.82 us
    ppermute x1, starting transfers between devices, body(): back = lax.ppermute(back, 'ctx', ends + [(b, a) for a, b in ends])  1.91 us
    ppermute x11, waiting for transfers between devices, swap(): return lax.ppermute(x, 'ctx', [(i, i ^ bits) for i in range(shards)])  1.9 us
  transfers between devices with their start and end apart: 18, of which 3 were waited for; matrix products, arithmetic and copies ran while one was open for 0% of the time, Pallas kernels for 36%

profile of v4, /device:TPU:1, one launch (start us, length us, event | category | flops | bytes accessed | tf_op | source)
XLA Modules:
  0.0 71.9 jit_solution(9717752095268650974)
XLA Ops:
  0.0 0.1 pad_add_fusion.refs_0_
  0.1 0.0 copy-start
  0.1 1.2 %copy-done = bf16[2048,256]{1,0:T(8,128)(2,1)S(1)} copy-done((bf16[2048,256]{1,0:T(8,128)(2,1)S(1)}, bf16[2048,256]{1,0:T(8,128)(2,1)}, u32[]{:S(2)}) %copy-start) | copy-done | bytes 1048600
  1.3 0.0 copy-start.3
  1.3 1.6 %copy-done.3 = bf16[2,2048,256]{2,1,0:T(8,128)(2,1)S(1)} copy-done((bf16[2,2048,256]{2,1,0:T(8,128)(2,1)S(1)}, bf16[2,2048,256]{2,1,0:T(8,128)(2,1)}, u32[]{:S(2)}) %copy-start.3) | copy-done | bytes 2097176
  2.9 0.0 copy-start.1
  2.9 0.0 copy-start.2
  2.9 1.5 %pyramid.1 = (bf16[2,3840,256]{2,1,0:T(8,128)(2,1)S(1)}, bf16[2,256,256]{2,1,0:T(8,128)(2,1)S(1)}, bf16[2,128,256]{2,1,0:T(8,128)(2,1)S(1)}) custom-call(s32[2]{0:T(128)S(1)} %pad_add_fusion.refs_0_, bf16[2,2048,256]{2,1,0:T(8,128)(2,1)S(1)} %copy-done.3, bf16[2048,256]{1,0:T(8,128)(2,1)S(1)} %copy-done), custom_call_target="tpu_custom_call" | custom-call | tf_op jit(solution)/shard_map/pyramid/pallas_call | solution.py:29
  4.4 3.3 %collective-permute-start = (bf16[2,256,256]{2,1,0:T(8,128)(2,1)S(1)}, bf16[2,256,256]{2,1,0:T(8,128)(2,1)S(1)}, u32[]{:S(2)}, u32[]{:S(2)}) collective-permute-start(bf16[2,256,256]{2,1,0:T(8,128)(2,1)S(1)} %get-tuple-element.40.refs_1_), channel_id=1, source_target_pairs={{0,4},{4,0},{8,12},{12,8},{16,20},{20,16},{24,28},{28,24},{32,36},... | collective-permute-start | bytes 786440 | tf_op jit(solution)/shard_map/ppermute | solution.py:254
  7.7 1.9 %collective-permute-start.1 = (bf16[2,128,256]{2,1,0:T(8,128)(2,1)S(1)}, bf16[2,128,256]{2,1,0:T(8,128)(2,1)S(1)}, u32[]{:S(2)}, u32[]{:S(2)}) collective-permute-start(bf16[2,128,256]{2,1,0:T(8,128)(2,1)S(1)} %get-tuple-element.41), channel_id=1, source_target_pairs={{4,8},{12,16},{20,24},{28,32},{36,40},{44,48},{52,56},{60,64},{68,... | collective-permute-start | bytes 393224 | tf_op jit(solution)/shard_map/ppermute | solution.py:269
  9.7 0.0 collective-permute-done.refs_2_.refs_3_.refs_5_
  9.7 0.8 %start.1 = (bf16[128,256]{1,0:T(8,128)(2,1)S(1)}, bf16[64,256]{1,0:T(8,128)(2,1)S(1)}) custom-call(s32[2]{0:T(128)S(1)} %pad_add_fusion.refs_0_, bf16[2,256,256]{2,1,0:T(8,128)(2,1)S(1)} %get-tuple-element.40.refs_1_, bf16[2,256,256]{2,1,0:T(8,128)(2,1)S(1)} %collective-permute-done.refs_2_.refs_3_.refs_5_), custom_call_target="tpu_custom_call" | custom-call | tf_op jit(solution)/shard_map/start/pallas_call | solution.py:29
  10.5 0.6 collective-permute-start.2
  11.1 2.8 %collective-permute-start.3 = (bf16[64,256]{1,0:T(8,128)(2,1)S(1)}, bf16[64,256]{1,0:T(8,128)(2,1)S(1)}, u32[]{:S(2)}, u32[]{:S(2)}) collective-permute-start(bf16[64,256]{1,0:T(8,128)(2,1)S(1)} %get-tuple-element.43), channel_id=1, source_target_pairs={{0,16},{4,20},{8,24},{12,28},{16,0},{20,4},{24,8},{28,12},{32,48},... | collective-permute-start | bytes 98312 | tf_op jit(solution)/shard_map/ppermute | solution.py:254
  13.9 0.5 collective-permute-start.4
  14.4 0.7 collective-permute-done.1.refs_4_
  15.1 0.0 copy-done.1
  15.1 3.3 %near.3 = (f32[512,256]{1,0:T(8,128)S(1)}, f32[512,256]{1,0:T(8,128)S(1)}, f32[512,256]{1,0:T(8,128)S(1)}) custom-call(s32[2]{0:T(128)S(1)} %pad_add_fusion.refs_0_, bf16[2048,256]{1,0:T(8,128)(2,1)S(1)} %copy-done.1, bf16[2,3840,256]{2,1,0:T(8,128)(2,1)S(1)} %get-tuple-element.39.refs_2_, ...), custom_call_target="tpu_custom_call" | custom-call | tf_op jit(solution)/shard_map/near/pallas_call | solution.py:29
  18.4 0.0 collective-permute-done.3.refs_3_
  18.4 0.0 collective-permute-done.4.refs_4_
  18.4 0.0 collective-permute-done.2.refs_2_.refs_5_
  18.4 0.0 copy-done.2
  18.4 1.0 %middle.1 = (bf16[128,256]{1,0:T(8,128)(2,1)S(1)}, bf16[128,256]{1,0:T(8,128)(2,1)S(1)}, bf16[64,256]{1,0:T(8,128)(2,1)S(1)}, bf16[128,1024]{1,0:T(8,128)(2,1)S(1)}) custom-call(s32[2]{0:T(128)S(1)} %pad_add_fusion.refs_0_, bf16[128,256]{1,0:T(8,128)(2,1)S(1)} %get-tuple-element.42.refs_5_.refs_1_, ...), custom_call_target="tpu_custom_call" | custom-call | tf_op jit(solution)/shard_map/middle/pallas_call | solution.py:29
  19.4 1.1 %collective-permute-start.5 = (bf16[128,256]{1,0:T(8,128)(2,1)S(1)}, bf16[128,256]{1,0:T(8,128)(2,1)S(1)}, u32[]{:S(2)}, u32[]{:S(2)}) collective-permute-start(bf16[128,256]{1,0:T(8,128)(2,1)S(1)} %get-tuple-element.48.refs_5_.refs_1_), channel_id=1, source_target_pairs={{0,32},{4,36},{8,40},{12,44},{16,48},{20,52},{24,56},{28,60},{32,0... | collective-permute-start | bytes 196616 | tf_op jit(solution)/shard_map/ppermute | solution.py:254
  20.5 4.2 %collective-permute-start.6 = (bf16[64,256]{1,0:T(8,128)(2,1)S(1)}, bf16[64,256]{1,0:T(8,128)(2,1)S(1)}, u32[]{:S(2)}, u32[]{:S(2)}) collective-permute-start(bf16[64,256]{1,0:T(8,128)(2,1)S(1)} %get-tuple-element.49), channel_id=1, source_target_pairs={{0,64},{4,68},{8,72},{12,76},{16,80},{20,84},{24,88},{28,92},{32,9... | collective-permute-start | bytes 98312 | tf_op jit(solution)/shard_map/ppermute | solution.py:254
  24.7 0.0 collective-permute-start.7
  24.7 1.3 %collective-permute-start.12 = (bf16[128,1024]{1,0:T(8,128)(2,1)S(1)}, bf16[128,1024]{1,0:T(8,128)(2,1)S(1)}, u32[]{:S(2)}, u32[]{:S(2)}) collective-permute-start(bf16[128,1024]{1,0:T(8,128)(2,1)S(1)} %get-tuple-element.55.refs_7_), channel_id=1, source_target_pairs={{0,1},{1,2},{2,3},{3,0},{4,5},{5,6},{6,7},{7,4},{8,9},{9,10},{10,1... | collective-permute-start | bytes 786440 | tf_op jit(solution)/shard_map/ppermute | solution.py:257
  26.0 2.6 %collective-permute-start.13 = (bf16[128,1024]{1,0:T(8,128)(2,1)S(1)}, bf16[128,1024]{1,0:T(8,128)(2,1)S(1)}, u32[]{:S(2)}, u32[]{:S(2)}) collective-permute-start(bf16[128,1024]{1,0:T(8,128)(2,1)S(1)} %get-tuple-element.55.refs_7_), channel_id=1, source_target_pairs={{0,2},{1,3},{2,0},{3,1},{4,6},{5,7},{6,4},{7,5},{8,10},{9,11},{10,... | collective-permute-start | bytes 786440 | tf_op jit(solution)/shard_map/ppermute | solution.py:257
  28.6 3.3 %near.4 = (f32[512,256]{1,0:T(8,128)S(1)}, f32[512,256]{1,0:T(8,128)S(1)}, f32[512,256]{1,0:T(8,128)S(1)}) custom-call(s32[2]{0:T(128)S(1)} %pad_add_fusion.refs_0_, bf16[2048,256]{1,0:T(8,128)(2,1)S(1)} %copy-done.1, bf16[2,3840,256]{2,1,0:T(8,128)(2,1)S(1)} %get-tuple-element.39.refs_2_, ...), custom_call_target="tpu_custom_call" | custom-call | tf_op jit(solution)/shard_map/near/pallas_call | solution.py:29
  31.9 0.0 collective-permute-done.6.refs_3_
  31.9 0.0 collective-permute-done.7.refs_4_
  31.9 0.0 collective-permute-done.5.refs_2_
  31.9 0.9 %last.1 = (bf16[128,256]{1,0:T(8,128)(2,1)S(1)}, bf16[4,128,256]{2,1,0:T(8,128)(2,1)S(1)}, bf16[128,1024]{1,0:T(8,128)(2,1)S(1)}) custom-call(s32[2]{0:T(128)S(1)} %pad_add_fusion.refs_0_, bf16[128,256]{1,0:T(8,128)(2,1)S(1)} %get-tuple-element.48.refs_5_.refs_1_, bf16[128,256]{1,0:T(8,128)(2,1)S(1)} %collective-permute-done.5.refs_2_, ...), custom_call_target="tpu_custom_call" | custom-call | tf_op jit(solution)/shard_map/last/pallas_call | solution.py:29
  32.8 1.3 %collective-permute-start.11 = (bf16[128,1024]{1,0:T(8,128)(2,1)S(1)}, bf16[128,1024]{1,0:T(8,128)(2,1)S(1)}, u32[]{:S(2)}, u32[]{:S(2)}) collective-permute-start(bf16[128,1024]{1,0:T(8,128)(2,1)S(1)} %get-tuple-element.63), channel_id=1, source_target_pairs={{0,3},{1,0},{2,1},{3,2},{4,7},{5,4},{6,5},{7,6},{8,11},{9,8},{10,9... | collective-permute-start | bytes 786440 | tf_op jit(solution)/shard_map/ppermute | solution.py:257
  34.1 2.5 %collective-permute-start.9 = (bf16[128,256]{1,0:T(8,128)(2,1)S(1)}, bf16[128,256]{1,0:T(8,128)(2,1)S(1)}, u32[]{:S(2)}, u32[]{:S(2)}) collective-permute-start(bf16[128,256]{1,0:T(8,128)(2,1)S(1)} %get-tuple-element.56.refs_5_), channel_id=1, source_target_pairs={{0,224},{4,228},{8,232},{12,236},{16,240},{20,244},{24,248},{28,25... | collective-permute-start | bytes 196616 | tf_op jit(solution)/shard_map/ppermute | solution.py:254
  36.6 5.6 %near.5 = (f32[512,256]{1,0:T(8,128)S(1)}, f32[512,256]{1,0:T(8,128)S(1)}, f32[512,256]{1,0:T(8,128)S(1)}, f32[512,256]{1,0:T(8,128)S(1)}, f32[512,256]{1,0:T(8,128)S(1)}, /*index=5*/f32[512,256]{1,0:T(8,128)S(1)}) custom-call(s32[2]{0:T(128)S(1)} %pad_add_fusion.refs_0_, bf16[2048,256]{1,0:T(8,128)(2,1)S(1)} %copy-done.1, ...), custom_call_target="tpu_custom_call" | custom-call | tf_op jit(solution)/shard_map/near/pallas_call | solution.py:29
  42.2 0.0 collective-permute-done.9.refs_8_
  42.2 0.0 collective-permute-done.12.refs_2_
  42.2 0.0 collective-permute-done.13.refs_3_
  42.3 0.0 collective-permute-done.11.refs_1_
  42.3 0.6 pack.1.refs_3_
  42.9 5.1 %collective-permute-start.14 = (bf16[3,128,1024]{2,1,0:T(8,128)(2,1)S(1)}, bf16[3,128,1024]{2,1,0:T(8,128)(2,1)S(1)}, u32[]{:S(2)}, u32[]{:S(2)}) collective-permute-start(bf16[3,128,1024]{2,1,0:T(8,128)(2,1)S(1)} %pack.1.refs_3_), channel_id=1, source_target_pairs={{0,4},{4,0},{8,12},{12,8},{16,20},{20,16},{24,28},{28,24},{32,36},... | collective-permute-start | bytes 2359304 | tf_op jit(solution)/shard_map/ppermute | solution.py:254
  47.9 0.1 collective-permute-start.8
  48.0 0.4 collective-permute-start.10
  48.5 1.9 %collective-permute-done.10.refs_9_ = bf16[128,256]{1,0:T(8,128)(2,1)S(1)} collective-permute-done((bf16[128,256]{1,0:T(8,128)(2,1)S(1)}, bf16[128,256]{1,0:T(8,128)(2,1)S(1)}, u32[]{:S(2)}, u32[]{:S(2)}) %collective-permute-start.10) | collective-permute-done | bytes 65568 | tf_op jit(solution)/shard_map/ppermute | solution.py:254
  50.3 0.0 collective-permute-done.8.refs_7_
  50.3 3.1 %far.7 = bf16[512,256]{1,0:T(8,128)(2,1)S(1)} custom-call(s32[2]{0:T(128)S(1)} %pad_add_fusion.refs_0_, bf16[2048,256]{1,0:T(8,128)(2,1)S(1)} %copy-done.1, f32[512,256]{1,0:T(8,128)S(1)} %get-tuple-element.64.refs_4_.refs_2_, f32[512,256]{1,0:T(8,128)S(1)} %get-tuple-element.71.refs_3_, f32[512,256]{1,0:T(8,128)S(1)} %get-tuple-element.72.refs_4_, ...), custom_call_target="tpu_custom_call" | custom-call | tf_op jit(solution)/shard_map/far/pallas_call | solution.py:29
  53.4 0.4 collective-permute-start.17
  53.8 3.1 %far.6 = bf16[512,256]{1,0:T(8,128)(2,1)S(1)} custom-call(s32[2]{0:T(128)S(1)} %pad_add_fusion.refs_0_, bf16[2048,256]{1,0:T(8,128)(2,1)S(1)} %copy-done.1, f32[512,256]{1,0:T(8,128)S(1)} %get-tuple-element.68.refs_2_, f32[512,256]{1,0:T(8,128)S(1)} %get-tuple-element.69.refs_3_, f32[512,256]{1,0:T(8,128)S(1)} %get-tuple-element.70.refs_4_, ...), custom_call_target="tpu_custom_call" | custom-call | tf_op jit(solution)/shard_map/far/pallas_call | solution.py:29
  56.9 0.4 collective-permute-start.16
  57.3 3.1 %far.5 = bf16[512,256]{1,0:T(8,128)(2,1)S(1)} custom-call(s32[2]{0:T(128)S(1)} %pad_add_fusion.refs_0_, bf16[2048,256]{1,0:T(8,128)(2,1)S(1)} %copy-done.1, f32[512,256]{1,0:T(8,128)S(1)} %get-tuple-element.65.refs_2_, f32[512,256]{1,0:T(8,128)S(1)} %get-tuple-element.66.refs_3_, f32[512,256]{1,0:T(8,128)S(1)} %get-tuple-element.67.refs_4_, ...), custom_call_target="tpu_custom_call" | custom-call | tf_op jit(solution)/shard_map/far/pallas_call | solution.py:29
  60.4 2.5 %collective-permute-start.15 = (bf16[512,256]{1,0:T(8,128)(2,1)S(1)}, bf16[512,256]{1,0:T(8,128)(2,1)S(1)}, u32[]{:S(2)}, u32[]{:S(2)}) collective-permute-start(bf16[512,256]{1,0:T(8,128)(2,1)S(1)} %far.5), channel_id=1, source_target_pairs={{0,3},{1,0},{2,1},{3,2},{4,7},{5,4},{6,5},{7,6},{8,11},{9,8},{10,9... | collective-permute-start | bytes 786440 | tf_op jit(solution)/shard_map/ppermute | solution.py:257
  62.9 3.1 %far.4.refs_1_ = bf16[512,256]{1,0:T(8,128)(2,1)S(1)} custom-call(s32[2]{0:T(128)S(1)} %pad_add_fusion.refs_0_, bf16[2048,256]{1,0:T(8,128)(2,1)S(1)} %copy-done.1, f32[512,256]{1,0:T(8,128)S(1)} %get-tuple-element.57.refs_2_, f32[512,256]{1,0:T(8,128)S(1)} %get-tuple-element.58.refs_3_, f32[512,256]{1,0:T(8,128)S(1)} %get-tuple-element.59.refs_4_, ...), custom_call_target="tpu_custom_call" | custom-call | tf_op jit(solution)/shard_map/far/pallas_call | solution.py:29
  66.0 0.0 collective-permute-done.17.refs_7_
  66.0 3.1 %collective-permute-done.16.refs_6_ = bf16[512,256]{1,0:T(8,128)(2,1)S(1)} collective-permute-done((bf16[512,256]{1,0:T(8,128)(2,1)S(1)}, bf16[512,256]{1,0:T(8,128)(2,1)S(1)}, u32[]{:S(2)}, u32[]{:S(2)}) %collective-permute-start.16) | collective-permute-done | bytes 262176 | tf_op jit(solution)/shard_map/ppermute | solution.py:257
  69.1 0.0 collective-permute-done.15.refs_5_
  69.1 0.0 collective-permute-done.14.refs_4_
  69.1 2.8 %project.1 = bf16[512,1024]{1,0:T(8,128)(2,1)} custom-call(s32[2]{0:T(128)S(1)} %pad_add_fusion.refs_0_, bf16[512,256]{1,0:T(8,128)(2,1)S(1)} %far.4.refs_1_, bf16[256,1024]{1,0:T(8,128)(2,1)S(1)} %copy-done.2, bf16[3,128,1024]{2,1,0:T(8,128)(2,1)S(1)} %pack.1.refs_3_, bf16[3,128,1024]{2,1,0:T(8,128)(2,1)S(1)} %collective-permute-done.14.refs_4_, ...), custom_call_target="tpu_custom_call" | custom-call | tf_op jit(solution)/shard_map/project/pallas_call | solution.py:29
Async XLA Ops:
  0.1 1.2 %copy-start = (bf16[2048,256]{1,0:T(8,128)(2,1)S(1)}, bf16[2048,256]{1,0:T(8,128)(2,1)}, u32[]{:S(2)}) copy-start(bf16[2048,256]{1,0:T(8,128)(2,1)} %refs_1_.15) | copy-start | bytes 3145732
  1.3 1.6 %copy-start.3 = (bf16[2,2048,256]{2,1,0:T(8,128)(2,1)S(1)}, bf16[2,2048,256]{2,1,0:T(8,128)(2,1)}, u32[]{:S(2)}) copy-start(bf16[2,2048,256]{2,1,0:T(8,128)(2,1)} %refs_1_.8) | copy-start | bytes 6291460
  2.9 12.2 %copy-start.1 = (bf16[2048,256]{1,0:T(8,128)(2,1)S(1)}, bf16[2048,256]{1,0:T(8,128)(2,1)}, u32[]{:S(2)}) copy-start(bf16[2048,256]{1,0:T(8,128)(2,1)} %refs_1_.15) | copy-start | bytes 3145732
  2.9 15.5 %copy-start.2 = (bf16[256,1024]{1,0:T(8,128)(2,1)S(1)}, bf16[256,1024]{1,0:T(8,128)(2,1)}, u32[]{:S(2)}) copy-start(bf16[256,1024]{1,0:T(8,128)(2,1)} %refs_2_.3) | copy-start | bytes 1572868
  4.4 5.2 %collective-permute-start = (bf16[2,256,256]{2,1,0:T(8,128)(2,1)S(1)}, bf16[2,256,256]{2,1,0:T(8,128)(2,1)S(1)}, u32[]{:S(2)}, u32[]{:S(2)}) collective-permute-start(bf16[2,256,256]{2,1,0:T(8,128)(2,1)S(1)} %get-tuple-element.40.refs_1_), channel_id=1, source_target_pairs={{0,4},{4,0},{8,12},{12,8},{16,20},{20,16},{24,28},{28,24},{32,36},... | collective-permute-start | bytes 786440 | tf_op jit(solution)/shard_map/ppermute | solution.py:254
  7.7 7.3 %collective-permute-start.1 = (bf16[2,128,256]{2,1,0:T(8,128)(2,1)S(1)}, bf16[2,128,256]{2,1,0:T(8,128)(2,1)S(1)}, u32[]{:S(2)}, u32[]{:S(2)}) collective-permute-start(bf16[2,128,256]{2,1,0:T(8,128)(2,1)S(1)} %get-tuple-element.41), channel_id=1, source_target_pairs={{4,8},{12,16},{20,24},{28,32},{36,40},{44,48},{52,56},{60,64},{68,... | collective-permute-start | bytes 393224 | tf_op jit(solution)/shard_map/ppermute | solution.py:269
  10.5 7.9 %collective-permute-start.2 = (bf16[128,256]{1,0:T(8,128)(2,1)S(1)}, bf16[128,256]{1,0:T(8,128)(2,1)S(1)}, u32[]{:S(2)}, u32[]{:S(2)}) collective-permute-start(bf16[128,256]{1,0:T(8,128)(2,1)S(1)} %get-tuple-element.42.refs_5_.refs_1_), channel_id=1, source_target_pairs={{0,8},{4,12},{8,0},{12,4},{16,24},{20,28},{24,16},{28,20},{32,40},... | collective-permute-start | bytes 196616 | tf_op jit(solution)/shard_map/ppermute | solution.py:254
  11.1 7.3 %collective-permute-start.3 = (bf16[64,256]{1,0:T(8,128)(2,1)S(1)}, bf16[64,256]{1,0:T(8,128)(2,1)S(1)}, u32[]{:S(2)}, u32[]{:S(2)}) collective-permute-start(bf16[64,256]{1,0:T(8,128)(2,1)S(1)} %get-tuple-element.43), channel_id=1, source_target_pairs={{0,16},{4,20},{8,24},{12,28},{16,0},{20,4},{24,8},{28,12},{32,48},... | collective-permute-start | bytes 98312 | tf_op jit(solution)/shard_map/ppermute | solution.py:254
  13.9 4.5 %collective-permute-start.4 = (bf16[64,256]{1,0:T(8,128)(2,1)S(1)}, bf16[64,256]{1,0:T(8,128)(2,1)S(1)}, u32[]{:S(2)}, u32[]{:S(2)}) collective-permute-start(bf16[64,256]{1,0:T(8,128)(2,1)S(1)} %get-tuple-element.43), channel_id=1, source_target_pairs={{0,24},{4,28},{8,16},{12,20},{16,8},{20,12},{24,0},{28,4},{32,56},... | collective-permute-start | bytes 98312 | tf_op jit(solution)/shard_map/ppermute | solution.py:254
  19.4 12.6 %collective-permute-start.5 = (bf16[128,256]{1,0:T(8,128)(2,1)S(1)}, bf16[128,256]{1,0:T(8,128)(2,1)S(1)}, u32[]{:S(2)}, u32[]{:S(2)}) collective-permute-start(bf16[128,256]{1,0:T(8,128)(2,1)S(1)} %get-tuple-element.48.refs_5_.refs_1_), channel_id=1, source_target_pairs={{0,32},{4,36},{8,40},{12,44},{16,48},{20,52},{24,56},{28,60},{32,0... | collective-permute-start | bytes 196616 | tf_op jit(solution)/shard_map/ppermute | solution.py:254
  20.5 11.4 %collective-permute-start.6 = (bf16[64,256]{1,0:T(8,128)(2,1)S(1)}, bf16[64,256]{1,0:T(8,128)(2,1)S(1)}, u32[]{:S(2)}, u32[]{:S(2)}) collective-permute-start(bf16[64,256]{1,0:T(8,128)(2,1)S(1)} %get-tuple-element.49), channel_id=1, source_target_pairs={{0,64},{4,68},{8,72},{12,76},{16,80},{20,84},{24,88},{28,92},{32,9... | collective-permute-start | bytes 98312 | tf_op jit(solution)/shard_map/ppermute | solution.py:254
  24.7 7.2 %collective-permute-start.7 = (bf16[64,256]{1,0:T(8,128)(2,1)S(1)}, bf16[64,256]{1,0:T(8,128)(2,1)S(1)}, u32[]{:S(2)}, u32[]{:S(2)}) collective-permute-start(bf16[64,256]{1,0:T(8,128)(2,1)S(1)} %get-tuple-element.49), channel_id=1, source_target_pairs={{0,96},{4,100},{8,104},{12,108},{16,112},{20,116},{24,120},{28,124... | collective-permute-start | bytes 98312 | tf_op jit(solution)/shard_map/ppermute | solution.py:254
  24.7 17.5 %collective-permute-start.12 = (bf16[128,1024]{1,0:T(8,128)(2,1)S(1)}, bf16[128,1024]{1,0:T(8,128)(2,1)S(1)}, u32[]{:S(2)}, u32[]{:S(2)}) collective-permute-start(bf16[128,1024]{1,0:T(8,128)(2,1)S(1)} %get-tuple-element.55.refs_7_), channel_id=1, source_target_pairs={{0,1},{1,2},{2,3},{3,0},{4,5},{5,6},{6,7},{7,4},{8,9},{9,10},{10,1... | collective-permute-start | bytes 786440 | tf_op jit(solution)/shard_map/ppermute | solution.py:257
  26.0 16.3 %collective-permute-start.13 = (bf16[128,1024]{1,0:T(8,128)(2,1)S(1)}, bf16[128,1024]{1,0:T(8,128)(2,1)S(1)}, u32[]{:S(2)}, u32[]{:S(2)}) collective-permute-start(bf16[128,1024]{1,0:T(8,128)(2,1)S(1)} %get-tuple-element.55.refs_7_), channel_id=1, source_target_pairs={{0,2},{1,3},{2,0},{3,1},{4,6},{5,7},{6,4},{7,5},{8,10},{9,11},{10,... | collective-permute-start | bytes 786440 | tf_op jit(solution)/shard_map/ppermute | solution.py:257
  32.8 9.5 %collective-permute-start.11 = (bf16[128,1024]{1,0:T(8,128)(2,1)S(1)}, bf16[128,1024]{1,0:T(8,128)(2,1)S(1)}, u32[]{:S(2)}, u32[]{:S(2)}) collective-permute-start(bf16[128,1024]{1,0:T(8,128)(2,1)S(1)} %get-tuple-element.63), channel_id=1, source_target_pairs={{0,3},{1,0},{2,1},{3,2},{4,7},{5,4},{6,5},{7,6},{8,11},{9,8},{10,9... | collective-permute-start | bytes 786440 | tf_op jit(solution)/shard_map/ppermute | solution.py:257
  34.1 8.1 %collective-permute-start.9 = (bf16[128,256]{1,0:T(8,128)(2,1)S(1)}, bf16[128,256]{1,0:T(8,128)(2,1)S(1)}, u32[]{:S(2)}, u32[]{:S(2)}) collective-permute-start(bf16[128,256]{1,0:T(8,128)(2,1)S(1)} %get-tuple-element.56.refs_5_), channel_id=1, source_target_pairs={{0,224},{4,228},{8,232},{12,236},{16,240},{20,244},{24,248},{28,25... | collective-permute-start | bytes 196616 | tf_op jit(solution)/shard_map/ppermute | solution.py:254
  42.9 26.2 %collective-permute-start.14 = (bf16[3,128,1024]{2,1,0:T(8,128)(2,1)S(1)}, bf16[3,128,1024]{2,1,0:T(8,128)(2,1)S(1)}, u32[]{:S(2)}, u32[]{:S(2)}) collective-permute-start(bf16[3,128,1024]{2,1,0:T(8,128)(2,1)S(1)} %pack.1.refs_3_), channel_id=1, source_target_pairs={{0,4},{4,0},{8,12},{12,8},{16,20},{20,16},{24,28},{28,24},{32,36},... | collective-permute-start | bytes 2359304 | tf_op jit(solution)/shard_map/ppermute | solution.py:254
  47.9 2.4 %collective-permute-start.8 = (bf16[4,128,256]{2,1,0:T(8,128)(2,1)S(1)}, bf16[4,128,256]{2,1,0:T(8,128)(2,1)S(1)}, u32[]{:S(2)}, u32[]{:S(2)}) collective-permute-start(bf16[4,128,256]{2,1,0:T(8,128)(2,1)S(1)} %get-tuple-element.60.refs_6_), channel_id=1, source_target_pairs={{0,4},{4,0},{8,12},{12,8},{16,20},{20,16},{24,28},{28,24},{32,36},... | collective-permute-start | bytes 786440 | tf_op jit(solution)/shard_map/ppermute | solution.py:254
  48.0 2.3 %collective-permute-start.10 = (bf16[128,256]{1,0:T(8,128)(2,1)S(1)}, bf16[128,256]{1,0:T(8,128)(2,1)S(1)}, u32[]{:S(2)}, u32[]{:S(2)}) collective-permute-start(bf16[128,256]{1,0:T(8,128)(2,1)S(1)} %collective-permute-done.9.refs_8_), channel_id=1, source_target_pairs={{0,4},{4,0},{8,12},{12,8},{16,20},{20,16},{24,28},{28,24},{32,36},... | collective-permute-start | bytes 196616 | tf_op jit(solution)/shard_map/ppermute | solution.py:254
  53.4 12.6 %collective-permute-start.17 = (bf16[512,256]{1,0:T(8,128)(2,1)S(1)}, bf16[512,256]{1,0:T(8,128)(2,1)S(1)}, u32[]{:S(2)}, u32[]{:S(2)}) collective-permute-start(bf16[512,256]{1,0:T(8,128)(2,1)S(1)} %far.7), channel_id=1, source_target_pairs={{0,2},{1,3},{2,0},{3,1},{4,6},{5,7},{6,4},{7,5},{8,10},{9,11},{10,... | collective-permute-start | bytes 786440 | tf_op jit(solution)/shard_map/ppermute | solution.py:257
  56.9 12.2 %collective-permute-start.16 = (bf16[512,256]{1,0:T(8,128)(2,1)S(1)}, bf16[512,256]{1,0:T(8,128)(2,1)S(1)}, u32[]{:S(2)}, u32[]{:S(2)}) collective-permute-start(bf16[512,256]{1,0:T(8,128)(2,1)S(1)} %far.6), channel_id=1, source_target_pairs={{0,1},{1,2},{2,3},{3,0},{4,5},{5,6},{6,7},{7,4},{8,9},{9,10},{10,1... | collective-permute-start | bytes 786440 | tf_op jit(solution)/shard_map/ppermute | solution.py:257
  60.4 8.7 %collective-permute-start.15 = (bf16[512,256]{1,0:T(8,128)(2,1)S(1)}, bf16[512,256]{1,0:T(8,128)(2,1)S(1)}, u32[]{:S(2)}, u32[]{:S(2)}) collective-permute-start(bf16[512,256]{1,0:T(8,128)(2,1)S(1)} %far.5), channel_id=1, source_target_pairs={{0,3},{1,0},{2,1},{3,2},{4,7},{5,4},{6,5},{7,6},{8,11},{9,8},{10,9... | collective-permute-start | bytes 786440 | tf_op jit(solution)/shard_map/ppermute | solution.py:257

commit v5 on v1

--- a/solution.py
+++ b/solution.py
@@ -231,11 +231,14 @@
     )
 
 
-def project_kernel(at_ref, own_ref, w_own_ref, *refs):
+def project_kernel(at_ref, own_ref, w_own_ref, a_ref, mine_ref, other_ref, sum_ref):
     total = jnp.dot(own_ref[...], w_own_ref[...], preferred_element_type=F32)
-    for i in range(3):
-        total = total + times(at_ref, *refs[3 * i : 3 * i + 3])
-    refs[9][...] = total.astype(BF16)
+    sum_ref[...] = total + times(at_ref, a_ref, mine_ref, other_ref)
+
+
+def finish_kernel(at_ref, sum_ref, *refs):
+    total = times(at_ref, *refs[:3]) + times(at_ref, *refs[3:6])
+    refs[6][...] = (sum_ref[...] + total).astype(BF16)
 
 
 def body(queries, keys_values, out_weight):
@@ -311,11 +314,11 @@
         )
         atts.append(turn(att, by) if by else att)
     pieces = list(zip(atts, w_mine, w_other))
+    (part,) = call(
+        project_kernel, "project", [((CHUNK, 1024), F32)], (at, atts[3], out_weight, *pieces[2])
+    )
     (out,) = call(
-        project_kernel,
-        "project",
-        [((CHUNK, 1024), BF16)],
-        (at, atts[3], out_weight, *pieces[2], *pieces[1], *pieces[0]),
+        finish_kernel, "finish", [((CHUNK, 1024), BF16)], (at, part, *pieces[1], *pieces[0])
     )
     return out
 

time: 70 us -> 73.3 us (1.047)
  waiting for transfers between devices: 5.08 us -> 7.14 us
    ppermute x6, waiting for transfers between devices: 2.1 us -> 6.4 us  [turn(): lax.ppermute(x, 'head', [(i, (i + by) % heads) for i in range(heads)])]
    ppermute x13, waiting for transfers between devices: 2.27 us -> 0.03 us  [swap(): return lax.ppermute(x, 'ctx', [(i, i ^ bits) for i in range(shards)])]
    pallas_call x12 -> x13, Pallas kernels: 31.5 us -> 32.2 us  [call(): pl.pallas_call(lambda *refs: kernel(*refs[:n], *refs[n + late:]), out_sha...]
  transfers between devices with their start and end apart: 20 -> 20, of which waited for: 5 -> 3; matrix products, arithmetic and copies ran while one was open for 0% -> 0% of each run, Pallas kernels for 37% -> 38%
where the time goes in v5:
time: 73.3 us; the launch traced here: 73.2 us
  Pallas kernels  32.2 us (44%)
  starting transfers between devices  30.8 us (42%)
  waiting for transfers between devices  7.14 us (10%)
  local copies, waits for them, and re-layouts  2.82 us (4%)
    pallas_call x13, Pallas kernels, call(): pl.pallas_call(lambda *refs: kernel(*refs[:n], *refs[n + late:]), out_sha...  32.2 us
    ppermute x13, starting transfers between devices, swap(): return lax.ppermute(x, 'ctx', [(i, i ^ bits) for i in range(shards)])  21.6 us
    ppermute x6, starting transfers between devices, turn(): lax.ppermute(x, 'head', [(i, (i + by) % heads) for i in range(heads)])  7.25 us
    ppermute x6, waiting for transfers between devices, turn(): lax.ppermute(x, 'head', [(i, (i + by) % heads) for i in range(heads)])  6.4 us
    unnamed x8, local copies, waits for them, and re-layouts  2.82 us
    ppermute x1, starting transfers between devices, body(): back = lax.ppermute(back, 'ctx', ends + [(b, a) for a, b in ends])  1.91 us
  transfers between devices with their start and end apart: 20, of which 3 were waited for; matrix products, arithmetic and copies ran while one was open for 0% of the time, Pallas kernels for 38%

profile of v5, /device:TPU:1, one launch (start us, length us, event | category | flops | bytes accessed | tf_op | source)
XLA Modules:
  0.0 73.2 jit_solution(6152493245786055690)
XLA Ops:
  0.0 0.1 pad_add_fusion.refs_0_
  0.1 0.0 copy-start
  0.1 1.2 %copy-done = bf16[2048,256]{1,0:T(8,128)(2,1)S(1)} copy-done((bf16[2048,256]{1,0:T(8,128)(2,1)S(1)}, bf16[2048,256]{1,0:T(8,128)(2,1)}, u32[]{:S(2)}) %copy-start) | copy-done | bytes 1048600
  1.3 0.0 copy-start.2
  1.3 1.6 %copy-done.2 = bf16[2,2048,256]{2,1,0:T(8,128)(2,1)S(1)} copy-done((bf16[2,2048,256]{2,1,0:T(8,128)(2,1)S(1)}, bf16[2,2048,256]{2,1,0:T(8,128)(2,1)}, u32[]{:S(2)}) %copy-start.2) | copy-done | bytes 2097176
  2.9 0.0 copy-start.1
  2.9 1.5 %pyramid.1 = (bf16[2,3840,256]{2,1,0:T(8,128)(2,1)S(1)}, bf16[2,256,256]{2,1,0:T(8,128)(2,1)S(1)}, bf16[2,128,256]{2,1,0:T(8,128)(2,1)S(1)}) custom-call(s32[2]{0:T(128)S(1)} %pad_add_fusion.refs_0_, bf16[2,2048,256]{2,1,0:T(8,128)(2,1)S(1)} %copy-done.2, bf16[2048,256]{1,0:T(8,128)(2,1)S(1)} %copy-done), custom_call_target="tpu_custom_call" | custom-call | tf_op jit(solution)/shard_map/pyramid/pallas_call | solution.py:29
  4.4 3.3 %collective-permute-start = (bf16[2,256,256]{2,1,0:T(8,128)(2,1)S(1)}, bf16[2,256,256]{2,1,0:T(8,128)(2,1)S(1)}, u32[]{:S(2)}, u32[]{:S(2)}) collective-permute-start(bf16[2,256,256]{2,1,0:T(8,128)(2,1)S(1)} %get-tuple-element.41.refs_1_), channel_id=1, source_target_pairs={{0,4},{4,0},{8,12},{12,8},{16,20},{20,16},{24,28},{28,24},{32,36},... | collective-permute-start | bytes 786440 | tf_op jit(solution)/shard_map/ppermute | solution.py:253
  7.7 1.9 %collective-permute-start.1 = (bf16[2,128,256]{2,1,0:T(8,128)(2,1)S(1)}, bf16[2,128,256]{2,1,0:T(8,128)(2,1)S(1)}, u32[]{:S(2)}, u32[]{:S(2)}) collective-permute-start(bf16[2,128,256]{2,1,0:T(8,128)(2,1)S(1)} %get-tuple-element.42), channel_id=1, source_target_pairs={{4,8},{12,16},{20,24},{28,32},{36,40},{44,48},{52,56},{60,64},{68,... | collective-permute-start | bytes 393224 | tf_op jit(solution)/shard_map/ppermute | solution.py:268
  9.7 0.0 collective-permute-done.refs_2_.refs_3_.refs_5_
  9.7 0.8 %start.1 = (bf16[128,256]{1,0:T(8,128)(2,1)S(1)}, bf16[64,256]{1,0:T(8,128)(2,1)S(1)}) custom-call(s32[2]{0:T(128)S(1)} %pad_add_fusion.refs_0_, bf16[2,256,256]{2,1,0:T(8,128)(2,1)S(1)} %get-tuple-element.41.refs_1_, bf16[2,256,256]{2,1,0:T(8,128)(2,1)S(1)} %collective-permute-done.refs_2_.refs_3_.refs_5_), custom_call_target="tpu_custom_call" | custom-call | tf_op jit(solution)/shard_map/start/pallas_call | solution.py:29
  10.5 0.6 collective-permute-start.2
  11.1 2.8 %collective-permute-start.3 = (bf16[64,256]{1,0:T(8,128)(2,1)S(1)}, bf16[64,256]{1,0:T(8,128)(2,1)S(1)}, u32[]{:S(2)}, u32[]{:S(2)}) collective-permute-start(bf16[64,256]{1,0:T(8,128)(2,1)S(1)} %get-tuple-element.44), channel_id=1, source_target_pairs={{0,16},{4,20},{8,24},{12,28},{16,0},{20,4},{24,8},{28,12},{32,48},... | collective-permute-start | bytes 98312 | tf_op jit(solution)/shard_map/ppermute | solution.py:253
  13.9 0.5 collective-permute-start.4
  14.4 0.7 collective-permute-done.1.refs_4_
  15.1 0.0 copy-done.1
  15.1 0.0 copy-start.3
  15.1 3.3 %near.3 = (f32[512,256]{1,0:T(8,128)S(1)}, f32[512,256]{1,0:T(8,128)S(1)}, f32[512,256]{1,0:T(8,128)S(1)}) custom-call(s32[2]{0:T(128)S(1)} %pad_add_fusion.refs_0_, bf16[2048,256]{1,0:T(8,128)(2,1)S(1)} %copy-done.1, bf16[2,3840,256]{2,1,0:T(8,128)(2,1)S(1)} %get-tuple-element.40.refs_2_, ...), custom_call_target="tpu_custom_call" | custom-call | tf_op jit(solution)/shard_map/near/pallas_call | solution.py:29
  18.4 0.0 collective-permute-done.3.refs_3_
  18.4 0.0 collective-permute-done.4.refs_4_
  18.4 0.0 collective-permute-done.2.refs_2_.refs_5_
  18.4 0.0 copy-done.3
  18.4 1.0 %middle.1 = (bf16[128,256]{1,0:T(8,128)(2,1)S(1)}, bf16[128,256]{1,0:T(8,128)(2,1)S(1)}, bf16[64,256]{1,0:T(8,128)(2,1)S(1)}, bf16[128,1024]{1,0:T(8,128)(2,1)S(1)}) custom-call(s32[2]{0:T(128)S(1)} %pad_add_fusion.refs_0_, bf16[128,256]{1,0:T(8,128)(2,1)S(1)} %get-tuple-element.43.refs_5_.refs_1_, ...), custom_call_target="tpu_custom_call" | custom-call | tf_op jit(solution)/shard_map/middle/pallas_call | solution.py:29
  19.4 1.1 %collective-permute-start.5 = (bf16[128,256]{1,0:T(8,128)(2,1)S(1)}, bf16[128,256]{1,0:T(8,128)(2,1)S(1)}, u32[]{:S(2)}, u32[]{:S(2)}) collective-permute-start(bf16[128,256]{1,0:T(8,128)(2,1)S(1)} %get-tuple-element.49.refs_5_.refs_1_), channel_id=1, source_target_pairs={{0,32},{4,36},{8,40},{12,44},{16,48},{20,52},{24,56},{28,60},{32,0... | collective-permute-start | bytes 196616 | tf_op jit(solution)/shard_map/ppermute | solution.py:253
  20.5 4.2 %collective-permute-start.6 = (bf16[64,256]{1,0:T(8,128)(2,1)S(1)}, bf16[64,256]{1,0:T(8,128)(2,1)S(1)}, u32[]{:S(2)}, u32[]{:S(2)}) collective-permute-start(bf16[64,256]{1,0:T(8,128)(2,1)S(1)} %get-tuple-element.50), channel_id=1, source_target_pairs={{0,64},{4,68},{8,72},{12,76},{16,80},{20,84},{24,88},{28,92},{32,9... | collective-permute-start | bytes 98312 | tf_op jit(solution)/shard_map/ppermute | solution.py:253
  24.7 0.0 collective-permute-start.7
  24.7 2.9 %collective-permute-start.12 = (bf16[128,1024]{1,0:T(8,128)(2,1)S(1)}, bf16[128,1024]{1,0:T(8,128)(2,1)S(1)}, u32[]{:S(2)}, u32[]{:S(2)}) collective-permute-start(bf16[128,1024]{1,0:T(8,128)(2,1)S(1)} %get-tuple-element.67), channel_id=1, source_target_pairs={{0,2},{1,3},{2,0},{3,1},{4,6},{5,7},{6,4},{7,5},{8,10},{9,11},{10,... | collective-permute-start | bytes 786440 | tf_op jit(solution)/shard_map/ppermute | solution.py:256
  27.6 3.3 %near.4 = (f32[512,256]{1,0:T(8,128)S(1)}, f32[512,256]{1,0:T(8,128)S(1)}, f32[512,256]{1,0:T(8,128)S(1)}) custom-call(s32[2]{0:T(128)S(1)} %pad_add_fusion.refs_0_, bf16[2048,256]{1,0:T(8,128)(2,1)S(1)} %copy-done.1, bf16[2,3840,256]{2,1,0:T(8,128)(2,1)S(1)} %get-tuple-element.40.refs_2_, ...), custom_call_target="tpu_custom_call" | custom-call | tf_op jit(solution)/shard_map/near/pallas_call | solution.py:29
  30.9 0.0 collective-permute-done.6.refs_3_
  30.9 0.0 collective-permute-done.7.refs_4_
  30.9 0.0 collective-permute-done.5.refs_2_
  30.9 0.9 %last.1 = (bf16[128,256]{1,0:T(8,128)(2,1)S(1)}, bf16[4,128,256]{2,1,0:T(8,128)(2,1)S(1)}) custom-call(s32[2]{0:T(128)S(1)} %pad_add_fusion.refs_0_, bf16[128,256]{1,0:T(8,128)(2,1)S(1)} %get-tuple-element.49.refs_5_.refs_1_, bf16[128,256]{1,0:T(8,128)(2,1)S(1)} %collective-permute-done.5.refs_2_, bf16[64,256]{1,0:T(8,128)(2,1)S(1)} %collective-permute-done.6.refs_3_, ...), custom_call_target="tpu_custom_call" | custom-call | tf_op jit(solution)/shard_map/last/pallas_call | solution.py:29
  31.8 1.1 %collective-permute-start.8 = (bf16[4,128,256]{2,1,0:T(8,128)(2,1)S(1)}, bf16[4,128,256]{2,1,0:T(8,128)(2,1)S(1)}, u32[]{:S(2)}, u32[]{:S(2)}) collective-permute-start(bf16[4,128,256]{2,1,0:T(8,128)(2,1)S(1)} %get-tuple-element.60.refs_6_), channel_id=1, source_target_pairs={{0,4},{4,0},{8,12},{12,8},{16,20},{20,16},{24,28},{28,24},{32,36},... | collective-permute-start | bytes 786440 | tf_op jit(solution)/shard_map/ppermute | solution.py:253
  32.8 5.6 %collective-permute-start.9 = (bf16[128,256]{1,0:T(8,128)(2,1)S(1)}, bf16[128,256]{1,0:T(8,128)(2,1)S(1)}, u32[]{:S(2)}, u32[]{:S(2)}) collective-permute-start(bf16[128,256]{1,0:T(8,128)(2,1)S(1)} %get-tuple-element.56.refs_5_), channel_id=1, source_target_pairs={{0,224},{4,228},{8,232},{12,236},{16,240},{20,244},{24,248},{28,25... | collective-permute-start | bytes 196616 | tf_op jit(solution)/shard_map/ppermute | solution.py:253
  38.5 5.6 %near.5 = (f32[512,256]{1,0:T(8,128)S(1)}, f32[512,256]{1,0:T(8,128)S(1)}, f32[512,256]{1,0:T(8,128)S(1)}, f32[512,256]{1,0:T(8,128)S(1)}, f32[512,256]{1,0:T(8,128)S(1)}, /*index=5*/f32[512,256]{1,0:T(8,128)S(1)}) custom-call(s32[2]{0:T(128)S(1)} %pad_add_fusion.refs_0_, bf16[2048,256]{1,0:T(8,128)(2,1)S(1)} %copy-done.1, ...), custom_call_target="tpu_custom_call" | custom-call | tf_op jit(solution)/shard_map/near/pallas_call | solution.py:29
  44.1 0.0 collective-permute-done.9.refs_8_
  44.1 0.6 collective-permute-start.10
  44.8 0.0 collective-permute-done.12.refs_6_
  44.8 0.8 %collective-permute-start.13 = (bf16[128,1024]{1,0:T(8,128)(2,1)S(1)}, bf16[128,1024]{1,0:T(8,128)(2,1)S(1)}, u32[]{:S(2)}, u32[]{:S(2)}) collective-permute-start(bf16[128,1024]{1,0:T(8,128)(2,1)S(1)} %get-tuple-element.67), channel_id=1, source_target_pairs={{0,3},{1,0},{2,1},{3,2},{4,7},{5,4},{6,5},{7,6},{8,11},{9,8},{10,9... | collective-permute-start | bytes 786440 | tf_op jit(solution)/shard_map/ppermute | solution.py:256
  45.6 0.7 collective-permute-start.16
  46.3 0.0 collective-permute-done.10.refs_9_
  46.3 0.0 collective-permute-done.8.refs_7_
  46.3 3.1 %far.5 = bf16[512,256]{1,0:T(8,128)(2,1)S(1)} custom-call(s32[2]{0:T(128)S(1)} %pad_add_fusion.refs_0_, bf16[2048,256]{1,0:T(8,128)(2,1)S(1)} %copy-done.1, f32[512,256]{1,0:T(8,128)S(1)} %get-tuple-element.63.refs_2_, f32[512,256]{1,0:T(8,128)S(1)} %get-tuple-element.64.refs_3_, f32[512,256]{1,0:T(8,128)S(1)} %get-tuple-element.65.refs_4_, ...), custom_call_target="tpu_custom_call" | custom-call | tf_op jit(solution)/shard_map/far/pallas_call | solution.py:29
  49.4 2.1 %collective-permute-start.11 = (bf16[512,256]{1,0:T(8,128)(2,1)S(1)}, bf16[512,256]{1,0:T(8,128)(2,1)S(1)}, u32[]{:S(2)}, u32[]{:S(2)}) collective-permute-start(bf16[512,256]{1,0:T(8,128)(2,1)S(1)} %far.5), channel_id=1, source_target_pairs={{0,3},{1,0},{2,1},{3,2},{4,7},{5,4},{6,5},{7,6},{8,11},{9,8},{10,9... | collective-permute-start | bytes 786440 | tf_op jit(solution)/shard_map/ppermute | solution.py:256
  51.4 0.9 %collective-permute-start.19 = (bf16[128,1024]{1,0:T(8,128)(2,1)S(1)}, bf16[128,1024]{1,0:T(8,128)(2,1)S(1)}, u32[]{:S(2)}, u32[]{:S(2)}) collective-permute-start(bf16[128,1024]{1,0:T(8,128)(2,1)S(1)} %collective-permute-done.12.refs_6_), channel_id=1, source_target_pairs={{0,4},{4,0},{8,12},{12,8},{16,20},{20,16},{24,28},{28,24},{32,36},... | collective-permute-start | bytes 786440 | tf_op jit(solution)/shard_map/ppermute | solution.py:253
  52.4 3.1 %far.7 = bf16[512,256]{1,0:T(8,128)(2,1)S(1)} custom-call(s32[2]{0:T(128)S(1)} %pad_add_fusion.refs_0_, bf16[2048,256]{1,0:T(8,128)(2,1)S(1)} %copy-done.1, f32[512,256]{1,0:T(8,128)S(1)} %get-tuple-element.71.refs_2_, f32[512,256]{1,0:T(8,128)S(1)} %get-tuple-element.72.refs_3_, f32[512,256]{1,0:T(8,128)S(1)} %get-tuple-element.73.refs_4_, ...), custom_call_target="tpu_custom_call" | custom-call | tf_op jit(solution)/shard_map/far/pallas_call | solution.py:29
  55.5 0.3 collective-permute-start.18
  55.7 0.0 collective-permute-done.13.refs_4_
  55.7 0.3 collective-permute-start.14
  56.0 3.1 %far.6 = bf16[512,256]{1,0:T(8,128)(2,1)S(1)} custom-call(s32[2]{0:T(128)S(1)} %pad_add_fusion.refs_0_, bf16[2048,256]{1,0:T(8,128)(2,1)S(1)} %copy-done.1, f32[512,256]{1,0:T(8,128)S(1)} %get-tuple-element.68.refs_2_, f32[512,256]{1,0:T(8,128)S(1)} %get-tuple-element.69.refs_3_, f32[512,256]{1,0:T(8,128)S(1)} %get-tuple-element.70.refs_4_, ...), custom_call_target="tpu_custom_call" | custom-call | tf_op jit(solution)/shard_map/far/pallas_call | solution.py:29
  59.1 0.0 collective-permute-done.16.refs_3_
  59.1 0.5 collective-permute-start.15
  59.7 0.0 collective-permute-done.11.refs_3_
  59.7 0.5 collective-permute-start.17
  60.1 3.1 %far.4.refs_1_ = bf16[512,256]{1,0:T(8,128)(2,1)S(1)} custom-call(s32[2]{0:T(128)S(1)} %pad_add_fusion.refs_0_, bf16[2048,256]{1,0:T(8,128)(2,1)S(1)} %copy-done.1, f32[512,256]{1,0:T(8,128)S(1)} %get-tuple-element.57.refs_2_, f32[512,256]{1,0:T(8,128)S(1)} %get-tuple-element.58.refs_3_, f32[512,256]{1,0:T(8,128)S(1)} %get-tuple-element.59.refs_4_, ...), custom_call_target="tpu_custom_call" | custom-call | tf_op jit(solution)/shard_map/far/pallas_call | solution.py:29
  63.2 0.0 collective-permute-done.14.refs_5_
  63.3 1.3 %project.1.refs_1_ = f32[512,1024]{1,0:T(8,128)S(1)} custom-call(s32[2]{0:T(128)S(1)} %pad_add_fusion.refs_0_, bf16[512,256]{1,0:T(8,128)(2,1)S(1)} %far.4.refs_1_, bf16[256,1024]{1,0:T(8,128)(2,1)S(1)} %copy-done.3, bf16[512,256]{1,0:T(8,128)(2,1)S(1)} %collective-permute-done.11.refs_3_, bf16[128,1024]{1,0:T(8,128)(2,1)S(1)} %collective-permute-done.13.refs_4_, ...), custom_call_target="tpu_custom_call" | custom-call | tf_op jit(solution)/shard_map/project/pallas_call | solution.py:29
  64.5 0.0 collective-permute-done.19.refs_7_
  64.5 0.5 collective-permute-done.18.refs_5_
  65.0 5.9 %collective-permute-done.15.refs_2_ = bf16[512,256]{1,0:T(8,128)(2,1)S(1)} collective-permute-done((bf16[512,256]{1,0:T(8,128)(2,1)S(1)}, bf16[512,256]{1,0:T(8,128)(2,1)S(1)}, u32[]{:S(2)}, u32[]{:S(2)}) %collective-permute-start.15) | collective-permute-done | bytes 262176 | tf_op jit(solution)/shard_map/ppermute | solution.py:256
  70.9 0.0 collective-permute-done.17.refs_4_
  70.9 2.2 %finish.1 = bf16[512,1024]{1,0:T(8,128)(2,1)} custom-call(s32[2]{0:T(128)S(1)} %pad_add_fusion.refs_0_, f32[512,1024]{1,0:T(8,128)S(1)} %project.1.refs_1_, bf16[512,256]{1,0:T(8,128)(2,1)S(1)} %collective-permute-done.15.refs_2_, bf16[128,1024]{1,0:T(8,128)(2,1)S(1)} %collective-permute-done.16.refs_3_, ...), custom_call_target="tpu_custom_call" | custom-call | tf_op jit(solution)/shard_map/finish/pallas_call | solution.py:29
Async XLA Ops:
  0.1 1.2 %copy-start = (bf16[2048,256]{1,0:T(8,128)(2,1)S(1)}, bf16[2048,256]{1,0:T(8,128)(2,1)}, u32[]{:S(2)}) copy-start(bf16[2048,256]{1,0:T(8,128)(2,1)} %refs_1_.15) | copy-start | bytes 3145732
  1.3 1.6 %copy-start.2 = (bf16[2,2048,256]{2,1,0:T(8,128)(2,1)S(1)}, bf16[2,2048,256]{2,1,0:T(8,128)(2,1)}, u32[]{:S(2)}) copy-start(bf16[2,2048,256]{2,1,0:T(8,128)(2,1)} %refs_1_.8) | copy-start | bytes 6291460
  2.9 12.2 %copy-start.1 = (bf16[2048,256]{1,0:T(8,128)(2,1)S(1)}, bf16[2048,256]{1,0:T(8,128)(2,1)}, u32[]{:S(2)}) copy-start(bf16[2048,256]{1,0:T(8,128)(2,1)} %refs_1_.15) | copy-start | bytes 3145732
  4.4 5.2 %collective-permute-start = (bf16[2,256,256]{2,1,0:T(8,128)(2,1)S(1)}, bf16[2,256,256]{2,1,0:T(8,128)(2,1)S(1)}, u32[]{:S(2)}, u32[]{:S(2)}) collective-permute-start(bf16[2,256,256]{2,1,0:T(8,128)(2,1)S(1)} %get-tuple-element.41.refs_1_), channel_id=1, source_target_pairs={{0,4},{4,0},{8,12},{12,8},{16,20},{20,16},{24,28},{28,24},{32,36},... | collective-permute-start | bytes 786440 | tf_op jit(solution)/shard_map/ppermute | solution.py:253
  7.7 7.3 %collective-permute-start.1 = (bf16[2,128,256]{2,1,0:T(8,128)(2,1)S(1)}, bf16[2,128,256]{2,1,0:T(8,128)(2,1)S(1)}, u32[]{:S(2)}, u32[]{:S(2)}) collective-permute-start(bf16[2,128,256]{2,1,0:T(8,128)(2,1)S(1)} %get-tuple-element.42), channel_id=1, source_target_pairs={{4,8},{12,16},{20,24},{28,32},{36,40},{44,48},{52,56},{60,64},{68,... | collective-permute-start | bytes 393224 | tf_op jit(solution)/shard_map/ppermute | solution.py:268
  10.5 7.9 %collective-permute-start.2 = (bf16[128,256]{1,0:T(8,128)(2,1)S(1)}, bf16[128,256]{1,0:T(8,128)(2,1)S(1)}, u32[]{:S(2)}, u32[]{:S(2)}) collective-permute-start(bf16[128,256]{1,0:T(8,128)(2,1)S(1)} %get-tuple-element.43.refs_5_.refs_1_), channel_id=1, source_target_pairs={{0,8},{4,12},{8,0},{12,4},{16,24},{20,28},{24,16},{28,20},{32,40},... | collective-permute-start | bytes 196616 | tf_op jit(solution)/shard_map/ppermute | solution.py:253
  11.1 7.3 %collective-permute-start.3 = (bf16[64,256]{1,0:T(8,128)(2,1)S(1)}, bf16[64,256]{1,0:T(8,128)(2,1)S(1)}, u32[]{:S(2)}, u32[]{:S(2)}) collective-permute-start(bf16[64,256]{1,0:T(8,128)(2,1)S(1)} %get-tuple-element.44), channel_id=1, source_target_pairs={{0,16},{4,20},{8,24},{12,28},{16,0},{20,4},{24,8},{28,12},{32,48},... | collective-permute-start | bytes 98312 | tf_op jit(solution)/shard_map/ppermute | solution.py:253
  13.9 4.5 %collective-permute-start.4 = (bf16[64,256]{1,0:T(8,128)(2,1)S(1)}, bf16[64,256]{1,0:T(8,128)(2,1)S(1)}, u32[]{:S(2)}, u32[]{:S(2)}) collective-permute-start(bf16[64,256]{1,0:T(8,128)(2,1)S(1)} %get-tuple-element.44), channel_id=1, source_target_pairs={{0,24},{4,28},{8,16},{12,20},{16,8},{20,12},{24,0},{28,4},{32,56},... | collective-permute-start | bytes 98312 | tf_op jit(solution)/shard_map/ppermute | solution.py:253
  15.1 3.3 %copy-start.3 = (bf16[256,1024]{1,0:T(8,128)(2,1)S(1)}, bf16[256,1024]{1,0:T(8,128)(2,1)}, u32[]{:S(2)}) copy-start(bf16[256,1024]{1,0:T(8,128)(2,1)} %refs_2_.3) | copy-start | bytes 1572868
  19.4 11.5 %collective-permute-start.5 = (bf16[128,256]{1,0:T(8,128)(2,1)S(1)}, bf16[128,256]{1,0:T(8,128)(2,1)S(1)}, u32[]{:S(2)}, u32[]{:S(2)}) collective-permute-start(bf16[128,256]{1,0:T(8,128)(2,1)S(1)} %get-tuple-element.49.refs_5_.refs_1_), channel_id=1, source_target_pairs={{0,32},{4,36},{8,40},{12,44},{16,48},{20,52},{24,56},{28,60},{32,0... | collective-permute-start | bytes 196616 | tf_op jit(solution)/shard_map/ppermute | solution.py:253
  20.5 10.4 %collective-permute-start.6 = (bf16[64,256]{1,0:T(8,128)(2,1)S(1)}, bf16[64,256]{1,0:T(8,128)(2,1)S(1)}, u32[]{:S(2)}, u32[]{:S(2)}) collective-permute-start(bf16[64,256]{1,0:T(8,128)(2,1)S(1)} %get-tuple-element.50), channel_id=1, source_target_pairs={{0,64},{4,68},{8,72},{12,76},{16,80},{20,84},{24,88},{28,92},{32,9... | collective-permute-start | bytes 98312 | tf_op jit(solution)/shard_map/ppermute | solution.py:253
  24.7 6.2 %collective-permute-start.7 = (bf16[64,256]{1,0:T(8,128)(2,1)S(1)}, bf16[64,256]{1,0:T(8,128)(2,1)S(1)}, u32[]{:S(2)}, u32[]{:S(2)}) collective-permute-start(bf16[64,256]{1,0:T(8,128)(2,1)S(1)} %get-tuple-element.50), channel_id=1, source_target_pairs={{0,96},{4,100},{8,104},{12,108},{16,112},{20,116},{24,120},{28,124... | collective-permute-start | bytes 98312 | tf_op jit(solution)/shard_map/ppermute | solution.py:253
  24.7 20.1 %collective-permute-start.12 = (bf16[128,1024]{1,0:T(8,128)(2,1)S(1)}, bf16[128,1024]{1,0:T(8,128)(2,1)S(1)}, u32[]{:S(2)}, u32[]{:S(2)}) collective-permute-start(bf16[128,1024]{1,0:T(8,128)(2,1)S(1)} %get-tuple-element.67), channel_id=1, source_target_pairs={{0,2},{1,3},{2,0},{3,1},{4,6},{5,7},{6,4},{7,5},{8,10},{9,11},{10,... | collective-permute-start | bytes 786440 | tf_op jit(solution)/shard_map/ppermute | solution.py:256
  31.8 14.5 %collective-permute-start.8 = (bf16[4,128,256]{2,1,0:T(8,128)(2,1)S(1)}, bf16[4,128,256]{2,1,0:T(8,128)(2,1)S(1)}, u32[]{:S(2)}, u32[]{:S(2)}) collective-permute-start(bf16[4,128,256]{2,1,0:T(8,128)(2,1)S(1)} %get-tuple-element.60.refs_6_), channel_id=1, source_target_pairs={{0,4},{4,0},{8,12},{12,8},{16,20},{20,16},{24,28},{28,24},{32,36},... | collective-permute-start | bytes 786440 | tf_op jit(solution)/shard_map/ppermute | solution.py:253
  32.8 11.3 %collective-permute-start.9 = (bf16[128,256]{1,0:T(8,128)(2,1)S(1)}, bf16[128,256]{1,0:T(8,128)(2,1)S(1)}, u32[]{:S(2)}, u32[]{:S(2)}) collective-permute-start(bf16[128,256]{1,0:T(8,128)(2,1)S(1)} %get-tuple-element.56.refs_5_), channel_id=1, source_target_pairs={{0,224},{4,228},{8,232},{12,236},{16,240},{20,244},{24,248},{28,25... | collective-permute-start | bytes 196616 | tf_op jit(solution)/shard_map/ppermute | solution.py:253
  44.1 2.1 %collective-permute-start.10 = (bf16[128,256]{1,0:T(8,128)(2,1)S(1)}, bf16[128,256]{1,0:T(8,128)(2,1)S(1)}, u32[]{:S(2)}, u32[]{:S(2)}) collective-permute-start(bf16[128,256]{1,0:T(8,128)(2,1)S(1)} %collective-permute-done.9.refs_8_), channel_id=1, source_target_pairs={{0,4},{4,0},{8,12},{12,8},{16,20},{20,16},{24,28},{28,24},{32,36},... | collective-permute-start | bytes 196616 | tf_op jit(solution)/shard_map/ppermute | solution.py:253
  44.8 11.0 %collective-permute-start.13 = (bf16[128,1024]{1,0:T(8,128)(2,1)S(1)}, bf16[128,1024]{1,0:T(8,128)(2,1)S(1)}, u32[]{:S(2)}, u32[]{:S(2)}) collective-permute-start(bf16[128,1024]{1,0:T(8,128)(2,1)S(1)} %get-tuple-element.67), channel_id=1, source_target_pairs={{0,3},{1,0},{2,1},{3,2},{4,7},{5,4},{6,5},{7,6},{8,11},{9,8},{10,9... | collective-permute-start | bytes 786440 | tf_op jit(solution)/shard_map/ppermute | solution.py:256
  45.6 13.6 %collective-permute-start.16 = (bf16[128,1024]{1,0:T(8,128)(2,1)S(1)}, bf16[128,1024]{1,0:T(8,128)(2,1)S(1)}, u32[]{:S(2)}, u32[]{:S(2)}) collective-permute-start(bf16[128,1024]{1,0:T(8,128)(2,1)S(1)} %get-tuple-element.67), channel_id=1, source_target_pairs={{0,1},{1,2},{2,3},{3,0},{4,5},{5,6},{6,7},{7,4},{8,9},{9,10},{10,1... | collective-permute-start | bytes 786440 | tf_op jit(solution)/shard_map/ppermute | solution.py:256
  49.4 10.3 %collective-permute-start.11 = (bf16[512,256]{1,0:T(8,128)(2,1)S(1)}, bf16[512,256]{1,0:T(8,128)(2,1)S(1)}, u32[]{:S(2)}, u32[]{:S(2)}) collective-permute-start(bf16[512,256]{1,0:T(8,128)(2,1)S(1)} %far.5), channel_id=1, source_target_pairs={{0,3},{1,0},{2,1},{3,2},{4,7},{5,4},{6,5},{7,6},{8,11},{9,8},{10,9... | collective-permute-start | bytes 786440 | tf_op jit(solution)/shard_map/ppermute | solution.py:256
  51.4 13.1 %collective-permute-start.19 = (bf16[128,1024]{1,0:T(8,128)(2,1)S(1)}, bf16[128,1024]{1,0:T(8,128)(2,1)S(1)}, u32[]{:S(2)}, u32[]{:S(2)}) collective-permute-start(bf16[128,1024]{1,0:T(8,128)(2,1)S(1)} %collective-permute-done.12.refs_6_), channel_id=1, source_target_pairs={{0,4},{4,0},{8,12},{12,8},{16,20},{20,16},{24,28},{28,24},{32,36},... | collective-permute-start | bytes 786440 | tf_op jit(solution)/shard_map/ppermute | solution.py:253
  55.5 9.6 %collective-permute-start.18 = (bf16[512,256]{1,0:T(8,128)(2,1)S(1)}, bf16[512,256]{1,0:T(8,128)(2,1)S(1)}, u32[]{:S(2)}, u32[]{:S(2)}) collective-permute-start(bf16[512,256]{1,0:T(8,128)(2,1)S(1)} %far.7), channel_id=1, source_target_pairs={{0,2},{1,3},{2,0},{3,1},{4,6},{5,7},{6,4},{7,5},{8,10},{9,11},{10,... | collective-permute-start | bytes 786440 | tf_op jit(solution)/shard_map/ppermute | solution.py:256
  55.7 7.5 %collective-permute-start.14 = (bf16[128,1024]{1,0:T(8,128)(2,1)S(1)}, bf16[128,1024]{1,0:T(8,128)(2,1)S(1)}, u32[]{:S(2)}, u32[]{:S(2)}) collective-permute-start(bf16[128,1024]{1,0:T(8,128)(2,1)S(1)} %collective-permute-done.13.refs_4_), channel_id=1, source_target_pairs={{0,4},{4,0},{8,12},{12,8},{16,20},{20,16},{24,28},{28,24},{32,36},... | collective-permute-start | bytes 786440 | tf_op jit(solution)/shard_map/ppermute | solution.py:253
  59.1 11.8 %collective-permute-start.15 = (bf16[512,256]{1,0:T(8,128)(2,1)S(1)}, bf16[512,256]{1,0:T(8,128)(2,1)S(1)}, u32[]{:S(2)}, u32[]{:S(2)}) collective-permute-start(bf16[512,256]{1,0:T(8,128)(2,1)S(1)} %far.6), channel_id=1, source_target_pairs={{0,1},{1,2},{2,3},{3,0},{4,5},{5,6},{6,7},{7,4},{8,9},{9,10},{10,1... | collective-permute-start | bytes 786440 | tf_op jit(solution)/shard_map/ppermute | solution.py:256
  59.7 11.3 %collective-permute-start.17 = (bf16[128,1024]{1,0:T(8,128)(2,1)S(1)}, bf16[128,1024]{1,0:T(8,128)(2,1)S(1)}, u32[]{:S(2)}, u32[]{:S(2)}) collective-permute-start(bf16[128,1024]{1,0:T(8,128)(2,1)S(1)} %collective-permute-done.16.refs_3_), channel_id=1, source_target_pairs={{0,4},{4,0},{8,12},{12,8},{16,20},{20,16},{24,28},{28,24},{32,36},... | collective-permute-start | bytes 786440 | tf_op jit(solution)/shard_map/ppermute | solution.py:253

commit v6 on v1

--- a/solution.py
+++ b/solution.py
@@ -76,7 +76,7 @@
     return jnp.where(low, x0, x1)
 
 
-def pyramid_kernel(at_ref, kv_ref, q_ref, lev_ref, face_ref, back_ref):
+def pyramid_kernel(at_ref, kv_ref, lev_ref, face_ref, back_ref):
     even = jnp.bitwise_and(at_ref[1], 1) == 0
     for side in range(2):
         for i in range(8):
@@ -257,7 +257,7 @@
         pyramid_kernel,
         "pyramid",
         [((2, 3840, WIDE), BF16), ((2, 2 * BLK, WIDE), BF16), ((2, BLK, WIDE), BF16)],
-        (at, keys_values, queries),
+        (at, keys_values),
     )
     turns = (2, 1, 3, 0)
     sibling = swap(face, 1)

time: 70 us -> 70.1 us (level)
    unnamed x8 -> x6, local copies, waits for them, and re-layouts: 2.82 us -> 2.82 us
where the time goes in v6:
time: 70.1 us; the launch traced here: 69.9 us
  Pallas kernels  31.5 us (45%)
  starting transfers between devices  30.2 us (43%)
  waiting for transfers between devices  5.19 us (7%)
  local copies, waits for them, and re-layouts  2.82 us (4%)
    pallas_call x12, Pallas kernels, call(): pl.pallas_call(lambda *refs: kernel(*refs[:n], *refs[n + late:]), out_sha...  31.5 us
    ppermute x13, starting transfers between devices, swap(): return lax.ppermute(x, 'ctx', [(i, i ^ bits) for i in range(shards)])  21.5 us
    ppermute x6, starting transfers between devices, turn(): lax.ppermute(x, 'head', [(i, (i + by) % heads) for i in range(heads)])  6.79 us
    unnamed x6, local copies, waits for them, and re-layouts  2.82 us
    ppermute x13, waiting for transfers between devices, swap(): return lax.ppermute(x, 'ctx', [(i, i ^ bits) for i in range(shards)])  2.38 us
    ppermute x6, waiting for transfers between devices, turn(): lax.ppermute(x, 'head', [(i, (i + by) % heads) for i in range(heads)])  2.1 us
    ppermute x1, starting transfers between devices, body(): back = lax.ppermute(back, 'ctx', ends + [(b, a) for a, b in ends])  1.91 us
  transfers between devices with their start and end apart: 20, of which 5 were waited for; matrix products, arithmetic and copies ran while one was open for 0% of the time, Pallas kernels for 37%

profile of v6, /device:TPU:1, one launch (start us, length us, event | category | flops | bytes accessed | tf_op | source)
XLA Modules:
  0.0 69.9 jit_solution(10872841469388181452)
XLA Ops:
  0.0 0.1 pad_add_fusion.refs_0_
  0.1 0.0 copy-start.2
  0.1 1.6 %copy-done.2 = bf16[2,2048,256]{2,1,0:T(8,128)(2,1)S(1)} copy-done((bf16[2,2048,256]{2,1,0:T(8,128)(2,1)S(1)}, bf16[2,2048,256]{2,1,0:T(8,128)(2,1)}, u32[]{:S(2)}) %copy-start.2) | copy-done | bytes 2097176
  1.7 0.0 copy-start.1
  1.7 1.5 %pyramid.1 = (bf16[2,3840,256]{2,1,0:T(8,128)(2,1)S(1)}, bf16[2,256,256]{2,1,0:T(8,128)(2,1)S(1)}, bf16[2,128,256]{2,1,0:T(8,128)(2,1)S(1)}) custom-call(s32[2]{0:T(128)S(1)} %pad_add_fusion.refs_0_, bf16[2,2048,256]{2,1,0:T(8,128)(2,1)S(1)} %copy-done.2), custom_call_target="tpu_custom_call" | custom-call | tf_op jit(solution)/shard_map/pyramid/pallas_call | solution.py:29
  3.2 3.3 %collective-permute-start = (bf16[2,256,256]{2,1,0:T(8,128)(2,1)S(1)}, bf16[2,256,256]{2,1,0:T(8,128)(2,1)S(1)}, u32[]{:S(2)}, u32[]{:S(2)}) collective-permute-start(bf16[2,256,256]{2,1,0:T(8,128)(2,1)S(1)} %get-tuple-element.41.refs_1_), channel_id=1, source_target_pairs={{0,4},{4,0},{8,12},{12,8},{16,20},{20,16},{24,28},{28,24},{32,36},... | collective-permute-start | bytes 786440 | tf_op jit(solution)/shard_map/ppermute | solution.py:250
  6.5 1.9 %collective-permute-start.1 = (bf16[2,128,256]{2,1,0:T(8,128)(2,1)S(1)}, bf16[2,128,256]{2,1,0:T(8,128)(2,1)S(1)}, u32[]{:S(2)}, u32[]{:S(2)}) collective-permute-start(bf16[2,128,256]{2,1,0:T(8,128)(2,1)S(1)} %get-tuple-element.42), channel_id=1, source_target_pairs={{4,8},{12,16},{20,24},{28,32},{36,40},{44,48},{52,56},{60,64},{68,... | collective-permute-start | bytes 393224 | tf_op jit(solution)/shard_map/ppermute | solution.py:265
  8.4 0.0 collective-permute-done.refs_2_.refs_3_.refs_5_
  8.4 0.8 %start.1 = (bf16[128,256]{1,0:T(8,128)(2,1)S(1)}, bf16[64,256]{1,0:T(8,128)(2,1)S(1)}) custom-call(s32[2]{0:T(128)S(1)} %pad_add_fusion.refs_0_, bf16[2,256,256]{2,1,0:T(8,128)(2,1)S(1)} %get-tuple-element.41.refs_1_, bf16[2,256,256]{2,1,0:T(8,128)(2,1)S(1)} %collective-permute-done.refs_2_.refs_3_.refs_5_), custom_call_target="tpu_custom_call" | custom-call | tf_op jit(solution)/shard_map/start/pallas_call | solution.py:29
  9.3 0.6 collective-permute-start.2
  9.9 2.8 %collective-permute-start.3 = (bf16[64,256]{1,0:T(8,128)(2,1)S(1)}, bf16[64,256]{1,0:T(8,128)(2,1)S(1)}, u32[]{:S(2)}, u32[]{:S(2)}) collective-permute-start(bf16[64,256]{1,0:T(8,128)(2,1)S(1)} %get-tuple-element.44), channel_id=1, source_target_pairs={{0,16},{4,20},{8,24},{12,28},{16,0},{20,4},{24,8},{28,12},{32,48},... | collective-permute-start | bytes 98312 | tf_op jit(solution)/shard_map/ppermute | solution.py:250
  12.7 0.5 collective-permute-start.4
  13.1 0.7 %collective-permute-done.1.refs_4_ = bf16[2,128,256]{2,1,0:T(8,128)(2,1)S(1)} collective-permute-done((bf16[2,128,256]{2,1,0:T(8,128)(2,1)S(1)}, bf16[2,128,256]{2,1,0:T(8,128)(2,1)S(1)}, u32[]{:S(2)}, u32[]{:S(2)}) %collective-permute-start.1) | collective-permute-done | bytes 131104 | tf_op jit(solution)/shard_map/ppermute | solution.py:265
  13.9 0.0 copy-start
  13.9 1.2 %copy-done = bf16[2048,256]{1,0:T(8,128)(2,1)S(1)} copy-done((bf16[2048,256]{1,0:T(8,128)(2,1)S(1)}, bf16[2048,256]{1,0:T(8,128)(2,1)}, u32[]{:S(2)}) %copy-start) | copy-done | bytes 1048600
  15.1 3.3 %near.3 = (f32[512,256]{1,0:T(8,128)S(1)}, f32[512,256]{1,0:T(8,128)S(1)}, f32[512,256]{1,0:T(8,128)S(1)}) custom-call(s32[2]{0:T(128)S(1)} %pad_add_fusion.refs_0_, bf16[2048,256]{1,0:T(8,128)(2,1)S(1)} %copy-done, bf16[2,3840,256]{2,1,0:T(8,128)(2,1)S(1)} %get-tuple-element.40.refs_2_, ...), custom_call_target="tpu_custom_call" | custom-call | tf_op jit(solution)/shard_map/near/pallas_call | solution.py:29
  18.4 0.0 collective-permute-done.3.refs_3_
  18.4 0.0 collective-permute-done.4.refs_4_
  18.4 0.0 collective-permute-done.2.refs_2_.refs_5_
  18.4 0.0 copy-done.1
  18.4 1.0 %middle.1 = (bf16[128,256]{1,0:T(8,128)(2,1)S(1)}, bf16[128,256]{1,0:T(8,128)(2,1)S(1)}, bf16[64,256]{1,0:T(8,128)(2,1)S(1)}, bf16[128,1024]{1,0:T(8,128)(2,1)S(1)}) custom-call(s32[2]{0:T(128)S(1)} %pad_add_fusion.refs_0_, bf16[128,256]{1,0:T(8,128)(2,1)S(1)} %get-tuple-element.43.refs_5_.refs_1_, ...), custom_call_target="tpu_custom_call" | custom-call | tf_op jit(solution)/shard_map/middle/pallas_call | solution.py:29
  19.4 1.7 %collective-permute-start.12 = (bf16[128,1024]{1,0:T(8,128)(2,1)S(1)}, bf16[128,1024]{1,0:T(8,128)(2,1)S(1)}, u32[]{:S(2)}, u32[]{:S(2)}) collective-permute-start(bf16[128,1024]{1,0:T(8,128)(2,1)S(1)} %get-tuple-element.67), channel_id=1, source_target_pairs={{0,2},{1,3},{2,0},{3,1},{4,6},{5,7},{6,4},{7,5},{8,10},{9,11},{10,... | collective-permute-start | bytes 786440 | tf_op jit(solution)/shard_map/ppermute | solution.py:253
  21.1 1.6 %collective-permute-start.5 = (bf16[128,256]{1,0:T(8,128)(2,1)S(1)}, bf16[128,256]{1,0:T(8,128)(2,1)S(1)}, u32[]{:S(2)}, u32[]{:S(2)}) collective-permute-start(bf16[128,256]{1,0:T(8,128)(2,1)S(1)} %get-tuple-element.49.refs_5_.refs_1_), channel_id=1, source_target_pairs={{0,32},{4,36},{8,40},{12,44},{16,48},{20,52},{24,56},{28,60},{32,0... | collective-permute-start | bytes 196616 | tf_op jit(solution)/shard_map/ppermute | solution.py:250
  22.7 4.2 %collective-permute-start.6 = (bf16[64,256]{1,0:T(8,128)(2,1)S(1)}, bf16[64,256]{1,0:T(8,128)(2,1)S(1)}, u32[]{:S(2)}, u32[]{:S(2)}) collective-permute-start(bf16[64,256]{1,0:T(8,128)(2,1)S(1)} %get-tuple-element.50), channel_id=1, source_target_pairs={{0,64},{4,68},{8,72},{12,76},{16,80},{20,84},{24,88},{28,92},{32,9... | collective-permute-start | bytes 98312 | tf_op jit(solution)/shard_map/ppermute | solution.py:250
  26.9 0.0 collective-permute-start.7
  26.9 3.3 %near.4 = (f32[512,256]{1,0:T(8,128)S(1)}, f32[512,256]{1,0:T(8,128)S(1)}, f32[512,256]{1,0:T(8,128)S(1)}) custom-call(s32[2]{0:T(128)S(1)} %pad_add_fusion.refs_0_, bf16[2048,256]{1,0:T(8,128)(2,1)S(1)} %copy-done, bf16[2,3840,256]{2,1,0:T(8,128)(2,1)S(1)} %get-tuple-element.40.refs_2_, ...), custom_call_target="tpu_custom_call" | custom-call | tf_op jit(solution)/shard_map/near/pallas_call | solution.py:29
  30.2 0.0 collective-permute-done.6.refs_3_
  30.2 1.4 %collective-permute-done.7.refs_4_ = bf16[64,256]{1,0:T(8,128)(2,1)S(1)} collective-permute-done((bf16[64,256]{1,0:T(8,128)(2,1)S(1)}, bf16[64,256]{1,0:T(8,128)(2,1)S(1)}, u32[]{:S(2)}, u32[]{:S(2)}) %collective-permute-start.7) | collective-permute-done | bytes 32800 | tf_op jit(solution)/shard_map/ppermute | solution.py:250
  31.6 0.0 collective-permute-done.5.refs_2_
  31.6 0.8 %last.1 = (bf16[128,256]{1,0:T(8,128)(2,1)S(1)}, bf16[4,128,256]{2,1,0:T(8,128)(2,1)S(1)}) custom-call(s32[2]{0:T(128)S(1)} %pad_add_fusion.refs_0_, bf16[128,256]{1,0:T(8,128)(2,1)S(1)} %get-tuple-element.49.refs_5_.refs_1_, bf16[128,256]{1,0:T(8,128)(2,1)S(1)} %collective-permute-done.5.refs_2_, bf16[64,256]{1,0:T(8,128)(2,1)S(1)} %collective-permute-done.6.refs_3_, ...), custom_call_target="tpu_custom_call" | custom-call | tf_op jit(solution)/shard_map/last/pallas_call | solution.py:29
  32.5 2.8 %collective-permute-start.8 = (bf16[4,128,256]{2,1,0:T(8,128)(2,1)S(1)}, bf16[4,128,256]{2,1,0:T(8,128)(2,1)S(1)}, u32[]{:S(2)}, u32[]{:S(2)}) collective-permute-start(bf16[4,128,256]{2,1,0:T(8,128)(2,1)S(1)} %get-tuple-element.60.refs_6_), channel_id=1, source_target_pairs={{0,4},{4,0},{8,12},{12,8},{16,20},{20,16},{24,28},{28,24},{32,36},... | collective-permute-start | bytes 786440 | tf_op jit(solution)/shard_map/ppermute | solution.py:250
  35.2 0.0 collective-permute-done.12.refs_10_
  35.2 0.8 %collective-permute-start.13 = (bf16[128,1024]{1,0:T(8,128)(2,1)S(1)}, bf16[128,1024]{1,0:T(8,128)(2,1)S(1)}, u32[]{:S(2)}, u32[]{:S(2)}) collective-permute-start(bf16[128,1024]{1,0:T(8,128)(2,1)S(1)} %get-tuple-element.67), channel_id=1, source_target_pairs={{0,3},{1,0},{2,1},{3,2},{4,7},{5,4},{6,5},{7,6},{8,11},{9,8},{10,9... | collective-permute-start | bytes 786440 | tf_op jit(solution)/shard_map/ppermute | solution.py:253
  36.0 0.7 collective-permute-start.16
  36.7 0.8 %collective-permute-start.19 = (bf16[128,1024]{1,0:T(8,128)(2,1)S(1)}, bf16[128,1024]{1,0:T(8,128)(2,1)S(1)}, u32[]{:S(2)}, u32[]{:S(2)}) collective-permute-start(bf16[128,1024]{1,0:T(8,128)(2,1)S(1)} %collective-permute-done.12.refs_10_), channel_id=1, source_target_pairs={{0,4},{4,0},{8,12},{12,8},{16,20},{20,16},{24,28},{28,24},{32,36},... | collective-permute-start | bytes 786440 | tf_op jit(solution)/shard_map/ppermute | solution.py:250
  37.5 3.3 %collective-permute-start.9 = (bf16[128,256]{1,0:T(8,128)(2,1)S(1)}, bf16[128,256]{1,0:T(8,128)(2,1)S(1)}, u32[]{:S(2)}, u32[]{:S(2)}) collective-permute-start(bf16[128,256]{1,0:T(8,128)(2,1)S(1)} %get-tuple-element.56.refs_5_), channel_id=1, source_target_pairs={{0,224},{4,228},{8,232},{12,236},{16,240},{20,244},{24,248},{28,25... | collective-permute-start | bytes 196616 | tf_op jit(solution)/shard_map/ppermute | solution.py:250
  40.8 5.6 %near.5 = (f32[512,256]{1,0:T(8,128)S(1)}, f32[512,256]{1,0:T(8,128)S(1)}, f32[512,256]{1,0:T(8,128)S(1)}, f32[512,256]{1,0:T(8,128)S(1)}, f32[512,256]{1,0:T(8,128)S(1)}, /*index=5*/f32[512,256]{1,0:T(8,128)S(1)}) custom-call(s32[2]{0:T(128)S(1)} %pad_add_fusion.refs_0_, bf16[2048,256]{1,0:T(8,128)(2,1)S(1)} %copy-done, ...), custom_call_target="tpu_custom_call" | custom-call | tf_op jit(solution)/shard_map/near/pallas_call | solution.py:29
  46.4 0.0 collective-permute-done.9.refs_8_
  46.4 0.4 collective-permute-start.10
  46.8 1.0 %collective-permute-done.10.refs_9_ = bf16[128,256]{1,0:T(8,128)(2,1)S(1)} collective-permute-done((bf16[128,256]{1,0:T(8,128)(2,1)S(1)}, bf16[128,256]{1,0:T(8,128)(2,1)S(1)}, u32[]{:S(2)}, u32[]{:S(2)}) %collective-permute-start.10) | collective-permute-done | bytes 65568 | tf_op jit(solution)/shard_map/ppermute | solution.py:250
  47.8 0.0 collective-permute-done.8.refs_7_
  47.8 3.1 %far.7 = bf16[512,256]{1,0:T(8,128)(2,1)S(1)} custom-call(s32[2]{0:T(128)S(1)} %pad_add_fusion.refs_0_, bf16[2048,256]{1,0:T(8,128)(2,1)S(1)} %copy-done, f32[512,256]{1,0:T(8,128)S(1)} %get-tuple-element.71.refs_2_, f32[512,256]{1,0:T(8,128)S(1)} %get-tuple-element.72.refs_3_, f32[512,256]{1,0:T(8,128)S(1)} %get-tuple-element.73.refs_4_, ...), custom_call_target="tpu_custom_call" | custom-call | tf_op jit(solution)/shard_map/far/pallas_call | solution.py:29
  50.9 0.7 %collective-permute-start.18 = (bf16[512,256]{1,0:T(8,128)(2,1)S(1)}, bf16[512,256]{1,0:T(8,128)(2,1)S(1)}, u32[]{:S(2)}, u32[]{:S(2)}) collective-permute-start(bf16[512,256]{1,0:T(8,128)(2,1)S(1)} %far.7), channel_id=1, source_target_pairs={{0,2},{1,3},{2,0},{3,1},{4,6},{5,7},{6,4},{7,5},{8,10},{9,11},{10,... | collective-permute-start | bytes 786440 | tf_op jit(solution)/shard_map/ppermute | solution.py:253
  51.6 3.1 %far.6 = bf16[512,256]{1,0:T(8,128)(2,1)S(1)} custom-call(s32[2]{0:T(128)S(1)} %pad_add_fusion.refs_0_, bf16[2048,256]{1,0:T(8,128)(2,1)S(1)} %copy-done, f32[512,256]{1,0:T(8,128)S(1)} %get-tuple-element.68.refs_2_, f32[512,256]{1,0:T(8,128)S(1)} %get-tuple-element.69.refs_3_, f32[512,256]{1,0:T(8,128)S(1)} %get-tuple-element.70.refs_4_, ...), custom_call_target="tpu_custom_call" | custom-call | tf_op jit(solution)/shard_map/far/pallas_call | solution.py:29
  54.7 2.2 %collective-permute-start.15 = (bf16[512,256]{1,0:T(8,128)(2,1)S(1)}, bf16[512,256]{1,0:T(8,128)(2,1)S(1)}, u32[]{:S(2)}, u32[]{:S(2)}) collective-permute-start(bf16[512,256]{1,0:T(8,128)(2,1)S(1)} %far.6), channel_id=1, source_target_pairs={{0,1},{1,2},{2,3},{3,0},{4,5},{5,6},{6,7},{7,4},{8,9},{9,10},{10,1... | collective-permute-start | bytes 786440 | tf_op jit(solution)/shard_map/ppermute | solution.py:253
  56.9 3.1 %far.5 = bf16[512,256]{1,0:T(8,128)(2,1)S(1)} custom-call(s32[2]{0:T(128)S(1)} %pad_add_fusion.refs_0_, bf16[2048,256]{1,0:T(8,128)(2,1)S(1)} %copy-done, f32[512,256]{1,0:T(8,128)S(1)} %get-tuple-element.63.refs_2_, f32[512,256]{1,0:T(8,128)S(1)} %get-tuple-element.64.refs_3_, f32[512,256]{1,0:T(8,128)S(1)} %get-tuple-element.65.refs_4_, ...), custom_call_target="tpu_custom_call" | custom-call | tf_op jit(solution)/shard_map/far/pallas_call | solution.py:29
  60.0 0.0 collective-permute-done.13.refs_4_
  60.0 0.6 collective-permute-start.11
  60.7 0.0 collective-permute-done.16.refs_7_
  60.7 1.1 %collective-permute-start.14 = (bf16[128,1024]{1,0:T(8,128)(2,1)S(1)}, bf16[128,1024]{1,0:T(8,128)(2,1)S(1)}, u32[]{:S(2)}, u32[]{:S(2)}) collective-permute-start(bf16[128,1024]{1,0:T(8,128)(2,1)S(1)} %collective-permute-done.13.refs_4_), channel_id=1, source_target_pairs={{0,4},{4,0},{8,12},{12,8},{16,20},{20,16},{24,28},{28,24},{32,36},... | collective-permute-start | bytes 786440 | tf_op jit(solution)/shard_map/ppermute | solution.py:250
  61.8 0.0 collective-permute-done.19.refs_11_
  61.8 0.1 collective-permute-start.17
  61.9 3.1 %far.4.refs_1_ = bf16[512,256]{1,0:T(8,128)(2,1)S(1)} custom-call(s32[2]{0:T(128)S(1)} %pad_add_fusion.refs_0_, bf16[2048,256]{1,0:T(8,128)(2,1)S(1)} %copy-done, f32[512,256]{1,0:T(8,128)S(1)} %get-tuple-element.57.refs_2_, f32[512,256]{1,0:T(8,128)S(1)} %get-tuple-element.58.refs_3_, f32[512,256]{1,0:T(8,128)S(1)} %get-tuple-element.59.refs_4_, ...), custom_call_target="tpu_custom_call" | custom-call | tf_op jit(solution)/shard_map/far/pallas_call | solution.py:29
  65.0 0.0 collective-permute-done.18.refs_9_
  65.0 1.5 %collective-permute-done.15.refs_6_ = bf16[512,256]{1,0:T(8,128)(2,1)S(1)} collective-permute-done((bf16[512,256]{1,0:T(8,128)(2,1)S(1)}, bf16[512,256]{1,0:T(8,128)(2,1)S(1)}, u32[]{:S(2)}, u32[]{:S(2)}) %collective-permute-start.15) | collective-permute-done | bytes 262176 | tf_op jit(solution)/shard_map/ppermute | solution.py:253
  66.5 0.6 collective-permute-done.11.refs_3_
  67.1 0.0 collective-permute-done.14.refs_5_
  67.1 0.0 collective-permute-done.17.refs_8_
  67.1 2.8 %project.1 = bf16[512,1024]{1,0:T(8,128)(2,1)} custom-call(s32[2]{0:T(128)S(1)} %pad_add_fusion.refs_0_, bf16[512,256]{1,0:T(8,128)(2,1)S(1)} %far.4.refs_1_, bf16[256,1024]{1,0:T(8,128)(2,1)S(1)} %copy-done.1, bf16[512,256]{1,0:T(8,128)(2,1)S(1)} %collective-permute-done.11.refs_3_, bf16[128,1024]{1,0:T(8,128)(2,1)S(1)} %collective-permute-done.13.refs_4_, ...), custom_call_target="tpu_custom_call" | custom-call | tf_op jit(solution)/shard_map/project/pallas_call | solution.py:29
Async XLA Ops:
  0.1 1.6 %copy-start.2 = (bf16[2,2048,256]{2,1,0:T(8,128)(2,1)S(1)}, bf16[2,2048,256]{2,1,0:T(8,128)(2,1)}, u32[]{:S(2)}) copy-start(bf16[2,2048,256]{2,1,0:T(8,128)(2,1)} %refs_1_.8) | copy-start | bytes 6291460
  1.7 16.7 %copy-start.1 = (bf16[256,1024]{1,0:T(8,128)(2,1)S(1)}, bf16[256,1024]{1,0:T(8,128)(2,1)}, u32[]{:S(2)}) copy-start(bf16[256,1024]{1,0:T(8,128)(2,1)} %refs_2_.1) | copy-start | bytes 1572868
  3.2 5.2 %collective-permute-start = (bf16[2,256,256]{2,1,0:T(8,128)(2,1)S(1)}, bf16[2,256,256]{2,1,0:T(8,128)(2,1)S(1)}, u32[]{:S(2)}, u32[]{:S(2)}) collective-permute-start(bf16[2,256,256]{2,1,0:T(8,128)(2,1)S(1)} %get-tuple-element.41.refs_1_), channel_id=1, source_target_pairs={{0,4},{4,0},{8,12},{12,8},{16,20},{20,16},{24,28},{28,24},{32,36},... | collective-permute-start | bytes 786440 | tf_op jit(solution)/shard_map/ppermute | solution.py:250
  6.5 7.3 %collective-permute-start.1 = (bf16[2,128,256]{2,1,0:T(8,128)(2,1)S(1)}, bf16[2,128,256]{2,1,0:T(8,128)(2,1)S(1)}, u32[]{:S(2)}, u32[]{:S(2)}) collective-permute-start(bf16[2,128,256]{2,1,0:T(8,128)(2,1)S(1)} %get-tuple-element.42), channel_id=1, source_target_pairs={{4,8},{12,16},{20,24},{28,32},{36,40},{44,48},{52,56},{60,64},{68,... | collective-permute-start | bytes 393224 | tf_op jit(solution)/shard_map/ppermute | solution.py:265
  9.3 9.1 %collective-permute-start.2 = (bf16[128,256]{1,0:T(8,128)(2,1)S(1)}, bf16[128,256]{1,0:T(8,128)(2,1)S(1)}, u32[]{:S(2)}, u32[]{:S(2)}) collective-permute-start(bf16[128,256]{1,0:T(8,128)(2,1)S(1)} %get-tuple-element.43.refs_5_.refs_1_), channel_id=1, source_target_pairs={{0,8},{4,12},{8,0},{12,4},{16,24},{20,28},{24,16},{28,20},{32,40},... | collective-permute-start | bytes 196616 | tf_op jit(solution)/shard_map/ppermute | solution.py:250
  9.9 8.5 %collective-permute-start.3 = (bf16[64,256]{1,0:T(8,128)(2,1)S(1)}, bf16[64,256]{1,0:T(8,128)(2,1)S(1)}, u32[]{:S(2)}, u32[]{:S(2)}) collective-permute-start(bf16[64,256]{1,0:T(8,128)(2,1)S(1)} %get-tuple-element.44), channel_id=1, source_target_pairs={{0,16},{4,20},{8,24},{12,28},{16,0},{20,4},{24,8},{28,12},{32,48},... | collective-permute-start | bytes 98312 | tf_op jit(solution)/shard_map/ppermute | solution.py:250
  12.7 5.7 %collective-permute-start.4 = (bf16[64,256]{1,0:T(8,128)(2,1)S(1)}, bf16[64,256]{1,0:T(8,128)(2,1)S(1)}, u32[]{:S(2)}, u32[]{:S(2)}) collective-permute-start(bf16[64,256]{1,0:T(8,128)(2,1)S(1)} %get-tuple-element.44), channel_id=1, source_target_pairs={{0,24},{4,28},{8,16},{12,20},{16,8},{20,12},{24,0},{28,4},{32,56},... | collective-permute-start | bytes 98312 | tf_op jit(solution)/shard_map/ppermute | solution.py:250
  13.9 1.2 %copy-start = (bf16[2048,256]{1,0:T(8,128)(2,1)S(1)}, bf16[2048,256]{1,0:T(8,128)(2,1)}, u32[]{:S(2)}) copy-start(bf16[2048,256]{1,0:T(8,128)(2,1)} %refs_1_.15) | copy-start | bytes 3145732
  19.4 15.9 %collective-permute-start.12 = (bf16[128,1024]{1,0:T(8,128)(2,1)S(1)}, bf16[128,1024]{1,0:T(8,128)(2,1)S(1)}, u32[]{:S(2)}, u32[]{:S(2)}) collective-permute-start(bf16[128,1024]{1,0:T(8,128)(2,1)S(1)} %get-tuple-element.67), channel_id=1, source_target_pairs={{0,2},{1,3},{2,0},{3,1},{4,6},{5,7},{6,4},{7,5},{8,10},{9,11},{10,... | collective-permute-start | bytes 786440 | tf_op jit(solution)/shard_map/ppermute | solution.py:253
  21.1 10.5 %collective-permute-start.5 = (bf16[128,256]{1,0:T(8,128)(2,1)S(1)}, bf16[128,256]{1,0:T(8,128)(2,1)S(1)}, u32[]{:S(2)}, u32[]{:S(2)}) collective-permute-start(bf16[128,256]{1,0:T(8,128)(2,1)S(1)} %get-tuple-element.49.refs_5_.refs_1_), channel_id=1, source_target_pairs={{0,32},{4,36},{8,40},{12,44},{16,48},{20,52},{24,56},{28,60},{32,0... | collective-permute-start | bytes 196616 | tf_op jit(solution)/shard_map/ppermute | solution.py:250
  22.7 7.5 %collective-permute-start.6 = (bf16[64,256]{1,0:T(8,128)(2,1)S(1)}, bf16[64,256]{1,0:T(8,128)(2,1)S(1)}, u32[]{:S(2)}, u32[]{:S(2)}) collective-permute-start(bf16[64,256]{1,0:T(8,128)(2,1)S(1)} %get-tuple-element.50), channel_id=1, source_target_pairs={{0,64},{4,68},{8,72},{12,76},{16,80},{20,84},{24,88},{28,92},{32,9... | collective-permute-start | bytes 98312 | tf_op jit(solution)/shard_map/ppermute | solution.py:250
  26.9 4.7 %collective-permute-start.7 = (bf16[64,256]{1,0:T(8,128)(2,1)S(1)}, bf16[64,256]{1,0:T(8,128)(2,1)S(1)}, u32[]{:S(2)}, u32[]{:S(2)}) collective-permute-start(bf16[64,256]{1,0:T(8,128)(2,1)S(1)} %get-tuple-element.50), channel_id=1, source_target_pairs={{0,96},{4,100},{8,104},{12,108},{16,112},{20,116},{24,120},{28,124... | collective-permute-start | bytes 98312 | tf_op jit(solution)/shard_map/ppermute | solution.py:250
  32.5 15.3 %collective-permute-start.8 = (bf16[4,128,256]{2,1,0:T(8,128)(2,1)S(1)}, bf16[4,128,256]{2,1,0:T(8,128)(2,1)S(1)}, u32[]{:S(2)}, u32[]{:S(2)}) collective-permute-start(bf16[4,128,256]{2,1,0:T(8,128)(2,1)S(1)} %get-tuple-element.60.refs_6_), channel_id=1, source_target_pairs={{0,4},{4,0},{8,12},{12,8},{16,20},{20,16},{24,28},{28,24},{32,36},... | collective-permute-start | bytes 786440 | tf_op jit(solution)/shard_map/ppermute | solution.py:250
  35.2 24.8 %collective-permute-start.13 = (bf16[128,1024]{1,0:T(8,128)(2,1)S(1)}, bf16[128,1024]{1,0:T(8,128)(2,1)S(1)}, u32[]{:S(2)}, u32[]{:S(2)}) collective-permute-start(bf16[128,1024]{1,0:T(8,128)(2,1)S(1)} %get-tuple-element.67), channel_id=1, source_target_pairs={{0,3},{1,0},{2,1},{3,2},{4,7},{5,4},{6,5},{7,6},{8,11},{9,8},{10,9... | collective-permute-start | bytes 786440 | tf_op jit(solution)/shard_map/ppermute | solution.py:253
  36.0 24.7 %collective-permute-start.16 = (bf16[128,1024]{1,0:T(8,128)(2,1)S(1)}, bf16[128,1024]{1,0:T(8,128)(2,1)S(1)}, u32[]{:S(2)}, u32[]{:S(2)}) collective-permute-start(bf16[128,1024]{1,0:T(8,128)(2,1)S(1)} %get-tuple-element.67), channel_id=1, source_target_pairs={{0,1},{1,2},{2,3},{3,0},{4,5},{5,6},{6,7},{7,4},{8,9},{9,10},{10,1... | collective-permute-start | bytes 786440 | tf_op jit(solution)/shard_map/ppermute | solution.py:253
  36.7 25.1 %collective-permute-start.19 = (bf16[128,1024]{1,0:T(8,128)(2,1)S(1)}, bf16[128,1024]{1,0:T(8,128)(2,1)S(1)}, u32[]{:S(2)}, u32[]{:S(2)}) collective-permute-start(bf16[128,1024]{1,0:T(8,128)(2,1)S(1)} %collective-permute-done.12.refs_10_), channel_id=1, source_target_pairs={{0,4},{4,0},{8,12},{12,8},{16,20},{20,16},{24,28},{28,24},{32,36},... | collective-permute-start | bytes 786440 | tf_op jit(solution)/shard_map/ppermute | solution.py:250
  37.5 8.9 %collective-permute-start.9 = (bf16[128,256]{1,0:T(8,128)(2,1)S(1)}, bf16[128,256]{1,0:T(8,128)(2,1)S(1)}, u32[]{:S(2)}, u32[]{:S(2)}) collective-permute-start(bf16[128,256]{1,0:T(8,128)(2,1)S(1)} %get-tuple-element.56.refs_5_), channel_id=1, source_target_pairs={{0,224},{4,228},{8,232},{12,236},{16,240},{20,244},{24,248},{28,25... | collective-permute-start | bytes 196616 | tf_op jit(solution)/shard_map/ppermute | solution.py:250
  46.4 1.3 %collective-permute-start.10 = (bf16[128,256]{1,0:T(8,128)(2,1)S(1)}, bf16[128,256]{1,0:T(8,128)(2,1)S(1)}, u32[]{:S(2)}, u32[]{:S(2)}) collective-permute-start(bf16[128,256]{1,0:T(8,128)(2,1)S(1)} %collective-permute-done.9.refs_8_), channel_id=1, source_target_pairs={{0,4},{4,0},{8,12},{12,8},{16,20},{20,16},{24,28},{28,24},{32,36},... | collective-permute-start | bytes 196616 | tf_op jit(solution)/shard_map/ppermute | solution.py:250
  50.9 14.1 %collective-permute-start.18 = (bf16[512,256]{1,0:T(8,128)(2,1)S(1)}, bf16[512,256]{1,0:T(8,128)(2,1)S(1)}, u32[]{:S(2)}, u32[]{:S(2)}) collective-permute-start(bf16[512,256]{1,0:T(8,128)(2,1)S(1)} %far.7), channel_id=1, source_target_pairs={{0,2},{1,3},{2,0},{3,1},{4,6},{5,7},{6,4},{7,5},{8,10},{9,11},{10,... | collective-permute-start | bytes 786440 | tf_op jit(solution)/shard_map/ppermute | solution.py:253
  54.7 11.8 %collective-permute-start.15 = (bf16[512,256]{1,0:T(8,128)(2,1)S(1)}, bf16[512,256]{1,0:T(8,128)(2,1)S(1)}, u32[]{:S(2)}, u32[]{:S(2)}) collective-permute-start(bf16[512,256]{1,0:T(8,128)(2,1)S(1)} %far.6), channel_id=1, source_target_pairs={{0,1},{1,2},{2,3},{3,0},{4,5},{5,6},{6,7},{7,4},{8,9},{9,10},{10,1... | collective-permute-start | bytes 786440 | tf_op jit(solution)/shard_map/ppermute | solution.py:253
  60.0 7.1 %collective-permute-start.11 = (bf16[512,256]{1,0:T(8,128)(2,1)S(1)}, bf16[512,256]{1,0:T(8,128)(2,1)S(1)}, u32[]{:S(2)}, u32[]{:S(2)}) collective-permute-start(bf16[512,256]{1,0:T(8,128)(2,1)S(1)} %far.5), channel_id=1, source_target_pairs={{0,3},{1,0},{2,1},{3,2},{4,7},{5,4},{6,5},{7,6},{8,11},{9,8},{10,9... | collective-permute-start | bytes 786440 | tf_op jit(solution)/shard_map/ppermute | solution.py:253
  60.7 6.4 %collective-permute-start.14 = (bf16[128,1024]{1,0:T(8,128)(2,1)S(1)}, bf16[128,1024]{1,0:T(8,128)(2,1)S(1)}, u32[]{:S(2)}, u32[]{:S(2)}) collective-permute-start(bf16[128,1024]{1,0:T(8,128)(2,1)S(1)} %collective-permute-done.13.refs_4_), channel_id=1, source_target_pairs={{0,4},{4,0},{8,12},{12,8},{16,20},{20,16},{24,28},{28,24},{32,36},... | collective-permute-start | bytes 786440 | tf_op jit(solution)/shard_map/ppermute | solution.py:250
  61.8 5.3 %collective-permute-start.17 = (bf16[128,1024]{1,0:T(8,128)(2,1)S(1)}, bf16[128,1024]{1,0:T(8,128)(2,1)S(1)}, u32[]{:S(2)}, u32[]{:S(2)}) collective-permute-start(bf16[128,1024]{1,0:T(8,128)(2,1)S(1)} %collective-permute-done.16.refs_7_), channel_id=1, source_target_pairs={{0,4},{4,0},{8,12},{12,8},{16,20},{20,16},{24,28},{28,24},{32,36},... | collective-permute-start | bytes 786440 | tf_op jit(solution)/shard_map/ppermute | solution.py:250
